TPU v7x, 32 devices: a whole 2x2x4 slice. The times are simulated.
32 devices in a mesh: tok: 8 (over y, x, core), col: 4 (over z).
Axes of the slice: x: 2, y: 2, z: 4, core: 2. Of those that a mesh axis runs over, the one named last changes fastest.
Arguments:
- rollout: bfloat16 [1024, 5120], P('tok'), may hold values from -6 to 6
- lengths: int32 [16], P('tok'), may hold values from 16 to 64
- route: int32 [1024, 1], P('tok'), may hold values from 0 to 7; in each aligned block of 128 rows (0 to 127, 128 to 255, ...) at most 32 rows name the same one
- up_codes: bfloat16 [5120, 2048], P('tok', 'col'), may hold values from -4 to 4
- up_scales: float32 [20, 8], P(None, 'col'), may hold values from 0.0069877123 to 0.02795085
- block_rows: int32 [8, 2], P('col'), may hold values from 0 to 19, as said below
- delta: float32 [256, 8, 2, 256], P('tok', 'col'), may hold values from -0.125 to 0.125
- adam_m: float32 [256, 8, 2, 256], P('tok', 'col'), may hold values from -12 to 12
- adam_v: float32 [256, 8, 2, 256], P('tok', 'col'), may hold values from 1 to 30
- gate_pre: bfloat16 [2048, 2048], P('tok', 'col'), may hold values from -8 to 8
- hidden_grad: bfloat16 [2048, 2048], P('tok', 'col'), may hold values from -0.875 to 0.875
Outputs:
- input_grad: bfloat16 [2048, 5120], P('tok', 'col')
- gate_grad: bfloat16 [2048, 2048], P('tok', 'col')
- new_delta: float32 [256, 8, 2, 256], P('tok', 'col')
- new_m: float32 [256, 8, 2, 256], P('tok', 'col')
- new_v: float32 [256, 8, 2, 256], P('tok', 'col')
- delta_scale: float32 [8, 2], P('col')
- delta_codes: bfloat16 [256, 8, 2, 256], P('tok', 'col')
Inputs may be any that keep to these rules, and one draw needn't show every extreme that they name: `route`: at most 32 of the 128 rows of one index of tok name the same learner shard, and some learner shard is named by exactly 32 of them. `block_rows`: the 2 row blocks of one column block are distinct.
All inputs are finite; a program needn't handle non-finite values. Where the computation divides by a largest or mean magnitude, that divisor is 1e-20 or more.
Results may differ from a plain program's by a relative error of at most 0.017.
Values may be sent and summed in bfloat16 or wider, within the bound.
No kernel may reach another device: no remote copies, remote signals or barrier semaphores. Data moves between devices by JAX's collectives and lax.ppermute only.
A program may use at most 128 MiB of HBM per device.

v0:
```python
import jax
import jax.numpy as jnp
from jax import lax
from jax.sharding import PartitionSpec as P

BLK = 256
K = 2
RESP = 64
STEP = 1000


beta_first = 0.9
beta_second = 0.999
step_rate = 0.01
adam_eps = 1e-08
scale_eps = 1e-06


def silu_slope(operand):
    sigmoid_value = jax.nn.sigmoid(operand)
    return sigmoid_value * (1.0 + operand * (1.0 - sigmoid_value))


def dequant(code_rows, scales):
    row_count = code_rows.shape[0]
    block_count = scales.shape[0]
    width_blocks = scales.shape[1]
    block_of_row = jnp.arange(row_count, dtype=jnp.int32) // BLK
    selector = (block_of_row[:, None] == jnp.arange(block_count, dtype=jnp.int32)[None, :]).astype(
        jnp.float32
    )
    row_scales = jnp.dot(selector, scales, precision=lax.Precision.HIGHEST)
    spread = (
        code_rows.astype(jnp.float32).reshape(row_count, width_blocks, -1) * row_scales[:, :, None]
    )
    return spread.reshape(row_count, -1).astype(jnp.bfloat16)


def per_device(
    rollout,
    lengths,
    route,
    up_codes,
    up_scales,
    block_rows,
    delta,
    adam_m,
    adam_v,
    gate_pre,
    hidden_grad,
):
    peer_count = lax.axis_size("tok")
    send_rows = rollout.shape[0]
    row_width = rollout.shape[1]
    capacity = 2 * send_rows // peer_count
    row_ids = jnp.arange(send_rows, dtype=jnp.int32)
    seq_len = jnp.repeat(lengths, RESP)
    position = row_ids % RESP
    row_weight = jnp.where(position < seq_len, RESP / seq_len.astype(jnp.float32), 0.0)
    destination = route[:, 0]
    onehot = (destination[:, None] == jnp.arange(peer_count, dtype=jnp.int32)[None, :]).astype(
        jnp.int32
    )
    slot_index = jnp.sum((jnp.cumsum(onehot, axis=0) - 1) * onehot, axis=1)
    target = destination * capacity + slot_index
    weight_slots = (
        jnp.zeros((peer_count * capacity,), jnp.float32)
        .at[target]
        .set(row_weight)
        .reshape(peer_count, capacity)
    )
    buffer = (
        jnp.zeros((peer_count * capacity, row_width), jnp.bfloat16)
        .at[target]
        .set(rollout)
        .reshape(peer_count, capacity, row_width)
    )
    arrived, arrived_weight = (
        lax.all_to_all(buffer, "tok", split_axis=0, concat_axis=0, tiled=True),
        lax.all_to_all(
            weight_slots.astype(jnp.bfloat16), "tok", split_axis=0, concat_axis=0, tiled=True
        ).astype(weight_slots.dtype),
    )
    learn_x = arrived.reshape(peer_count * capacity, row_width)
    learn_w = arrived_weight.reshape(peer_count * capacity)
    rows_learn = learn_x.shape[0]
    column_count = up_codes.shape[1]
    blocks_here = column_count // BLK
    block_total = up_scales.shape[0]
    delta_full = lax.all_gather(delta.astype(jnp.bfloat16), "tok", axis=0, tiled=True)
    chosen = jnp.take(
        learn_x.reshape(rows_learn, block_total, BLK), block_rows.reshape(-1), axis=1
    ).reshape(rows_learn, blocks_here, K, BLK)
    activation = jax.nn.silu(gate_pre.astype(jnp.float32))
    up_grad = (hidden_grad.astype(jnp.float32) * activation * learn_w[:, None]).astype(jnp.bfloat16)
    up_grad_blocks = up_grad.reshape(rows_learn, blocks_here, BLK)
    delta_up = jnp.einsum(
        "rjkb,bjkc->rjc", chosen, delta_full, preferred_element_type=jnp.float32
    ).reshape(rows_learn, column_count)
    delta_back = jnp.einsum(
        "rjc,bjkc->rjkb", up_grad_blocks, delta_full, preferred_element_type=jnp.float32
    )
    selector = (
        block_rows.reshape(-1)[:, None] == jnp.arange(block_total, dtype=jnp.int32)[None, :]
    ).astype(jnp.float32)
    delta_input = jnp.einsum(
        "rqb,qd->rdb",
        delta_back.reshape(rows_learn, -1, BLK),
        selector,
        precision=lax.Precision.HIGHEST,
    ).reshape(rows_learn, row_width)
    weight = dequant(lax.all_gather(up_codes, "tok", axis=0, tiled=True), up_scales)
    base_up = jnp.dot(learn_x, weight, preferred_element_type=jnp.float32)
    weight = dequant(lax.all_gather(up_codes, "tok", axis=0, tiled=True), up_scales)
    base_input = lax.dot_general(
        up_grad, weight, (((1,), (1,)), ((), ())), preferred_element_type=jnp.float32
    )
    up_value = base_up + delta_up
    gate_grad = (
        hidden_grad.astype(jnp.float32)
        * up_value
        * silu_slope(gate_pre.astype(jnp.float32))
        * learn_w[:, None]
    ).astype(jnp.bfloat16)
    input_grad = lax.psum_scatter(
        base_input + delta_input, "col", scatter_dimension=1, tiled=True
    ).astype(jnp.bfloat16)
    owned_rows = BLK // peer_count
    summed_grad = lax.psum(
        jnp.einsum("rjkb,rjc->bjkc", chosen, up_grad_blocks, preferred_element_type=jnp.float32),
        "tok",
    )
    gradient = lax.dynamic_slice_in_dim(
        summed_grad, lax.axis_index("tok") * owned_rows, owned_rows, 0
    )
    new_m = beta_first * adam_m + (1.0 - beta_first) * gradient
    new_v = beta_second * adam_v + (1.0 - beta_second) * gradient * gradient
    corrected_m = new_m / (1.0 - beta_first**STEP)
    corrected_v = new_v / (1.0 - beta_second**STEP)
    new_delta = delta - step_rate * corrected_m / (jnp.sqrt(corrected_v) + adam_eps)
    local_max = jnp.max(jnp.abs(new_delta), axis=(0, 3))
    block_scale = lax.pmax(local_max, "tok")
    new_codes = (new_delta / (block_scale + scale_eps)[None, :, :, None]).astype(jnp.bfloat16)
    return (input_grad, gate_grad, new_delta, new_m, new_v, block_scale, new_codes)


def solution(mesh):
    placed = (
        P("tok", None),
        P("tok"),
        P("tok", None),
        P("tok", "col"),
        P(None, "col"),
        P("col", None),
        P("tok", "col", None, None),
        P("tok", "col", None, None),
        P("tok", "col", None, None),
        P("tok", "col"),
        P("tok", "col"),
    )
    return jax.shard_map(
        per_device,
        mesh=mesh,
        in_specs=placed,
        out_specs=(
            P("tok", "col"),
            P("tok", "col"),
            P("tok", "col", None, None),
            P("tok", "col", None, None),
            P("tok", "col", None, None),
            P("col", None),
            P("tok", "col", None, None),
        ),
        check_vma=False,
    )
```

profile of v0, /device:TPU:17, one launch (start us, length us, event | category | flops | bytes accessed | tf_op | source)
XLA Modules:
  0.0 273.1 jit_solution(436679259064735516)
XLA Ops:
  9.7 0.8 select_reduce_fusion
  11.2 1.0 scatter_custom_fusion
  12.8 4.4 %all-to-all-start = ((bf16[8,1,32]{2,1,0:T(2,128)(2,1)}), bf16[8,1,32]{2,1,0:T(2,128)(2,1)S(1)}, u32[]{:S(2)}, u32[]{:S(2)}) async-start(bf16[8,1,32]{2,1,0:T(2,128)(2,1)} %convert_element_type.79), calls=%async_computation | async-start | bytes 8192 | tf_op jit(solution)/shard_map/all_to_all | solution.py:80
  17.2 5.1 %scatter_custom_fusion.1 = bf16[256,5120]{1,0:T(8,128)(2,1)} fusion(s32[128]{0:T(128)S(1)} %fusion.30, bf16[128,5120]{1,0:T(8,128)(2,1)} %param.11, bf16[]{:T(256)} %constant.85.clone.1), kind=kCustom, calls=%fused_computation.7 | custom fusion | bytes 2621952 | tf_op jit(solution)/shard_map/scatter | solution.py:75
  22.4 4.2 %all-to-all-start.1 = ((bf16[8,32,5120]{2,1,0:T(8,128)(2,1)}), bf16[8,32,5120]{2,1,0:T(8,128)(2,1)S(1)}, u32[]{:S(2)}, u32[]{:S(2)}) async-start(bf16[8,32,5120]{2,1,0:T(8,128)(2,1)} %bitcast.47), calls=%async_computation.2 | async-start | bytes 5242880 | tf_op jit(solution)/shard_map/all_to_all | solution.py:79
  26.8 1.5 fusion.18
  28.3 6.1 %mul.101 = f32[5120,2,256]{2,1,0:T(2,128)S(1)} broadcast(f32[5120,2]{1,0:T(8,128)S(1)} %fusion.18), dimensions={0,1} | broadcast | bytes 10526720 | tf_op jit(solution)/shard_map/mul | solution.py:34
  34.4 5.2 %copy.109 = f32[640,8,2,256]{3,1,2,0:T(8,128)} copy(f32[640,8,2,256]{3,2,1,0:T(2,128)S(1)} %bitcast.44) | data formatting | bytes 20971520
  39.6 37.5 %all_gather.8 = bf16[256,2,2,256]{3,0,2,1:T(8,128)(2,1)S(1)} all-gather(bf16[32,2,2,256]{3,0,2,1:T(8,128)(2,1)S(1)} %copy.120), channel_id=1, replica_groups=mesh['tok'=8,'col'=4] {'tok'}, dimensions={0}, use_global_device_ids=true | all-gather | bytes 589824 | tf_op jit(solution)/shard_map/all_gather | solution.py:90
  77.2 1.2 fusion.8
  78.5 0.8 reshape.119
  79.2 1.8 copy.102
  81.1 1.3 fusion.38
  82.4 4.9 %convolution_bitcast_fusion = f32[256,20,256]{2,1,0:T(8,128)} fusion(f32[256,4,256]{2,0,1:T(8,128)S(1)} %bitcast.50, s32[4]{0:T(128)S(1)} %eq.59), kind=kOutput, calls=%fused_computation.5 | convolution fusion | flops 62914640 | bytes 6291472 | tf_op jit(solution)/shard_map/rqb,qd->rdb/dot_general | solution.py:106
  87.3 6.4 %copy.86 = f32[256,20,256]{0,2,1:T(8,128)} copy(f32[256,20,256]{2,1,0:T(8,128)} %convolution_bitcast_fusion) | data formatting | bytes 10485760 | tf_op jit(solution)/shard_map/rqb,qd->rdb/transpose | solution.py:106
  93.6 5.9 %copy.87 = f32[256,5120]{1,0:T(8,128)} copy(f32[256,5120]{0,1:T(8,128)} %bitcast.46) | data formatting | bytes 10485760 | tf_op jit(solution)/shard_map/reshape | solution.py:111
  99.5 3.0 %reshape_reshape.3 = bf16[256,20,256]{2,1,0:T(8,128)(2,1)} reshape(bf16[8,32,5120]{2,1,0:T(8,128)(2,1)S(1)} %all-to-all-done.1) | data formatting | bytes 5242880 | tf_op jit(solution)/shard_map/reshape;reshape | solution.py:92
  102.5 4.1 %copy.88 = bf16[256,20,256]{2,0,1:T(8,128)(2,1)} copy(bf16[256,20,256]{2,1,0:T(8,128)(2,1)} %reshape_reshape.3) | data formatting | bytes 5242880 | tf_op jit(solution)/shard_map/reshape;reshape | solution.py:92
  106.6 3.1 %gather_fusion = bf16[4,256,256]{2,1,0:T(8,128)(2,1)} fusion(bf16[256,20,256]{2,0,1:T(8,128)(2,1)} %copy.88, s32[1024]{0:T(1024)S(1)} %pad_clamp_fusion), kind=kCustom, calls=%fused_computation | custom fusion | bytes 1048592 | tf_op jit(solution)/shard_map/jit(_take)/gather | solution.py:91
  109.7 2.5 convolution_bitcast_fusion.1
  112.3 11.3 %convolution_add_fusion = f32[256,5120]{1,0:T(8,128)} fusion(f32[256,5120]{1,0:T(8,128)} %copy.87, bf16[256,512]{1,0:T(8,128)(2,1)S(1)} %fusion.8, f32[5120,512]{1,0:T(8,128)} %bitcast.42, bf16[5120,512]{1,0:T(8,128)(2,1)} %all-gather.2.cloned.1.call-done), kind=kOutput, calls=%fused_computation.4 | convolution fusion | flops 1351352320 | bytes 26476544 | tf_op jit(solution)/shard_map/dot_general | solution.py:115
  123.7 2.3 fusion.15
  126.0 1.2 copy.106
  127.2 40.3 %all-reduce.2.cloned.1.call-done = f32[256,2,2,256]{3,0,2,1:T(8,128)} async-done(((f32[256,2,2,256]{3,0,2,1:T(8,128)}), f32[256,2,2,256]{3,0,2,1:T(8,128)}) %all-reduce.2.cloned.1.call-update) | async-done | bytes 1048592 | tf_op jit(solution)/shard_map/psum | solution.py:129
  167.5 1.9 abs_reduce_fusion
  169.5 12.7 %pmax.7 = f32[2,2]{1,0:T(2,128)S(1)} all-reduce(f32[2,2]{1,0:T(2,128)S(1)} %get-tuple-element.42), channel_id=1, replica_groups=mesh['tok'=8,'col'=4] {'tok'}, use_global_device_ids=true, to_apply=%region_7.8 | all-reduce | flops 4 | bytes 32 | tf_op jit(solution)/shard_map/pmax | solution.py:142
  182.2 0.8 copy.95
  182.9 1.7 copy.96
  184.6 1.7 copy.97
  187.0 8.1 %fusion.5 = bf16[256,512]{1,0:T(8,128)(2,1)} fusion(f32[256,512]{1,0:T(8,128)S(1)} %copy.106, bf16[256,5120]{1,0:T(8,128)(2,1)S(1)} %bitcast.45, bf16[256,512]{1,0:T(8,128)(2,1)S(1)} %copy-done.2, bf16[256,512]{1,0:T(8,128)(2,1)} %param.20, f32[256]{0:T(256)S(1)} %reshape.126, f32[5120,512]{1,0:T(8,128)} %bitcast.43, ...), kind=kOutput, calls=%fused_computation.13 | convolution fusion | flops 1351876608 | bytes 19661824 | tf_op jit(solution)/shard_map/dot_general | solution.py:113
  195.1 69.2 %reduce-scatter.2.cloned.1.call-done = f32[256,1280]{1,0:T(8,128)} async-done(((f32[256,5120]{1,0:T(8,128)}), f32[256,1280]{1,0:T(8,128)}) %reduce-scatter.2.cloned.1.call-update) | async-done | bytes 1310736 | tf_op jit(solution)/shard_map/reduce_scatter | solution.py:125
  264.3 2.2 convert_element_type.75
  (41 shorter events, 5.0 us)
Async XLA Ops:
  7.2 19.6 %copy-start = (f32[20,2]{0,1:T(2,128)S(1)}, f32[20,2]{0,1:T(2,128)}, u32[]{:S(2)}) copy-start(f32[20,2]{0,1:T(2,128)} %param.15) | copy-start | bytes 484
  7.2 19.4 %copy-start.5 = (s32[2,2]{1,0:T(2,128)S(1)}, s32[2,2]{1,0:T(2,128)}, u32[]{:S(2)}) copy-start(s32[2,2]{1,0:T(2,128)} %param.16) | copy-start | bytes 52
  7.2 19.5 %copy-start.3 = (f32[32,2,2,256]{3,2,1,0:T(2,128)S(1)}, f32[32,2,2,256]{3,2,1,0:T(2,128)}, u32[]{:S(2)}) copy-start(f32[32,2,2,256]{3,2,1,0:T(2,128)} %param.17) | copy-start | bytes 393220
  7.2 105.1 %all-gather.2.cloned.1.call-start = ((), (), s32[]{:S(2)}) async-start(), calls=%async_computation.3 | async-start | bytes 5898240 | tf_op jit(solution)/shard_map/all_gather | solution.py:114
  12.8 9.5 %all-to-all-start = ((bf16[8,1,32]{2,1,0:T(2,128)(2,1)}), bf16[8,1,32]{2,1,0:T(2,128)(2,1)S(1)}, u32[]{:S(2)}, u32[]{:S(2)}) async-start(bf16[8,1,32]{2,1,0:T(2,128)(2,1)} %convert_element_type.79), calls=%async_computation | async-start | bytes 8192 | tf_op jit(solution)/shard_map/all_to_all | solution.py:80
  22.4 77.2 %all-to-all-start.1 = ((bf16[8,32,5120]{2,1,0:T(8,128)(2,1)}), bf16[8,32,5120]{2,1,0:T(8,128)(2,1)S(1)}, u32[]{:S(2)}, u32[]{:S(2)}) async-start(bf16[8,32,5120]{2,1,0:T(8,128)(2,1)} %bitcast.47), calls=%async_computation.2 | async-start | bytes 5242880 | tf_op jit(solution)/shard_map/all_to_all | solution.py:79
  26.6 141.0 %all-reduce.2.cloned.1.call-start = ((), (), s32[]{:S(2)}) async-start(), calls=%async_computation.5 | async-start | bytes 2097152 | tf_op jit(solution)/shard_map/psum | solution.py:129
  112.2 152.1 %reduce-scatter.2.cloned.1.call-start = ((), (), s32[]{:S(2)}) async-start(), calls=%async_computation.4 | async-start | bytes 6553600 | tf_op jit(solution)/shard_map/reduce_scatter | solution.py:125
  123.6 63.4 %copy-start.2 = (bf16[256,512]{1,0:T(8,128)(2,1)S(1)}, bf16[256,512]{1,0:T(8,128)(2,1)}, u32[]{:S(2)}) copy-start(bf16[256,512]{1,0:T(8,128)(2,1)} %param.21) | copy-start | bytes 786436
  182.2 12.9 %copy-start.4 = (f32[2,2]{1,0:T(2,128)}, f32[2,2]{1,0:T(2,128)S(1)}, u32[]{:S(2)}) copy-start(f32[2,2]{1,0:T(2,128)S(1)} %pmax.7) | copy-start | bytes 52
  187.0 79.5 %copy-start.1 = (f32[20,2]{0,1:T(2,128)S(1)}, f32[20,2]{0,1:T(2,128)}, u32[]{:S(2)}) copy-start(f32[20,2]{0,1:T(2,128)} %param.15) | copy-start | bytes 484
Sparse Core Ops, SparseCore 0:
  9.9 57.5 all-gather.1
  112.4 55.1 all-reduce.1
  169.9 94.4 reduce-scatter.1
where the time goes:
time: 275 us; the launch traced here: 273 us
  waiting for transfers between devices  110 us (40%)
  local copies, waits for them, and re-layouts  50.3 us (18%)
  blocking collectives  50.2 us (18%)
  matrix products  31.9 us (12%)
  between operations  13.9 us (5%)
  starting transfers between devices  8.68 us (3%)
  other arithmetic  7.88 us (3%)
    reduce_scatter x1, waiting for transfers between devices, per_device(): lax.psum_scatter(base_input + delta_input, 'col', scatter_dimension=1, ti...  69.2 us
    psum x1, waiting for transfers between devices, per_device(): lax.psum(jnp.einsum('rjkb,rjc->bjkc', chosen, up_grad_blocks, preferred_e...  40.3 us
    all_gather x1, blocking collectives, per_device(): lax.all_gather(delta.astype(jnp.bfloat16), 'tok', axis=0, tiled=True)  37.5 us
    pmax x1, blocking collectives, per_device(): block_scale = lax.pmax(local_max, 'tok')  12.7 us
    dot_general x1, matrix products, per_device(): lax.dot_general(up_grad, weight, (((1,), (1,)), ((), ())), preferred_elem...  11.3 us
    unnamed x18, local copies, waits for them, and re-layouts  10.1 us
    dot_general x1, matrix products, per_device(): base_up = jnp.dot(learn_x, weight, preferred_element_type=jnp.float32)  8.07 us
    another operation x2, local copies, waits for them, and re-layouts, per_device(): learn_x.reshape(rows_learn, block_total, BLK)  7.04 us
  transfers between devices with their start and end apart: 5, of which 2 were waited for; matrix products, arithmetic and copies ran while one was open for 32% of the time, Pallas kernels for 0%

commit v1 on v0

--- a/solution.py
+++ b/solution.py
@@ -1,6 +1,10 @@
+import functools
+
 import jax
 import jax.numpy as jnp
 from jax import lax
+from jax.experimental import pallas as pl
+from jax.experimental.pallas import tpu as pltpu
 from jax.sharding import PartitionSpec as P
 
 BLK = 256
@@ -36,7 +40,7 @@
     return spread.reshape(row_count, -1).astype(jnp.bfloat16)
 
 
-def per_device(
+def any_mesh(
     rollout,
     lengths,
     route,
@@ -144,6 +148,531 @@
     return (input_grad, gate_grad, new_delta, new_m, new_v, block_scale, new_codes)
 
 
+LANE = 128
+META = 16
+FAST_LIMIT = 64 * 1024 * 1024
+
+
+def call(kernel, out_shape, flops=0, moved=0, **extra):
+    return pl.pallas_call(
+        kernel,
+        out_shape=out_shape,
+        compiler_params=pltpu.CompilerParams(vmem_limit_bytes=FAST_LIMIT),
+        cost_estimate=pl.CostEstimate(flops=flops, bytes_accessed=moved, transcendentals=0),
+        **extra,
+    )
+
+
+VMEM = pl.BlockSpec(memory_space=pltpu.VMEM)
+SMEM = pl.BlockSpec(memory_space=pltpu.SMEM)
+HBM = pl.BlockSpec(memory_space=pltpu.HBM)
+AFTER = pl.BlockSpec(memory_space=pl.ANY)
+
+
+def own_place():
+    token = lax.axis_index("tok")
+    return token & 1, lax.shift_right_logical(token, 1)
+
+
+def fetch(pairs, sems):
+    copies = [pltpu.make_async_copy(*pair, sems.at[n]) for n, pair in enumerate(pairs)]
+    for copy in copies:
+        copy.start()
+    return copies
+
+
+def learner_kernel(gate_hbm, hidden_hbm, delta_hbm, out_ref, gate_ref, hidden_ref, delta_ref, sems):
+    copies = fetch([(gate_hbm, gate_ref), (hidden_hbm, hidden_ref), (delta_hbm, delta_ref)], sems)
+    peers, _, width = out_ref.shape
+    cap = gate_ref.shape[0] // peers
+    owned = delta_ref.shape[0]
+    copies[0].wait()
+    copies[1].wait()
+    gate = gate_ref[...].astype(jnp.float32)
+    raw = hidden_ref[...].astype(jnp.float32) * gate / (1.0 + jnp.exp(-gate))
+    out_ref[:, :cap, :] = raw.astype(jnp.bfloat16).reshape(peers, cap, width)
+    copies[2].wait()
+    for j in range(delta_ref.shape[1]):
+        for k in range(K):
+            half = delta_ref[:, j, k, :].astype(jnp.bfloat16)
+            for peer in range(k, peers, K):
+                out_ref[peer, cap:, j * BLK : (j + 1) * BLK] = half
+
+
+def place_matrix(target_row, slots):
+    rows = target_row.shape[1]
+    ids = lax.broadcasted_iota(jnp.int32, (slots, rows), 0)
+    return (ids == target_row).astype(jnp.bfloat16)
+
+
+def as_column(row):
+    size = row.shape[1]
+    first = lax.broadcasted_iota(jnp.int32, (size, size), 0)
+    second = lax.broadcasted_iota(jnp.int32, (size, size), 1)
+    return jnp.sum(jnp.where(first == second, row, 0.0), axis=1, keepdims=True)
+
+
+def weight_of(length_row):
+    position = lax.rem(lax.broadcasted_iota(jnp.int32, length_row.shape, 1), RESP)
+    return jnp.where(position.astype(jnp.float32) < length_row, RESP / length_row, 0.0)
+
+
+def sender_kernel(lengths_ref, route_ref, arrived_hbm, out_ref, raw_ref, delta_ref, sems):
+    peers, cap, width = raw_ref.shape
+    rows = route_ref.shape[1]
+    copies = fetch([(arrived_hbm.at[:, :cap, :], raw_ref), (arrived_hbm.at[:, cap:, :], delta_ref)], sems)
+    route = route_ref[...]
+    named = (lax.broadcasted_iota(jnp.int32, (max(peers, 16), rows), 0) == route).astype(jnp.float32)
+    before = (
+        lax.broadcasted_iota(jnp.int32, (rows, rows), 0)
+        < lax.broadcasted_iota(jnp.int32, (rows, rows), 1)
+    ).astype(jnp.bfloat16)
+    ranks = jnp.dot(named.astype(jnp.bfloat16), before, preferred_element_type=jnp.float32)
+    slot = jnp.sum(named * ranks, axis=0, keepdims=True).astype(jnp.int32)
+    target = route * cap + slot
+    row_ids = lax.broadcasted_iota(jnp.int32, (1, rows), 1)
+    length_row = jnp.zeros((1, rows), jnp.float32)
+    for seq in range(rows // RESP):
+        mine = (row_ids >= seq * RESP) & (row_ids < (seq + 1) * RESP)
+        length_row = jnp.where(mine, lengths_ref[seq].astype(jnp.float32), length_row)
+    place = place_matrix(target, peers * cap)
+    copies[0].wait()
+    raw = raw_ref[...].reshape(peers * cap, width)
+    picked = lax.dot_general(
+        place, raw, (((0,), (0,)), ((), ())), preferred_element_type=jnp.float32
+    )
+    out_ref[:rows, :] = (picked * as_column(weight_of(length_row))).astype(jnp.bfloat16)
+    out_ref[rows : rows + META, :] = jnp.zeros((META, width), jnp.bfloat16)
+    meta_ids = lax.broadcasted_iota(jnp.int32, (META, rows), 0)
+    meta = jnp.where(meta_ids == 0, target.astype(jnp.float32), 0.0)
+    meta = jnp.where(meta_ids == 1, length_row, meta)
+    out_ref[rows : rows + META, :rows] = meta.astype(jnp.bfloat16)
+    copies[1].wait()
+    out_ref[rows + META :, :] = delta_ref[...].reshape(-1, width)
+
+
+def gradient_kernel(rows_ref, own_x, mate_x, own_up, mate_up, *refs):
+    out_refs, (held_ref, x_ref, up_ref, sems) = refs[:-4], refs[-4:]
+    chips, spots, owned, width = held_ref.shape
+    rows = own_x.shape[0]
+    pairs = []
+    for seat, (x_hbm, up_hbm) in enumerate(((own_x, own_up), (mate_x, mate_up))):
+        lines = slice(seat * rows, (seat + 1) * rows)
+        pairs.append((up_hbm.at[:rows, :], up_ref.at[lines]))
+        for spot in range(spots):
+            lanes = pl.ds(pl.multiple_of(rows_ref[spot // K, spot % K] * BLK, BLK), BLK)
+            pairs.append((x_hbm.at[:, lanes], x_ref.at[spot, lines]))
+    for copy in fetch(pairs, sems):
+        copy.wait()
+    core, own_chip = own_place()
+    for spot in range(spots):
+        j = spot // K
+        full = lax.dot_general(
+            x_ref[spot],
+            up_ref[:, j * BLK : (j + 1) * BLK],
+            (((0,), (0,)), ((), ())),
+            preferred_element_type=jnp.float32,
+        ).reshape(chips, 2, owned, width)
+        held_ref[:, spot] = jnp.where(core == 0, full[:, 0], full[:, 1]).astype(jnp.bfloat16)
+    for distance, out_ref in enumerate(out_refs):
+        out_ref[...] = held_ref[own_chip ^ distance]
+
+
+def adam_kernel(delta_hbm, m_hbm, v_hbm, *refs):
+    delta_out, m_out, v_out, max_out, delta_ref, m_ref, v_ref, grad_ref, sems = refs[-9:]
+    chips = grad_ref.shape[0]
+    pairs = [(delta_hbm, delta_ref), (m_hbm, m_ref), (v_hbm, v_ref)]
+    for copy in fetch(pairs + [(refs[chip], grad_ref.at[chip]) for chip in range(chips)], sems):
+        copy.wait()
+    ids = lax.broadcasted_iota(jnp.int32, max_out.shape, 1)
+    tops = jnp.zeros(max_out.shape, jnp.float32)
+    for j in range(delta_ref.shape[1]):
+        for k in range(K):
+            spot = j * K + k
+            gradient = grad_ref[0, spot].astype(jnp.float32)
+            for chip in range(1, chips):
+                gradient = gradient + grad_ref[chip, spot].astype(jnp.float32)
+            new_m = beta_first * m_ref[:, j, k, :] + (1.0 - beta_first) * gradient
+            new_v = beta_second * v_ref[:, j, k, :] + (1.0 - beta_second) * gradient * gradient
+            corrected_m = new_m / (1.0 - beta_first**STEP)
+            corrected_v = new_v / (1.0 - beta_second**STEP)
+            new_delta = delta_ref[:, j, k, :] - step_rate * corrected_m / (
+                jnp.sqrt(corrected_v) + adam_eps
+            )
+            m_out[:, j, k, :] = new_m
+            v_out[:, j, k, :] = new_v
+            delta_out[:, j, k, :] = new_delta
+            tops = jnp.where(ids == spot, jnp.max(jnp.abs(new_delta)), tops)
+    high = tops.astype(jnp.bfloat16).astype(jnp.float32)
+    middle = (tops - high).astype(jnp.bfloat16).astype(jnp.float32)
+    low = tops - high - middle
+    kinds = lax.broadcasted_iota(jnp.int32, max_out.shape, 0)
+    tops = jnp.where(kinds == 0, high, jnp.where(kinds == 1, middle, low))
+    max_out[...] = jnp.where(kinds < 3, tops, 0.0).astype(jnp.bfloat16)
+
+
+def block_order(core, step):
+    return (0, 1 + core, 2 - core, 3)[step]
+
+
+def product_kernel(scales_ref, rows_ref, own_up, mate_up, *refs, steps, rows):
+    last = steps[-1] == 3
+    codes_hbm, refs = refs[: len(steps)], refs[len(steps) :]
+    if last:
+        refs = refs[4:]
+        weight_out, *back_refs = refs[:5]
+    else:
+        own_x, mate_x, sum_ref, *back_refs = refs[:7]
+    codes, weight, up, delta, sems, *rest = refs[5 if last else 7 :]
+    core, own_chip = own_place()
+    turn = own_chip ^ lax.axis_index("col")
+    size, width = weight.shape[1:]
+    tiles = size // LANE
+    pairs = []
+    for seat, up_hbm in enumerate((own_up, mate_up)):
+        pairs.append((up_hbm.at[:rows, :], up.at[seat * rows : (seat + 1) * rows]))
+        pairs.append((up_hbm.at[rows + META :, :], delta.at[core ^ seat]))
+    shared = len(pairs)
+    each = 1 if last else 3
+    starts = []
+    for spot, step in enumerate(steps):
+        first_tile = (2 * (own_chip ^ block_order(core, step)) + core) * tiles
+        starts.append(first_tile)
+        pairs.append((codes_hbm[spot], codes.at[spot]))
+        if not last:
+            lanes = pl.ds(pl.multiple_of(first_tile * LANE, LANE), size)
+            pairs.append((own_x.at[:, lanes], rest[0].at[spot, :rows]))
+            pairs.append((mate_x.at[:, lanes], rest[0].at[spot, rows:]))
+    copies = fetch(pairs, sems)
+    for spot, step in enumerate(steps):
+        for copy in copies[shared + each * spot : shared + each * (spot + 1)]:
+            copy.wait()
+        for tile in range(tiles):
+            block = lax.div(starts[spot] + tile, BLK // LANE)
+            lines = slice(tile * LANE, (tile + 1) * LANE)
+            for j in range(width // BLK):
+                lanes = slice(j * BLK, (j + 1) * BLK)
+                plain = codes[spot, lines, lanes].astype(jnp.float32) * scales_ref[j, block]
+                weight[spot, lines, lanes] = plain.astype(jnp.bfloat16)
+        if spot == 0:
+            for copy in copies[:shared]:
+                copy.wait()
+        for j in range(width // BLK):
+            lanes = slice(j * BLK, (j + 1) * BLK)
+            for k in range(K):
+                for piece in range(BLK // LANE):
+                    tile = rows_ref[j, k] * (BLK // LANE) + piece - starts[spot]
+
+                    @pl.when((tile >= 0) & (tile < tiles))
+                    def _():
+                        lines = pl.ds(pl.multiple_of(tile * LANE, LANE), LANE)
+                        extra = delta[k, piece * LANE : (piece + 1) * LANE, lanes].astype(jnp.float32)
+                        held = weight[spot, lines, lanes].astype(jnp.float32)
+                        weight[spot, lines, lanes] = (held + extra).astype(jnp.bfloat16)
+
+        back = lax.dot_general(
+            up[...], weight[spot], (((1,), (1,)), ((), ())), preferred_element_type=jnp.float32
+        ).astype(jnp.bfloat16)
+        if last:
+            rest[0][...] = back
+            weight_copy = pltpu.make_async_copy(weight.at[spot], weight_out, rest[1].at[1])
+            weight_copy.start()
+        for shift, back_ref in enumerate(back_refs):
+
+            @pl.when((turn ^ block_order(core, step)) == shift)
+            def _():
+                if last:
+                    back_copy = pltpu.make_async_copy(rest[0], back_ref, rest[1].at[0])
+                    back_copy.start()
+                    back_copy.wait()
+                else:
+                    back_ref[...] = back
+
+        if last:
+            weight_copy.wait()
+        elif spot == 0:
+            sum_ref[...] = jnp.dot(rest[0][spot], weight[spot], preferred_element_type=jnp.float32)
+        else:
+            sum_ref[...] += jnp.dot(rest[0][spot], weight[spot], preferred_element_type=jnp.float32)
+
+
+def products(steps, scales, block_rows, own_up, mate_up, codes, *more):
+    size, width = codes[0].shape
+    rows = own_up.shape[0] - META - BLK
+    count = len(steps)
+    last = steps[-1] == 3
+    back = jax.ShapeDtypeStruct((2 * rows, size), jnp.bfloat16)
+    if last:
+        first = jax.ShapeDtypeStruct((size, width), jnp.bfloat16)
+        rest = [pltpu.VMEM(back.shape, jnp.bfloat16), pltpu.SemaphoreType.DMA((2,))]
+    else:
+        first = jax.ShapeDtypeStruct((2 * rows, width), jnp.float32)
+        rest = [pltpu.VMEM((count, 2 * rows, size), jnp.bfloat16)]
+    return call(
+        functools.partial(product_kernel, steps=steps, rows=rows),
+        [first] + [back] * 4,
+        in_specs=[SMEM] * 2 + [HBM] * (2 + count + len(more)),
+        out_specs=[HBM if last else VMEM] * 5,
+        scratch_shapes=[
+            pltpu.VMEM((count, size, width), jnp.bfloat16),
+            pltpu.VMEM((count, size, width), jnp.bfloat16),
+            pltpu.VMEM((2 * rows, width), jnp.bfloat16),
+            pltpu.VMEM((K, BLK, width), jnp.bfloat16),
+            pltpu.SemaphoreType.DMA((4 + 3 * count,)),
+        ]
+        + rest,
+        input_output_aliases={4 + count + n: 1 + n for n in range(4)} if last else {},
+    )(scales, block_rows, own_up, mate_up, *codes, *more)
+
+
+def forward_kernel(own_x, mate_x, weight_hbm, sum_hbm, own_out, mate_out, x, weight, total, sems):
+    size = weight.shape[0]
+    rows = own_out.shape[0]
+    core, own_chip = own_place()
+    lanes = pl.ds(pl.multiple_of((2 * (own_chip ^ 3) + core) * size, LANE), size)
+    pairs = [(own_x.at[:, lanes], x.at[:rows]), (mate_x.at[:, lanes], x.at[rows:])]
+    for copy in fetch(pairs + [(weight_hbm, weight), (sum_hbm, total)], sems):
+        copy.wait()
+    full = total[...] + jnp.dot(x[...], weight[...], preferred_element_type=jnp.float32)
+    own_out[...] = full[:rows]
+    mate_out[...] = full[rows:]
+
+
+def spread_up_kernel(own_up, own_sum, other_sum, tops_ref, out_ref):
+    peers, lines, _ = out_ref.shape
+    rows, width = own_sum.shape
+    cap, half = lines // 2, width // 2
+    target = own_up[rows : rows + META, :rows].astype(jnp.float32)
+    place = place_matrix(target[0:1].astype(jnp.int32), peers * cap)
+    value = (own_sum[...] + other_sum[...]) * as_column(weight_of(target[1:2]))
+    placed = jnp.dot(place, value.astype(jnp.bfloat16), preferred_element_type=jnp.float32)
+    placed = placed.astype(jnp.bfloat16).reshape(peers, cap, width)
+    for side in range(2):
+        out_ref[:, side * cap : (side + 1) * cap, :half] = placed[:, :, side * half : (side + 1) * half]
+    for peer in range(peers):
+        out_ref[peer, :META, half:] = tops_ref[...]
+        out_ref[peer, META:, half:] = jnp.zeros((lines - META, LANE), jnp.bfloat16)
+
+
+def spread_kernel(own_up, mate_up, up_slots, *refs):
+    parts_hbm, out_refs = refs[:4], refs[4:-4]
+    held_ref, meta_ref, parts_ref, sems = refs[-4:]
+    _, rows, size = parts_ref.shape
+    rows = rows // 2
+    peers = held_ref.shape[0]
+    cap = 2 * rows // peers
+    core, _ = own_place()
+    token = lax.axis_index("tok")
+    pairs = [(up.at[rows : rows + META, :rows], meta_ref.at[seat]) for seat, up in enumerate((own_up, mate_up))]
+    pairs += [(part, parts_ref.at[n]) for n, part in enumerate(parts_hbm)]
+    pairs += [(up_slots.at[token ^ d], far.at[:, size:]) for d, far in enumerate(out_refs)]
+    copies = fetch(pairs, sems)
+    for copy in copies[: 2 + len(parts_hbm)]:
+        copy.wait()
+    for seat in range(2):
+        lines = slice(seat * rows, (seat + 1) * rows)
+        summed = parts_ref[0, lines].astype(jnp.float32)
+        for part in range(1, len(parts_hbm)):
+            summed = summed + parts_ref[part, lines].astype(jnp.float32)
+        target = meta_ref[seat].astype(jnp.float32)
+        place = place_matrix(target[0:1].astype(jnp.int32), peers * cap)
+        placed = jnp.dot(place, summed.astype(jnp.bfloat16), preferred_element_type=jnp.float32)
+        start = pl.multiple_of((core ^ seat) * cap, cap)
+        held_ref[:, pl.ds(start, cap), :] = placed.astype(jnp.bfloat16).reshape(peers, cap, size)
+    for d, far_ref in enumerate(out_refs):
+        far_ref[:, :size] = held_ref[token ^ d]
+    for copy in copies[2 + len(parts_hbm) :]:
+        copy.wait()
+
+
+def finish_kernel(gate_hbm, hidden_hbm, delta_hbm, *refs):
+    arrived_refs = refs[:-8]
+    input_out, gate_out, scale_out, codes_out, gate_ref, hidden_ref, delta_ref, sems = refs[-8:]
+    copies = fetch([(gate_hbm, gate_ref), (hidden_hbm, hidden_ref), (delta_hbm, delta_ref)], sems)
+    size = input_out.shape[1] // 2
+    cap = gate_ref.shape[0] // len(arrived_refs)
+    half = gate_ref.shape[1] // 2
+    token = lax.axis_index("tok")
+    for distance, arrived_ref in enumerate(arrived_refs):
+        sender = token ^ distance
+        lines = pl.ds(pl.multiple_of((sender >> 1) * 2 * cap, 2 * cap), 2 * cap)
+        lanes = pl.ds(pl.multiple_of((sender & 1) * size, LANE), size)
+        input_out[lines, lanes] = arrived_ref[:, :size]
+    for copy in copies:
+        copy.wait()
+    tops = jnp.zeros((1, LANE), jnp.float32)
+    for distance, arrived_ref in enumerate(arrived_refs):
+        sender = token ^ distance
+        lines = pl.ds(pl.multiple_of(sender * cap, cap), cap)
+        for side in range(2):
+            lanes = slice(side * half, (side + 1) * half)
+            gate = gate_ref[lines, lanes].astype(jnp.float32)
+            sigmoid_value = 1.0 / (1.0 + jnp.exp(-gate))
+            slope = sigmoid_value * (1.0 + gate * (1.0 - sigmoid_value))
+            value = arrived_ref[side * cap : (side + 1) * cap, size : size + half].astype(jnp.float32)
+            hidden = hidden_ref[lines, lanes].astype(jnp.float32)
+            gate_out[lines, lanes] = (hidden * value * slope).astype(jnp.bfloat16)
+        kinds = arrived_ref[:META, size + half :].astype(jnp.float32)
+        tops = jnp.maximum(tops, kinds[0:1] + kinds[1:2] + kinds[2:3])
+    lanes = lax.broadcasted_iota(jnp.int32, (1, LANE), 1)
+    first = lax.broadcasted_iota(jnp.int32, scale_out.shape, 0)
+    second = lax.broadcasted_iota(jnp.int32, scale_out.shape, 1)
+    scales = jnp.zeros(scale_out.shape, jnp.float32)
+    for j in range(delta_ref.shape[1]):
+        for k in range(K):
+            top = jnp.max(jnp.where(lanes == j * K + k, tops, 0.0))
+            scales = jnp.where((first == j) & (second == k), top, scales)
+            codes_out[:, j, k, :] = (delta_ref[:, j, k, :] / (top + scale_eps)).astype(jnp.bfloat16)
+    scale_out[...] = scales
+
+
+def paired(
+    peer_count, rollout, lengths, route, up_codes, up_scales, block_rows, delta, adam_m, adam_v, gate_pre, hidden_grad
+):
+    send_rows, row_width = rollout.shape
+    cap = 2 * send_rows // peer_count
+    chips = peer_count // 2
+    owned = BLK // peer_count
+    own_rows, width = up_codes.shape
+    mates = [(t, t ^ 1) for t in range(peer_count)]
+    scales = up_scales.T
+    spots = block_rows.size
+
+    def hop(codes, turned):
+        return lax.ppermute(codes, "tok", [(t, t ^ (4 if (t & 1) ^ turned else 2)) for t in range(peer_count)])
+
+    codes_near = hop(up_codes, 0)
+    codes_side = hop(up_codes, 1)
+    mate_x = lax.ppermute(rollout, "tok", mates)
+    first_out = call(
+        learner_kernel,
+        jax.ShapeDtypeStruct((peer_count, cap + owned, width), jnp.bfloat16),
+        in_specs=[HBM] * 3,
+        out_specs=VMEM,
+        scratch_shapes=[
+            pltpu.VMEM(gate_pre.shape, jnp.bfloat16),
+            pltpu.VMEM(hidden_grad.shape, jnp.bfloat16),
+            pltpu.VMEM(delta.shape, jnp.float32),
+            pltpu.SemaphoreType.DMA((3,)),
+        ],
+    )(gate_pre, hidden_grad, delta)
+    arrived = lax.all_to_all(first_out, "tok", split_axis=0, concat_axis=0, tiled=True)
+    own_up = call(
+        sender_kernel,
+        jax.ShapeDtypeStruct((send_rows + META + BLK, width), jnp.bfloat16),
+        in_specs=[SMEM, VMEM, HBM],
+        out_specs=VMEM,
+        scratch_shapes=[
+            pltpu.VMEM((peer_count, cap, width), jnp.bfloat16),
+            pltpu.VMEM((peer_count, owned, width), jnp.bfloat16),
+            pltpu.SemaphoreType.DMA((2,)),
+        ],
+    )(lengths, route.reshape(1, send_rows), arrived)
+    mate_up = lax.ppermute(own_up, "tok", mates)
+
+    codes_far = hop(codes_near, 1)
+    shared = (scales, block_rows, own_up, mate_up)
+    early_sum, *backs = products((0, 1, 2), *shared, [up_codes, codes_near, codes_side], rollout, mate_x)
+    weight_far, *backs = products((3,), *shared, [codes_far], *backs)
+    parts = [backs[0]]
+    for shift in range(1, chips):
+        parts.append(lax.ppermute(backs[shift], "col", [(z, z ^ shift) for z in range(chips)]))
+    own_sum, mate_sum = call(
+        forward_kernel,
+        [jax.ShapeDtypeStruct((send_rows, width), jnp.float32)] * 2,
+        in_specs=[HBM] * 4,
+        out_specs=[VMEM] * 2,
+        scratch_shapes=[
+            pltpu.VMEM((2 * send_rows, own_rows), jnp.bfloat16),
+            pltpu.VMEM((own_rows, width), jnp.bfloat16),
+            pltpu.VMEM((2 * send_rows, width), jnp.float32),
+            pltpu.SemaphoreType.DMA((4,)),
+        ],
+    )(rollout, mate_x, weight_far, early_sum)
+    other_sum = lax.ppermute(mate_sum, "tok", mates)
+
+    gradient_parts = call(
+        gradient_kernel,
+        [jax.ShapeDtypeStruct((spots, owned, BLK), jnp.bfloat16)] * chips,
+        in_specs=[SMEM] + [HBM] * 4,
+        out_specs=[VMEM] * chips,
+        scratch_shapes=[
+            pltpu.VMEM((chips, spots, owned, BLK), jnp.bfloat16),
+            pltpu.VMEM((spots, 2 * send_rows, BLK), jnp.bfloat16),
+            pltpu.VMEM((2 * send_rows, width), jnp.bfloat16),
+            pltpu.SemaphoreType.DMA((2 * spots + 2,)),
+        ],
+    )(block_rows, rollout, mate_x, own_up, mate_up)
+    gradient_arrived = [gradient_parts[0]] + [
+        lax.ppermute(gradient_parts[step], "tok", [(t, t ^ (2 * step)) for t in range(peer_count)])
+        for step in range(1, chips)
+    ]
+    moment = jax.ShapeDtypeStruct(delta.shape, jnp.float32)
+    new_delta, new_m, new_v, tops = call(
+        adam_kernel,
+        (moment, moment, moment, jax.ShapeDtypeStruct((META, LANE), jnp.bfloat16)),
+        in_specs=[HBM] * (3 + chips),
+        out_specs=(VMEM,) * 4,
+        scratch_shapes=[pltpu.VMEM(delta.shape, jnp.float32)] * 3
+        + [pltpu.VMEM((chips, spots, owned, BLK), jnp.bfloat16), pltpu.SemaphoreType.DMA((3 + chips,))],
+    )(delta, adam_m, adam_v, *gradient_arrived)
+
+    up_slots = call(
+        spread_up_kernel,
+        jax.ShapeDtypeStruct((peer_count, 2 * cap, width // 2 + LANE), jnp.bfloat16),
+        in_specs=[VMEM] * 4,
+        out_specs=VMEM,
+    )(own_up, own_sum, other_sum, tops)
+    spread_width = own_rows + width // 2 + LANE
+    slots = call(
+        spread_kernel,
+        [jax.ShapeDtypeStruct((2 * cap, spread_width), jnp.bfloat16)] * peer_count,
+        in_specs=[HBM] * (3 + len(parts)),
+        out_specs=[VMEM] * peer_count,
+        scratch_shapes=[
+            pltpu.VMEM((peer_count, 2 * cap, own_rows), jnp.bfloat16),
+            pltpu.VMEM((2, META, send_rows), jnp.bfloat16),
+            pltpu.VMEM((len(parts), 2 * send_rows, own_rows), jnp.bfloat16),
+            pltpu.SemaphoreType.DMA((2 + len(parts) + peer_count,)),
+        ],
+    )(own_up, mate_up, up_slots, *parts)
+    sent = [slots[0]] + [
+        lax.ppermute(slots[distance], "tok", [(t, t ^ distance) for t in range(peer_count)])
+        for distance in range(1, peer_count)
+    ]
+    input_grad, gate_grad, delta_scale, delta_codes = call(
+        finish_kernel,
+        (
+            jax.ShapeDtypeStruct((peer_count * cap, 2 * own_rows), jnp.bfloat16),
+            jax.ShapeDtypeStruct(gate_pre.shape, jnp.bfloat16),
+            jax.ShapeDtypeStruct(block_rows.shape, jnp.float32),
+            jax.ShapeDtypeStruct(delta.shape, jnp.bfloat16),
+        ),
+        in_specs=[HBM] * 3 + [VMEM] * peer_count,
+        out_specs=(VMEM,) * 4,
+        scratch_shapes=[
+            pltpu.VMEM(gate_pre.shape, jnp.bfloat16),
+            pltpu.VMEM(hidden_grad.shape, jnp.bfloat16),
+            pltpu.VMEM(delta.shape, jnp.float32),
+            pltpu.SemaphoreType.DMA((3,)),
+        ],
+    )(gate_pre, hidden_grad, new_delta, *sent)
+    return (input_grad, gate_grad, new_delta, new_m, new_v, delta_scale, delta_codes)
+
+
+def per_device(tok_size, col_size, *arrays):
+    rollout, up_codes = arrays[0], arrays[3]
+    fits = (
+        tok_size == 8 and col_size == 4
+        and rollout.shape[0] == LANE
+        and up_codes.shape[0] % LANE == 0
+        and up_codes.shape[1] % BLK == 0
+    )
+    if fits:
+        return paired(tok_size, *arrays)
+    return any_mesh(*arrays)
+
+
 def solution(mesh):
     placed = (
         P("tok", None),
@@ -159,7 +688,7 @@
         P("tok", "col"),
     )
     return jax.shard_map(
-        per_device,
+        functools.partial(per_device, mesh.shape["tok"], mesh.shape["col"]),
         mesh=mesh,
         in_specs=placed,
         out_specs=(

time: 275 us -> 90.3 us (0.33)
  waiting for transfers between devices: 110 us -> 28.8 us
  local copies, waits for them, and re-layouts: 50.3 us -> 0 us
  blocking collectives: 50.2 us -> 0 us
  matrix products: 31.9 us -> 0 us
  Pallas kernels: 0 us -> 30.7 us
  starting transfers between devices: 8.68 us -> 29.6 us
  between operations: 13.9 us -> 0.72 us
  other arithmetic: 7.88 us -> 0 us
    reduce_scatter x1 -> x0, waiting for transfers between devices: 69.2 us -> none  [per_device(): lax.psum_scatter(base_input + delta_input, 'col', scatter_dimension=1, ti...]
    psum x1 -> x0, waiting for transfers between devices: 40.3 us -> none  [per_device(): lax.psum(jnp.einsum('rjkb,rjc->bjkc', chosen, up_grad_blocks, preferred_e...]
    all_gather x1 -> x0, blocking collectives: 37.5 us -> none  [per_device(): lax.all_gather(delta.astype(jnp.bfloat16), 'tok', axis=0, tiled=True)]
    dot_general x7 -> x0, matrix products: 31.9 us -> none  [the longest x1 11.3 us: per_device(): lax.dot_general(up_grad, weight, (((1,), (1,)), ((), ())), preferred_elem...]
    pallas_call x0 -> x10, Pallas kernels: none -> 30.7 us  [the longest x2 9.59 us: products(): call(functools.partial(product_kernel, steps=steps, rows=rows), [first] +...]
    ppermute x0 -> x19, waiting for transfers between devices: none -> 25.5 us  [the longest x3 8.81 us: paired(): lax.ppermute(gradient_parts[step], 'tok', [(t, t ^ 2 * step) for t in ran...]
    ppermute x0 -> x19, starting transfers between devices: none -> 25.2 us  [the longest x7 8.79 us: paired(): lax.ppermute(slots[distance], 'tok', [(t, t ^ distance) for t in range(pe...]
    pmax x1 -> x0, blocking collectives: 12.7 us -> none  [per_device(): block_scale = lax.pmax(local_max, 'tok')]
  transfers between devices with their start and end apart: 5 -> 20, of which waited for: 2 -> 11; matrix products, arithmetic and copies ran while one was open for 32% -> 0% of each run, Pallas kernels for 0% -> 23%
where the time goes in v1:
time: 90.3 us; the launch traced here: 89.8 us
  Pallas kernels  30.7 us (34%)
  starting transfers between devices  29.6 us (33%)
  waiting for transfers between devices  28.8 us (32%)
    pallas_call x2, Pallas kernels, products(): call(functools.partial(product_kernel, steps=steps, rows=rows), [first] +...  9.59 us
    ppermute x3, waiting for transfers between devices, paired(): lax.ppermute(gradient_parts[step], 'tok', [(t, t ^ 2 * step) for t in ran...  8.81 us
    ppermute x7, starting transfers between devices, paired(): lax.ppermute(slots[distance], 'tok', [(t, t ^ distance) for t in range(pe...  8.79 us
    ppermute x7, waiting for transfers between devices, paired(): lax.ppermute(slots[distance], 'tok', [(t, t ^ distance) for t in range(pe...  7.42 us
    ppermute x3, waiting for transfers between devices, paired(): lax.ppermute(backs[shift], 'col', [(z, z ^ shift) for z in range(chips)])  4.87 us
    all_to_all x1, starting transfers between devices, paired(): lax.all_to_all(first_out, 'tok', split_axis=0, concat_axis=0, tiled=True)  4.35 us
    ppermute x3, waiting for transfers between devices, hop(): lax.ppermute(codes, 'tok', [(t, t ^ (4 if t & 1 ^ turned else 2)) for t i...  4.35 us
    ppermute x3, starting transfers between devices, hop(): lax.ppermute(codes, 'tok', [(t, t ^ (4 if t & 1 ^ turned else 2)) for t i...  3.84 us
  transfers between devices with their start and end apart: 20, of which 11 were waited for; matrix products, arithmetic and copies ran while one was open for 0% of the time, Pallas kernels for 23%

profile of v1, /device:TPU:17, one launch (start us, length us, event | category | flops | bytes accessed | tf_op | source)
XLA Modules:
  0.0 89.8 jit_solution(17711876827114646772)
XLA Ops:
  1.4 1.2 %collective-permute-start.5 = (bf16[640,512]{1,0:T(8,128)(2,1)}, bf16[640,512]{1,0:T(8,128)(2,1)}, u32[]{:S(2)}, u32[]{:S(2)}) collective-permute-start(bf16[640,512]{1,0:T(8,128)(2,1)} %refs_0_.1), channel_id=1, source_target_pairs={{0,8},{4,20},{8,0},{12,28},{16,24},{20,4},{24,16},{28,12},{1,9},{5... | collective-permute-start | bytes 1966088 | tf_op jit(solution)/shard_map/ppermute | solution.py:542
  2.6 2.2 %shard_map.162 = bf16[8,64,512]{2,1,0:T(8,128)(2,1)} custom-call(bf16[256,512]{1,0:T(8,128)(2,1)} %gate_hbm.3, bf16[256,512]{1,0:T(8,128)(2,1)} %hidden_hbm.3, f32[32,2,2,256]{3,2,1,0:T(2,128)} %delta_hbm.3), custom_call_target="tpu_custom_call" | custom-call | tf_op jit(solution)/shard_map/pallas_call | solution.py:547
  4.8 4.4 %all-to-all-start = ((bf16[8,64,512]{2,1,0:T(8,128)(2,1)}), bf16[8,64,512]{2,1,0:T(8,128)(2,1)}, u32[]{:S(2)}, u32[]{:S(2)}) async-start(bf16[8,64,512]{2,1,0:T(8,128)(2,1)} %shard_map.162), calls=%async_computation | async-start | bytes 1048576 | tf_op jit(solution)/shard_map/all_to_all | solution.py:559
  9.1 1.4 %collective-permute-start.7 = (bf16[640,512]{1,0:T(8,128)(2,1)}, bf16[640,512]{1,0:T(8,128)(2,1)}, u32[]{:S(2)}, u32[]{:S(2)}) collective-permute-start(bf16[640,512]{1,0:T(8,128)(2,1)} %refs_0_.1), channel_id=1, source_target_pairs={{0,16},{4,12},{8,24},{12,4},{16,0},{20,28},{24,8},{28,20},{1,17},{... | collective-permute-start | bytes 1966088 | tf_op jit(solution)/shard_map/ppermute | solution.py:542
  11.4 1.2 %collective-permute-start.6 = (bf16[640,512]{1,0:T(8,128)(2,1)}, bf16[640,512]{1,0:T(8,128)(2,1)}, u32[]{:S(2)}, u32[]{:S(2)}) collective-permute-start(bf16[640,512]{1,0:T(8,128)(2,1)} %collective-permute-done.5.refs_1_), channel_id=1, source_target_pairs={{0,16},{4,12},{8,24},{12,4},{16,0},{20,28},{24,8},{28,20},{1,17},{... | collective-permute-start | bytes 1966088 | tf_op jit(solution)/shard_map/ppermute | solution.py:542
  12.6 3.4 %all-to-all-done.arrived_hbm = bf16[8,64,512]{2,1,0:T(8,128)(2,1)} async-done(((bf16[8,64,512]{2,1,0:T(8,128)(2,1)}), bf16[8,64,512]{2,1,0:T(8,128)(2,1)}, u32[]{:S(2)}, u32[]{:S(2)}) %all-to-all-start) | async-done | bytes 524320 | tf_op jit(solution)/shard_map/all_to_all | solution.py:559
  16.0 2.6 %shard_map.163.own_up = bf16[400,512]{1,0:T(8,128)(2,1)} custom-call(s32[2]{0:T(128)} %lengths_ref.1, s32[1,128]{1,0:T(1,128)} %bitcast.4, bf16[8,64,512]{2,1,0:T(8,128)(2,1)} %all-to-all-done.arrived_hbm), custom_call_target="tpu_custom_call" | custom-call | tf_op jit(solution)/shard_map/pallas_call | solution.py:560
  18.6 3.6 %collective-permute-start.1 = (bf16[400,512]{1,0:T(8,128)(2,1)}, bf16[400,512]{1,0:T(8,128)(2,1)}, u32[]{:S(2)}, u32[]{:S(2)}) collective-permute-start(bf16[400,512]{1,0:T(8,128)(2,1)} %shard_map.163.own_up), channel_id=1, source_target_pairs={{0,4},{4,0},{8,12},{12,8},{16,20},{20,16},{24,28},{28,24},{1,5},{5... | collective-permute-start | bytes 1228808 | tf_op jit(solution)/shard_map/ppermute | solution.py:571
  22.2 2.5 %collective-permute-done.7.refs_2_ = bf16[640,512]{1,0:T(8,128)(2,1)} collective-permute-done((bf16[640,512]{1,0:T(8,128)(2,1)}, bf16[640,512]{1,0:T(8,128)(2,1)}, u32[]{:S(2)}, u32[]{:S(2)}) %collective-permute-start.7) | collective-permute-done | bytes 655392 | tf_op jit(solution)/shard_map/ppermute | solution.py:542
  24.7 6.1 %shard_map.166 = (f32[256,512]{1,0:T(8,128)}, bf16[256,640]{1,0:T(8,128)(2,1)}, bf16[256,640]{1,0:T(8,128)(2,1)}, bf16[256,640]{1,0:T(8,128)(2,1)}, bf16[256,640]{1,0:T(8,128)(2,1)}) custom-call(f32[2,20]{1,0:T(2,128)} %bitcast.2, s32[2,2]{1,0:T(2,128)} %rows_ref.5, bf16[400,512]{1,0:T(8,128)(2,1)} %shard_map.163.own_up, ...), custom_call_target="tpu_custom_call" | custom-call | tf_op jit(solution)/shard_map/pallas_call | solution.py:411
  30.8 0.9 %collective-permute-done.6.refs_0_ = bf16[640,512]{1,0:T(8,128)(2,1)} collective-permute-done((bf16[640,512]{1,0:T(8,128)(2,1)}, bf16[640,512]{1,0:T(8,128)(2,1)}, u32[]{:S(2)}, u32[]{:S(2)}) %collective-permute-start.6) | collective-permute-done | bytes 655392 | tf_op jit(solution)/shard_map/ppermute | solution.py:542
  31.7 3.5 %shard_map.167 = (bf16[640,512]{1,0:T(8,128)(2,1)}, bf16[256,640]{1,0:T(8,128)(2,1)}, bf16[256,640]{1,0:T(8,128)(2,1)}, bf16[256,640]{1,0:T(8,128)(2,1)}, bf16[256,640]{1,0:T(8,128)(2,1)}) custom-call(f32[2,20]{1,0:T(2,128)} %bitcast.3, s32[2,2]{1,0:T(2,128)} %rows_ref.5, ...), custom_call_target="tpu_custom_call", output_to_operand_aliasing={{1}: (5, {}), {2}: (6, {}), {3}: (7, {}), {4}: (8, {})} | custom-call | tf_op jit(solution)/shard_map/pallas_call | solution.py:411
  35.4 2.4 %collective-permute-start.11 = (bf16[256,640]{1,0:T(8,128)(2,1)}, bf16[256,640]{1,0:T(8,128)(2,1)}, u32[]{:S(2)}, u32[]{:S(2)}) collective-permute-start(bf16[256,640]{1,0:T(8,128)(2,1)} %get-tuple-element.56), channel_id=1, source_target_pairs={{0,3},{1,2},{2,1},{3,0},{4,7},{5,6},{6,5},{7,4},{8,11},{9,10},{10,... | collective-permute-start | bytes 983048 | tf_op jit(solution)/shard_map/ppermute | solution.py:579
  37.8 1.1 %collective-permute-start.9 = (bf16[256,640]{1,0:T(8,128)(2,1)}, bf16[256,640]{1,0:T(8,128)(2,1)}, u32[]{:S(2)}, u32[]{:S(2)}) collective-permute-start(bf16[256,640]{1,0:T(8,128)(2,1)} %get-tuple-element.54), channel_id=1, source_target_pairs={{0,1},{1,0},{2,3},{3,2},{4,5},{5,4},{6,7},{7,6},{8,9},{9,8},{10,11... | collective-permute-start | bytes 983048 | tf_op jit(solution)/shard_map/ppermute | solution.py:579
  38.9 2.6 %shard_map.168 = (f32[128,512]{1,0:T(8,128)}, f32[128,512]{1,0:T(8,128)}) custom-call(bf16[128,5120]{1,0:T(8,128)(2,1)} %own_x.3, bf16[128,5120]{1,0:T(8,128)(2,1)} %collective-permute-done.mate_x.refs_4_, bf16[640,512]{1,0:T(8,128)(2,1)} %get-tuple-element.48.weight_hbm, f32[256,512]{1,0:T(8,128)} %get-tuple-element.49.sum_hbm), custom_call_target="tpu_custom_call" | custom-call | tf_op jit(solution)/shard_map/pallas_call | solution.py:580
  41.4 1.3 %collective-permute-start.8 = (f32[128,512]{1,0:T(8,128)}, f32[128,512]{1,0:T(8,128)}, u32[]{:S(2)}, u32[]{:S(2)}) collective-permute-start(f32[128,512]{1,0:T(8,128)} %get-tuple-element.51), channel_id=1, source_target_pairs={{0,4},{4,0},{8,12},{12,8},{16,20},{20,16},{24,28},{28,24},{1,5},{5... | collective-permute-start | bytes 786440 | tf_op jit(solution)/shard_map/ppermute | solution.py:592
  42.8 3.0 %shard_map.164 = (bf16[4,32,256]{2,1,0:T(8,128)(2,1)}, bf16[4,32,256]{2,1,0:T(8,128)(2,1)}, bf16[4,32,256]{2,1,0:T(8,128)(2,1)}, bf16[4,32,256]{2,1,0:T(8,128)(2,1)}) custom-call(s32[2,2]{1,0:T(2,128)} %rows_ref.5, bf16[128,5120]{1,0:T(8,128)(2,1)} %own_x.3, bf16[128,5120]{1,0:T(8,128)(2,1)} %collective-permute-done.mate_x.refs_4_, ...), custom_call_target="tpu_custom_call" | custom-call | tf_op jit(solution)/shard_map/pallas_call | solution.py:594
  45.7 1.3 %collective-permute-start.2 = (bf16[4,32,256]{2,1,0:T(8,128)(2,1)}, bf16[4,32,256]{2,1,0:T(8,128)(2,1)}, u32[]{:S(2)}, u32[]{:S(2)}) collective-permute-start(bf16[4,32,256]{2,1,0:T(8,128)(2,1)} %get-tuple-element.40), channel_id=1, source_target_pairs={{0,8},{4,12},{8,0},{12,4},{16,24},{20,28},{24,16},{28,20},{1,9},{5... | collective-permute-start | bytes 196616 | tf_op jit(solution)/shard_map/ppermute | solution.py:607
  47.0 2.8 %collective-permute-done.2.refs_1_ = bf16[4,32,256]{2,1,0:T(8,128)(2,1)} collective-permute-done((bf16[4,32,256]{2,1,0:T(8,128)(2,1)}, bf16[4,32,256]{2,1,0:T(8,128)(2,1)}, u32[]{:S(2)}, u32[]{:S(2)}) %collective-permute-start.2) | collective-permute-done | bytes 65568 | tf_op jit(solution)/shard_map/ppermute | solution.py:607
  50.4 3.2 %collective-permute-done.3.refs_2_ = bf16[4,32,256]{2,1,0:T(8,128)(2,1)} collective-permute-done((bf16[4,32,256]{2,1,0:T(8,128)(2,1)}, bf16[4,32,256]{2,1,0:T(8,128)(2,1)}, u32[]{:S(2)}, u32[]{:S(2)}) %collective-permute-start.3) | collective-permute-done | bytes 65568 | tf_op jit(solution)/shard_map/ppermute | solution.py:607
  53.6 1.5 %collective-permute-start.4 = (bf16[4,32,256]{2,1,0:T(8,128)(2,1)}, bf16[4,32,256]{2,1,0:T(8,128)(2,1)}, u32[]{:S(2)}, u32[]{:S(2)}) collective-permute-start(bf16[4,32,256]{2,1,0:T(8,128)(2,1)} %get-tuple-element.42), channel_id=1, source_target_pairs={{0,24},{4,28},{8,16},{12,20},{16,8},{20,12},{24,0},{28,4},{1,25},{... | collective-permute-start | bytes 196616 | tf_op jit(solution)/shard_map/ppermute | solution.py:607
  55.1 2.8 %collective-permute-done.4.refs_3_ = bf16[4,32,256]{2,1,0:T(8,128)(2,1)} collective-permute-done((bf16[4,32,256]{2,1,0:T(8,128)(2,1)}, bf16[4,32,256]{2,1,0:T(8,128)(2,1)}, u32[]{:S(2)}, u32[]{:S(2)}) %collective-permute-start.4) | collective-permute-done | bytes 65568 | tf_op jit(solution)/shard_map/ppermute | solution.py:607
  57.9 2.3 %shard_map.165 = (f32[32,2,2,256]{3,2,1,0:T(2,128)}, f32[32,2,2,256]{3,2,1,0:T(2,128)}, f32[32,2,2,256]{3,2,1,0:T(2,128)}, bf16[16,128]{1,0:T(8,128)(2,1)}) custom-call(f32[32,2,2,256]{3,2,1,0:T(2,128)} %delta_hbm.3, f32[32,2,2,256]{3,2,1,0:T(2,128)} %m_hbm.1, f32[32,2,2,256]{3,2,1,0:T(2,128)} %v_hbm.1, bf16[4,32,256]{2,1,0:T(8,128)(2,1)} %get-tuple-element.39.refs_0_, ...), custom_call_target="tpu_custom_call" | custom-call | tf_op jit(solution)/shard_map/pallas_call | solution.py:611
  60.2 2.2 %shard_map.169.up_slots = bf16[8,64,384]{2,1,0:T(8,128)(2,1)} custom-call(bf16[400,512]{1,0:T(8,128)(2,1)} %shard_map.163.own_up, f32[128,512]{1,0:T(8,128)} %get-tuple-element.50.own_sum, f32[128,512]{1,0:T(8,128)} %collective-permute-done.8.other_sum, bf16[16,128]{1,0:T(8,128)(2,1)} %get-tuple-element.52.tops_ref), custom_call_target="tpu_custom_call" | custom-call | tf_op jit(solution)/shard_map/pallas_call | solution.py:620
  62.4 4.9 %collective-permute-done.11.refs_3_ = bf16[256,640]{1,0:T(8,128)(2,1)} collective-permute-done((bf16[256,640]{1,0:T(8,128)(2,1)}, bf16[256,640]{1,0:T(8,128)(2,1)}, u32[]{:S(2)}, u32[]{:S(2)}) %collective-permute-start.11) | collective-permute-done | bytes 327712 | tf_op jit(solution)/shard_map/ppermute | solution.py:579
  67.3 2.8 %shard_map.170 = (bf16[64,1024]{1,0:T(8,128)(2,1)}, bf16[64,1024]{1,0:T(8,128)(2,1)}, bf16[64,1024]{1,0:T(8,128)(2,1)}, bf16[64,1024]{1,0:T(8,128)(2,1)}, bf16[6...) custom-call(bf16[400,512]{1,0:T(8,128)(2,1)} %shard_map.163.own_up, ...), custom_call_target="tpu_custom_call" | custom-call | tf_op jit(solution)/shard_map/pallas_call | solution.py:627
  70.6 1.1 %collective-permute-start.13 = (bf16[64,1024]{1,0:T(8,128)(2,1)}, bf16[64,1024]{1,0:T(8,128)(2,1)}, u32[]{:S(2)}, u32[]{:S(2)}) collective-permute-start(bf16[64,1024]{1,0:T(8,128)(2,1)} %get-tuple-element.59), channel_id=1, source_target_pairs={{0,8},{4,12},{8,0},{12,4},{16,24},{20,28},{24,16},{28,20},{1,9},{5... | collective-permute-start | bytes 393224 | tf_op jit(solution)/shard_map/ppermute | solution.py:640
  72.3 0.9 %collective-permute-start.15 = (bf16[64,1024]{1,0:T(8,128)(2,1)}, bf16[64,1024]{1,0:T(8,128)(2,1)}, u32[]{:S(2)}, u32[]{:S(2)}) collective-permute-start(bf16[64,1024]{1,0:T(8,128)(2,1)} %get-tuple-element.61), channel_id=1, source_target_pairs={{0,16},{4,20},{8,24},{12,28},{16,0},{20,4},{24,8},{28,12},{1,17},{... | collective-permute-start | bytes 393224 | tf_op jit(solution)/shard_map/ppermute | solution.py:640
  74.1 1.8 %collective-permute-start.17 = (bf16[64,1024]{1,0:T(8,128)(2,1)}, bf16[64,1024]{1,0:T(8,128)(2,1)}, u32[]{:S(2)}, u32[]{:S(2)}) collective-permute-start(bf16[64,1024]{1,0:T(8,128)(2,1)} %get-tuple-element.63), channel_id=1, source_target_pairs={{0,24},{4,28},{8,16},{12,20},{16,8},{20,12},{24,0},{28,4},{1,25},{... | collective-permute-start | bytes 393224 | tf_op jit(solution)/shard_map/ppermute | solution.py:640
  76.0 3.0 %collective-permute-start.18 = (bf16[64,1024]{1,0:T(8,128)(2,1)}, bf16[64,1024]{1,0:T(8,128)(2,1)}, u32[]{:S(2)}, u32[]{:S(2)}) collective-permute-start(bf16[64,1024]{1,0:T(8,128)(2,1)} %get-tuple-element.64), channel_id=1, source_target_pairs={{0,28},{4,24},{8,20},{12,16},{16,12},{20,8},{24,4},{28,0},{1,29},{... | collective-permute-start | bytes 393224 | tf_op jit(solution)/shard_map/ppermute | solution.py:640
  79.7 6.6 %collective-permute-done.16.refs_5_ = bf16[64,1024]{1,0:T(8,128)(2,1)} collective-permute-done((bf16[64,1024]{1,0:T(8,128)(2,1)}, bf16[64,1024]{1,0:T(8,128)(2,1)}, u32[]{:S(2)}, u32[]{:S(2)}) %collective-permute-start.16) | collective-permute-done | bytes 131104 | tf_op jit(solution)/shard_map/ppermute | solution.py:640
  86.3 3.5 %shard_map.171 = (bf16[256,1280]{1,0:T(8,128)(2,1)}, bf16[256,512]{1,0:T(8,128)(2,1)}, f32[2,2]{1,0:T(2,128)}, bf16[32,2,2,256]{3,2,1,0:T(2,128)(2,1)}) custom-call(bf16[256,512]{1,0:T(8,128)(2,1)} %gate_hbm.3, bf16[256,512]{1,0:T(8,128)(2,1)} %hidden_hbm.3, f32[32,2,2,256]{3,2,1,0:T(2,128)} %get-tuple-element.34.delta_hbm, ...), custom_call_target="tpu_custom_call" | custom-call | tf_op jit(solution)/shard_map/pallas_call | solution.py:643
  (18 shorter events, 5.2 us)
Async XLA Ops:
  0.6 24.1 %collective-permute-start = (bf16[128,5120]{1,0:T(8,128)(2,1)}, bf16[128,5120]{1,0:T(8,128)(2,1)}, u32[]{:S(2)}, u32[]{:S(2)}) collective-permute-start(bf16[128,5120]{1,0:T(8,128)(2,1)} %own_x.3), channel_id=1, source_target_pairs={{0,4},{4,0},{8,12},{12,8},{16,20},{20,16},{24,28},{28,24},{1,5},{5... | collective-permute-start | bytes 3932168 | tf_op jit(solution)/shard_map/ppermute | solution.py:546
  1.4 10.0 %collective-permute-start.5 = (bf16[640,512]{1,0:T(8,128)(2,1)}, bf16[640,512]{1,0:T(8,128)(2,1)}, u32[]{:S(2)}, u32[]{:S(2)}) collective-permute-start(bf16[640,512]{1,0:T(8,128)(2,1)} %refs_0_.1), channel_id=1, source_target_pairs={{0,8},{4,20},{8,0},{12,28},{16,24},{20,4},{24,16},{28,12},{1,9},{5... | collective-permute-start | bytes 1966088 | tf_op jit(solution)/shard_map/ppermute | solution.py:542
  4.8 11.2 %all-to-all-start = ((bf16[8,64,512]{2,1,0:T(8,128)(2,1)}), bf16[8,64,512]{2,1,0:T(8,128)(2,1)}, u32[]{:S(2)}, u32[]{:S(2)}) async-start(bf16[8,64,512]{2,1,0:T(8,128)(2,1)} %shard_map.162), calls=%async_computation | async-start | bytes 1048576 | tf_op jit(solution)/shard_map/all_to_all | solution.py:559
  9.1 15.6 %collective-permute-start.7 = (bf16[640,512]{1,0:T(8,128)(2,1)}, bf16[640,512]{1,0:T(8,128)(2,1)}, u32[]{:S(2)}, u32[]{:S(2)}) collective-permute-start(bf16[640,512]{1,0:T(8,128)(2,1)} %refs_0_.1), channel_id=1, source_target_pairs={{0,16},{4,12},{8,24},{12,4},{16,0},{20,28},{24,8},{28,20},{1,17},{... | collective-permute-start | bytes 1966088 | tf_op jit(solution)/shard_map/ppermute | solution.py:542
  11.4 20.3 %collective-permute-start.6 = (bf16[640,512]{1,0:T(8,128)(2,1)}, bf16[640,512]{1,0:T(8,128)(2,1)}, u32[]{:S(2)}, u32[]{:S(2)}) collective-permute-start(bf16[640,512]{1,0:T(8,128)(2,1)} %collective-permute-done.5.refs_1_), channel_id=1, source_target_pairs={{0,16},{4,12},{8,24},{12,4},{16,0},{20,28},{24,8},{28,20},{1,17},{... | collective-permute-start | bytes 1966088 | tf_op jit(solution)/shard_map/ppermute | solution.py:542
  18.6 6.1 %collective-permute-start.1 = (bf16[400,512]{1,0:T(8,128)(2,1)}, bf16[400,512]{1,0:T(8,128)(2,1)}, u32[]{:S(2)}, u32[]{:S(2)}) collective-permute-start(bf16[400,512]{1,0:T(8,128)(2,1)} %shard_map.163.own_up), channel_id=1, source_target_pairs={{0,4},{4,0},{8,12},{12,8},{16,20},{20,16},{24,28},{28,24},{1,5},{5... | collective-permute-start | bytes 1228808 | tf_op jit(solution)/shard_map/ppermute | solution.py:571
  35.2 27.2 %collective-permute-start.10 = (bf16[256,640]{1,0:T(8,128)(2,1)}, bf16[256,640]{1,0:T(8,128)(2,1)}, u32[]{:S(2)}, u32[]{:S(2)}) collective-permute-start(bf16[256,640]{1,0:T(8,128)(2,1)} %get-tuple-element.55), channel_id=1, source_target_pairs={{0,2},{1,3},{2,0},{3,1},{4,6},{5,7},{6,4},{7,5},{8,10},{9,11},{10,... | collective-permute-start | bytes 983048 | tf_op jit(solution)/shard_map/ppermute | solution.py:579
  35.4 31.9 %collective-permute-start.11 = (bf16[256,640]{1,0:T(8,128)(2,1)}, bf16[256,640]{1,0:T(8,128)(2,1)}, u32[]{:S(2)}, u32[]{:S(2)}) collective-permute-start(bf16[256,640]{1,0:T(8,128)(2,1)} %get-tuple-element.56), channel_id=1, source_target_pairs={{0,3},{1,2},{2,1},{3,0},{4,7},{5,6},{6,5},{7,4},{8,11},{9,10},{10,... | collective-permute-start | bytes 983048 | tf_op jit(solution)/shard_map/ppermute | solution.py:579
  37.8 29.5 %collective-permute-start.9 = (bf16[256,640]{1,0:T(8,128)(2,1)}, bf16[256,640]{1,0:T(8,128)(2,1)}, u32[]{:S(2)}, u32[]{:S(2)}) collective-permute-start(bf16[256,640]{1,0:T(8,128)(2,1)} %get-tuple-element.54), channel_id=1, source_target_pairs={{0,1},{1,0},{2,3},{3,2},{4,5},{5,4},{6,7},{7,6},{8,9},{9,8},{10,11... | collective-permute-start | bytes 983048 | tf_op jit(solution)/shard_map/ppermute | solution.py:579
  41.4 18.8 %collective-permute-start.8 = (f32[128,512]{1,0:T(8,128)}, f32[128,512]{1,0:T(8,128)}, u32[]{:S(2)}, u32[]{:S(2)}) collective-permute-start(f32[128,512]{1,0:T(8,128)} %get-tuple-element.51), channel_id=1, source_target_pairs={{0,4},{4,0},{8,12},{12,8},{16,20},{20,16},{24,28},{28,24},{1,5},{5... | collective-permute-start | bytes 786440 | tf_op jit(solution)/shard_map/ppermute | solution.py:592
  45.7 4.1 %collective-permute-start.2 = (bf16[4,32,256]{2,1,0:T(8,128)(2,1)}, bf16[4,32,256]{2,1,0:T(8,128)(2,1)}, u32[]{:S(2)}, u32[]{:S(2)}) collective-permute-start(bf16[4,32,256]{2,1,0:T(8,128)(2,1)} %get-tuple-element.40), channel_id=1, source_target_pairs={{0,8},{4,12},{8,0},{12,4},{16,24},{20,28},{24,16},{28,20},{1,9},{5... | collective-permute-start | bytes 196616 | tf_op jit(solution)/shard_map/ppermute | solution.py:607
  49.8 3.7 %collective-permute-start.3 = (bf16[4,32,256]{2,1,0:T(8,128)(2,1)}, bf16[4,32,256]{2,1,0:T(8,128)(2,1)}, u32[]{:S(2)}, u32[]{:S(2)}) collective-permute-start(bf16[4,32,256]{2,1,0:T(8,128)(2,1)} %get-tuple-element.41), channel_id=1, source_target_pairs={{0,16},{4,20},{8,24},{12,28},{16,0},{20,4},{24,8},{28,12},{1,17},{... | collective-permute-start | bytes 196616 | tf_op jit(solution)/shard_map/ppermute | solution.py:607
  53.6 4.3 %collective-permute-start.4 = (bf16[4,32,256]{2,1,0:T(8,128)(2,1)}, bf16[4,32,256]{2,1,0:T(8,128)(2,1)}, u32[]{:S(2)}, u32[]{:S(2)}) collective-permute-start(bf16[4,32,256]{2,1,0:T(8,128)(2,1)} %get-tuple-element.42), channel_id=1, source_target_pairs={{0,24},{4,28},{8,16},{12,20},{16,8},{20,12},{24,0},{28,4},{1,25},{... | collective-permute-start | bytes 196616 | tf_op jit(solution)/shard_map/ppermute | solution.py:607
  70.1 4.1 %collective-permute-start.12 = (bf16[64,1024]{1,0:T(8,128)(2,1)}, bf16[64,1024]{1,0:T(8,128)(2,1)}, u32[]{:S(2)}, u32[]{:S(2)}) collective-permute-start(bf16[64,1024]{1,0:T(8,128)(2,1)} %get-tuple-element.58), channel_id=1, source_target_pairs={{0,4},{4,0},{8,12},{12,8},{16,20},{20,16},{24,28},{28,24},{1,5},{5... | collective-permute-start | bytes 393224 | tf_op jit(solution)/shard_map/ppermute | solution.py:640
  70.6 5.4 %collective-permute-start.13 = (bf16[64,1024]{1,0:T(8,128)(2,1)}, bf16[64,1024]{1,0:T(8,128)(2,1)}, u32[]{:S(2)}, u32[]{:S(2)}) collective-permute-start(bf16[64,1024]{1,0:T(8,128)(2,1)} %get-tuple-element.59), channel_id=1, source_target_pairs={{0,8},{4,12},{8,0},{12,4},{16,24},{20,28},{24,16},{28,20},{1,9},{5... | collective-permute-start | bytes 393224 | tf_op jit(solution)/shard_map/ppermute | solution.py:640
  71.7 8.0 %collective-permute-start.14 = (bf16[64,1024]{1,0:T(8,128)(2,1)}, bf16[64,1024]{1,0:T(8,128)(2,1)}, u32[]{:S(2)}, u32[]{:S(2)}) collective-permute-start(bf16[64,1024]{1,0:T(8,128)(2,1)} %get-tuple-element.60), channel_id=1, source_target_pairs={{0,12},{4,8},{8,4},{12,0},{16,28},{20,24},{24,20},{28,16},{1,13},{... | collective-permute-start | bytes 393224 | tf_op jit(solution)/shard_map/ppermute | solution.py:640
  72.3 7.4 %collective-permute-start.15 = (bf16[64,1024]{1,0:T(8,128)(2,1)}, bf16[64,1024]{1,0:T(8,128)(2,1)}, u32[]{:S(2)}, u32[]{:S(2)}) collective-permute-start(bf16[64,1024]{1,0:T(8,128)(2,1)} %get-tuple-element.61), channel_id=1, source_target_pairs={{0,16},{4,20},{8,24},{12,28},{16,0},{20,4},{24,8},{28,12},{1,17},{... | collective-permute-start | bytes 393224 | tf_op jit(solution)/shard_map/ppermute | solution.py:640
  73.2 13.1 %collective-permute-start.16 = (bf16[64,1024]{1,0:T(8,128)(2,1)}, bf16[64,1024]{1,0:T(8,128)(2,1)}, u32[]{:S(2)}, u32[]{:S(2)}) collective-permute-start(bf16[64,1024]{1,0:T(8,128)(2,1)} %get-tuple-element.62), channel_id=1, source_target_pairs={{0,20},{4,16},{8,28},{12,24},{16,4},{20,0},{24,12},{28,8},{1,21},{... | collective-permute-start | bytes 393224 | tf_op jit(solution)/shard_map/ppermute | solution.py:640
  74.1 12.2 %collective-permute-start.17 = (bf16[64,1024]{1,0:T(8,128)(2,1)}, bf16[64,1024]{1,0:T(8,128)(2,1)}, u32[]{:S(2)}, u32[]{:S(2)}) collective-permute-start(bf16[64,1024]{1,0:T(8,128)(2,1)} %get-tuple-element.63), channel_id=1, source_target_pairs={{0,24},{4,28},{8,16},{12,20},{16,8},{20,12},{24,0},{28,4},{1,25},{... | collective-permute-start | bytes 393224 | tf_op jit(solution)/shard_map/ppermute | solution.py:640
  76.0 10.3 %collective-permute-start.18 = (bf16[64,1024]{1,0:T(8,128)(2,1)}, bf16[64,1024]{1,0:T(8,128)(2,1)}, u32[]{:S(2)}, u32[]{:S(2)}) collective-permute-start(bf16[64,1024]{1,0:T(8,128)(2,1)} %get-tuple-element.64), channel_id=1, source_target_pairs={{0,28},{4,24},{8,20},{12,16},{16,12},{20,8},{24,4},{28,0},{1,29},{... | collective-permute-start | bytes 393224 | tf_op jit(solution)/shard_map/ppermute | solution.py:640

commit v2 on v1

--- a/solution.py
+++ b/solution.py
@@ -315,114 +315,127 @@
     return (0, 1 + core, 2 - core, 3)[step]
 
 
-def product_kernel(scales_ref, rows_ref, own_up, mate_up, *refs, steps, rows):
-    last = steps[-1] == 3
-    codes_hbm, refs = refs[: len(steps)], refs[len(steps) :]
-    if last:
-        refs = refs[4:]
-        weight_out, *back_refs = refs[:5]
-    else:
-        own_x, mate_x, sum_ref, *back_refs = refs[:7]
-    codes, weight, up, delta, sems, *rest = refs[5 if last else 7 :]
+def scaled(codes_ref, scales_ref, block, spot, lines, lanes):
+    return (codes_ref[spot, lines, lanes].astype(jnp.float32) * scales_ref[lanes.start // BLK, block]).astype(
+        jnp.bfloat16
+    )
+
+
+def product_kernel(
+    scales_ref, rows_ref, own_up, mate_up, own_x, mate_x, *refs
+):
+    codes_hbm, (sum_ref, *back_refs), (codes, weight, up, delta, x, sems) = refs[:3], refs[3:8], refs[8:]
+    rows = own_x.shape[0]
     core, own_chip = own_place()
     turn = own_chip ^ lax.axis_index("col")
     size, width = weight.shape[1:]
     tiles = size // LANE
-    pairs = []
-    for seat, up_hbm in enumerate((own_up, mate_up)):
-        pairs.append((up_hbm.at[:rows, :], up.at[seat * rows : (seat + 1) * rows]))
-        pairs.append((up_hbm.at[rows + META :, :], delta.at[core ^ seat]))
+    pairs = row_pairs(own_up, mate_up, up, delta, core)
     shared = len(pairs)
-    each = 1 if last else 3
     starts = []
-    for spot, step in enumerate(steps):
+    for step in range(3):
         first_tile = (2 * (own_chip ^ block_order(core, step)) + core) * tiles
         starts.append(first_tile)
-        pairs.append((codes_hbm[spot], codes.at[spot]))
-        if not last:
-            lanes = pl.ds(pl.multiple_of(first_tile * LANE, LANE), size)
-            pairs.append((own_x.at[:, lanes], rest[0].at[spot, :rows]))
-            pairs.append((mate_x.at[:, lanes], rest[0].at[spot, rows:]))
+        lanes = pl.ds(pl.multiple_of(first_tile * LANE, LANE), size)
+        pairs.append((codes_hbm[step], codes.at[step]))
+        pairs.append((own_x.at[:, lanes], x.at[step, :rows]))
+        pairs.append((mate_x.at[:, lanes], x.at[step, rows:]))
     copies = fetch(pairs, sems)
-    for spot, step in enumerate(steps):
-        for copy in copies[shared + each * spot : shared + each * (spot + 1)]:
+    for step in range(3):
+        for copy in copies[shared + 3 * step : shared + 3 * (step + 1)]:
             copy.wait()
         for tile in range(tiles):
-            block = lax.div(starts[spot] + tile, BLK // LANE)
+            block = lax.div(starts[step] + tile, BLK // LANE)
             lines = slice(tile * LANE, (tile + 1) * LANE)
             for j in range(width // BLK):
                 lanes = slice(j * BLK, (j + 1) * BLK)
-                plain = codes[spot, lines, lanes].astype(jnp.float32) * scales_ref[j, block]
-                weight[spot, lines, lanes] = plain.astype(jnp.bfloat16)
-        if spot == 0:
+                weight[step, lines, lanes] = scaled(codes, scales_ref, block, step, lines, lanes)
+        if step == 0:
             for copy in copies[:shared]:
                 copy.wait()
         for j in range(width // BLK):
             lanes = slice(j * BLK, (j + 1) * BLK)
             for k in range(K):
                 for piece in range(BLK // LANE):
-                    tile = rows_ref[j, k] * (BLK // LANE) + piece - starts[spot]
+                    tile = rows_ref[j, k] * (BLK // LANE) + piece - starts[step]
 
                     @pl.when((tile >= 0) & (tile < tiles))
                     def _():
                         lines = pl.ds(pl.multiple_of(tile * LANE, LANE), LANE)
                         extra = delta[k, piece * LANE : (piece + 1) * LANE, lanes].astype(jnp.float32)
-                        held = weight[spot, lines, lanes].astype(jnp.float32)
-                        weight[spot, lines, lanes] = (held + extra).astype(jnp.bfloat16)
+                        held = weight[step, lines, lanes].astype(jnp.float32)
+                        weight[step, lines, lanes] = (held + extra).astype(jnp.bfloat16)
 
         back = lax.dot_general(
-            up[...], weight[spot], (((1,), (1,)), ((), ())), preferred_element_type=jnp.float32
+            up[...], weight[step], (((1,), (1,)), ((), ())), preferred_element_type=jnp.float32
         ).astype(jnp.bfloat16)
-        if last:
-            rest[0][...] = back
-            weight_copy = pltpu.make_async_copy(weight.at[spot], weight_out, rest[1].at[1])
-            weight_copy.start()
         for shift, back_ref in enumerate(back_refs):
 
             @pl.when((turn ^ block_order(core, step)) == shift)
             def _():
-                if last:
-                    back_copy = pltpu.make_async_copy(rest[0], back_ref, rest[1].at[0])
-                    back_copy.start()
-                    back_copy.wait()
-                else:
-                    back_ref[...] = back
-
-        if last:
-            weight_copy.wait()
-        elif spot == 0:
-            sum_ref[...] = jnp.dot(rest[0][spot], weight[spot], preferred_element_type=jnp.float32)
+                back_ref[...] = back
+
+        part_sum = jnp.dot(x[step], weight[step], preferred_element_type=jnp.float32)
+        if step == 0:
+            sum_ref[...] = part_sum
         else:
-            sum_ref[...] += jnp.dot(rest[0][spot], weight[spot], preferred_element_type=jnp.float32)
-
-
-def products(steps, scales, block_rows, own_up, mate_up, codes, *more):
-    size, width = codes[0].shape
-    rows = own_up.shape[0] - META - BLK
-    count = len(steps)
-    last = steps[-1] == 3
-    back = jax.ShapeDtypeStruct((2 * rows, size), jnp.bfloat16)
-    if last:
-        first = jax.ShapeDtypeStruct((size, width), jnp.bfloat16)
-        rest = [pltpu.VMEM(back.shape, jnp.bfloat16), pltpu.SemaphoreType.DMA((2,))]
-    else:
-        first = jax.ShapeDtypeStruct((2 * rows, width), jnp.float32)
-        rest = [pltpu.VMEM((count, 2 * rows, size), jnp.bfloat16)]
-    return call(
-        functools.partial(product_kernel, steps=steps, rows=rows),
-        [first] + [back] * 4,
-        in_specs=[SMEM] * 2 + [HBM] * (2 + count + len(more)),
-        out_specs=[HBM if last else VMEM] * 5,
-        scratch_shapes=[
-            pltpu.VMEM((count, size, width), jnp.bfloat16),
-            pltpu.VMEM((count, size, width), jnp.bfloat16),
-            pltpu.VMEM((2 * rows, width), jnp.bfloat16),
-            pltpu.VMEM((K, BLK, width), jnp.bfloat16),
-            pltpu.SemaphoreType.DMA((4 + 3 * count,)),
-        ]
-        + rest,
-        input_output_aliases={4 + count + n: 1 + n for n in range(4)} if last else {},
-    )(scales, block_rows, own_up, mate_up, *codes, *more)
+            sum_ref[...] += part_sum
+
+
+def row_pairs(own_up, mate_up, up, delta, core):
+    rows = up.shape[0] // 2
+    pairs = []
+    for seat, up_hbm in enumerate((own_up, mate_up)):
+        pairs.append((up_hbm.at[:rows, :], up.at[seat * rows : (seat + 1) * rows]))
+        pairs.append((up_hbm.at[rows + META :, :], delta.at[core ^ seat]))
+    return pairs
+
+
+def far_kernel(scales_ref, rows_ref, own_up, mate_up, codes_hbm, *refs):
+    weight_out, *back_refs = refs[4:9]
+    codes, weight, up, delta, back, sems, out_sems = refs[9:]
+    core, own_chip = own_place()
+    turn = own_chip ^ lax.axis_index("col")
+    size, width = weight.shape
+    tiles = size // LANE
+    first_tile = (2 * (own_chip ^ 3) + core) * tiles
+    copies = fetch([(codes_hbm, codes.at[0])] + row_pairs(own_up, mate_up, up, delta, core), sems)
+    copies[0].wait()
+    for tile in range(tiles):
+        block = lax.div(first_tile + tile, BLK // LANE)
+        lines = slice(tile * LANE, (tile + 1) * LANE)
+        for j in range(width // BLK):
+            lanes = slice(j * BLK, (j + 1) * BLK)
+            weight[lines, lanes] = scaled(codes, scales_ref, block, 0, lines, lanes)
+    for copy in copies[1:]:
+        copy.wait()
+    for j in range(width // BLK):
+        lanes = slice(j * BLK, (j + 1) * BLK)
+        for k in range(K):
+            for piece in range(BLK // LANE):
+                tile = rows_ref[j, k] * (BLK // LANE) + piece - first_tile
+
+                @pl.when((tile >= 0) & (tile < tiles))
+                def _():
+                    lines = pl.ds(pl.multiple_of(tile * LANE, LANE), LANE)
+                    extra = delta[k, piece * LANE : (piece + 1) * LANE, lanes].astype(jnp.float32)
+                    held = weight[lines, lanes].astype(jnp.float32)
+                    weight[lines, lanes] = (held + extra).astype(jnp.bfloat16)
+
+    weight_copy = pltpu.make_async_copy(weight, weight_out, out_sems.at[1])
+    weight_copy.start()
+    back[...] = lax.dot_general(
+        up[...], weight[...], (((1,), (1,)), ((), ())), preferred_element_type=jnp.float32
+    ).astype(jnp.bfloat16)
+    for shift, back_ref in enumerate(back_refs):
+
+        @pl.when((turn ^ 3) == shift)
+        def _():
+            back_copy = pltpu.make_async_copy(back, back_ref, out_sems.at[0])
+            back_copy.start()
+            back_copy.wait()
+
+    weight_copy.wait()
 
 
 def forward_kernel(own_x, mate_x, weight_hbm, sum_hbm, own_out, mate_out, x, weight, total, sems):
@@ -455,8 +468,8 @@
 
 
 def spread_kernel(own_up, mate_up, up_slots, *refs):
-    parts_hbm, out_refs = refs[:4], refs[4:-4]
-    held_ref, meta_ref, parts_ref, sems = refs[-4:]
+    parts_hbm, out_refs = refs[:4], refs[4:-5]
+    held_ref, meta_ref, parts_ref, sems, out_sems = refs[-5:]
     _, rows, size = parts_ref.shape
     rows = rows // 2
     peers = held_ref.shape[0]
@@ -465,9 +478,9 @@
     token = lax.axis_index("tok")
     pairs = [(up.at[rows : rows + META, :rows], meta_ref.at[seat]) for seat, up in enumerate((own_up, mate_up))]
     pairs += [(part, parts_ref.at[n]) for n, part in enumerate(parts_hbm)]
-    pairs += [(up_slots.at[token ^ d], far.at[:, size:]) for d, far in enumerate(out_refs)]
+    pairs.append((up_slots, held_ref.at[:, :, size:]))
     copies = fetch(pairs, sems)
-    for copy in copies[: 2 + len(parts_hbm)]:
+    for copy in copies[:-1]:
         copy.wait()
     for seat in range(2):
         lines = slice(seat * rows, (seat + 1) * rows)
@@ -478,41 +491,50 @@
         place = place_matrix(target[0:1].astype(jnp.int32), peers * cap)
         placed = jnp.dot(place, summed.astype(jnp.bfloat16), preferred_element_type=jnp.float32)
         start = pl.multiple_of((core ^ seat) * cap, cap)
-        held_ref[:, pl.ds(start, cap), :] = placed.astype(jnp.bfloat16).reshape(peers, cap, size)
-    for d, far_ref in enumerate(out_refs):
-        far_ref[:, :size] = held_ref[token ^ d]
-    for copy in copies[2 + len(parts_hbm) :]:
+        held_ref[:, pl.ds(start, cap), :size] = placed.astype(jnp.bfloat16).reshape(peers, cap, size)
+    copies[-1].wait()
+    out_copies = fetch([(held_ref.at[token ^ d], far_ref) for d, far_ref in enumerate(out_refs)], out_sems)
+    for copy in out_copies:
         copy.wait()
 
 
-def finish_kernel(gate_hbm, hidden_hbm, delta_hbm, *refs):
-    arrived_refs = refs[:-8]
-    input_out, gate_out, scale_out, codes_out, gate_ref, hidden_ref, delta_ref, sems = refs[-8:]
-    copies = fetch([(gate_hbm, gate_ref), (hidden_hbm, hidden_ref), (delta_hbm, delta_ref)], sems)
+def finish_kernel(gate_hbm, hidden_hbm, delta_hbm, *refs, order):
+    arrived_hbm = refs[:-10]
+    input_out, gate_out, scale_out, codes_out, gate_ref, hidden_ref, delta_ref, held_ref, sems, out_sems = refs[-10:]
     size = input_out.shape[1] // 2
-    cap = gate_ref.shape[0] // len(arrived_refs)
+    peers = len(arrived_hbm)
+    cap = gate_ref.shape[0] // peers
     half = gate_ref.shape[1] // 2
     token = lax.axis_index("tok")
-    for distance, arrived_ref in enumerate(arrived_refs):
+    pairs = [(gate_hbm, gate_ref), (hidden_hbm, hidden_ref), (delta_hbm, delta_ref)]
+    pairs += [(ref, held_ref.at[number]) for number, ref in enumerate(arrived_hbm)]
+    copies = fetch(pairs, sems)
+    out_copies = []
+    for number, distance in enumerate(order):
         sender = token ^ distance
         lines = pl.ds(pl.multiple_of((sender >> 1) * 2 * cap, 2 * cap), 2 * cap)
         lanes = pl.ds(pl.multiple_of((sender & 1) * size, LANE), size)
-        input_out[lines, lanes] = arrived_ref[:, :size]
-    for copy in copies:
+        copies[3 + number].wait()
+        out_copies.append(
+            pltpu.make_async_copy(
+                held_ref.at[number, :, :size], input_out.at[lines, lanes], out_sems.at[number]
+            )
+        )
+        out_copies[-1].start()
+    for copy in copies[:3]:
         copy.wait()
     tops = jnp.zeros((1, LANE), jnp.float32)
-    for distance, arrived_ref in enumerate(arrived_refs):
-        sender = token ^ distance
-        lines = pl.ds(pl.multiple_of(sender * cap, cap), cap)
+    for number, distance in enumerate(order):
+        lines = pl.ds(pl.multiple_of((token ^ distance) * cap, cap), cap)
         for side in range(2):
             lanes = slice(side * half, (side + 1) * half)
             gate = gate_ref[lines, lanes].astype(jnp.float32)
             sigmoid_value = 1.0 / (1.0 + jnp.exp(-gate))
             slope = sigmoid_value * (1.0 + gate * (1.0 - sigmoid_value))
-            value = arrived_ref[side * cap : (side + 1) * cap, size : size + half].astype(jnp.float32)
+            value = held_ref[number, side * cap : (side + 1) * cap, size : size + half].astype(jnp.float32)
             hidden = hidden_ref[lines, lanes].astype(jnp.float32)
             gate_out[lines, lanes] = (hidden * value * slope).astype(jnp.bfloat16)
-        kinds = arrived_ref[:META, size + half :].astype(jnp.float32)
+        kinds = held_ref[number, :META, size + half :].astype(jnp.float32)
         tops = jnp.maximum(tops, kinds[0:1] + kinds[1:2] + kinds[2:3])
     lanes = lax.broadcasted_iota(jnp.int32, (1, LANE), 1)
     first = lax.broadcasted_iota(jnp.int32, scale_out.shape, 0)
@@ -524,6 +546,8 @@
             scales = jnp.where((first == j) & (second == k), top, scales)
             codes_out[:, j, k, :] = (delta_ref[:, j, k, :] / (top + scale_eps)).astype(jnp.bfloat16)
     scale_out[...] = scales
+    for copy in out_copies:
+        copy.wait()
 
 
 def paired(
@@ -571,9 +595,37 @@
     mate_up = lax.ppermute(own_up, "tok", mates)
 
     codes_far = hop(codes_near, 1)
-    shared = (scales, block_rows, own_up, mate_up)
-    early_sum, *backs = products((0, 1, 2), *shared, [up_codes, codes_near, codes_side], rollout, mate_x)
-    weight_far, *backs = products((3,), *shared, [codes_far], *backs)
+    back = jax.ShapeDtypeStruct((2 * send_rows, own_rows), jnp.bfloat16)
+    row_scratch = [
+        pltpu.VMEM((2 * send_rows, width), jnp.bfloat16),
+        pltpu.VMEM((K, BLK, width), jnp.bfloat16),
+    ]
+    early_sum, *backs = call(
+        product_kernel,
+        [jax.ShapeDtypeStruct((2 * send_rows, width), jnp.float32)] + [back] * chips,
+        in_specs=[SMEM] * 2 + [HBM] * 7,
+        out_specs=[VMEM] * (1 + chips),
+        scratch_shapes=[pltpu.VMEM((3, own_rows, width), jnp.bfloat16)] * 2
+        + row_scratch
+        + [pltpu.VMEM((3, 2 * send_rows, own_rows), jnp.bfloat16), pltpu.SemaphoreType.DMA((13,))],
+    )(scales, block_rows, own_up, mate_up, rollout, mate_x, up_codes, codes_near, codes_side)
+    weight_far, *backs = call(
+        far_kernel,
+        [jax.ShapeDtypeStruct((own_rows, width), jnp.bfloat16)] + [back] * chips,
+        in_specs=[SMEM] * 2 + [HBM] * (3 + chips),
+        out_specs=[HBM] * (1 + chips),
+        scratch_shapes=[
+            pltpu.VMEM((1, own_rows, width), jnp.bfloat16),
+            pltpu.VMEM((own_rows, width), jnp.bfloat16),
+        ]
+        + row_scratch
+        + [
+            pltpu.VMEM(back.shape, jnp.bfloat16),
+            pltpu.SemaphoreType.DMA((5,)),
+            pltpu.SemaphoreType.DMA((2,)),
+        ],
+        input_output_aliases={5 + n: 1 + n for n in range(chips)},
+    )(scales, block_rows, own_up, mate_up, codes_far, *backs)
     parts = [backs[0]]
     for shift in range(1, chips):
         parts.append(lax.ppermute(backs[shift], "col", [(z, z ^ shift) for z in range(chips)]))
@@ -628,35 +680,41 @@
         spread_kernel,
         [jax.ShapeDtypeStruct((2 * cap, spread_width), jnp.bfloat16)] * peer_count,
         in_specs=[HBM] * (3 + len(parts)),
-        out_specs=[VMEM] * peer_count,
+        out_specs=[HBM] * peer_count,
         scratch_shapes=[
-            pltpu.VMEM((peer_count, 2 * cap, own_rows), jnp.bfloat16),
+            pltpu.VMEM((peer_count, 2 * cap, spread_width), jnp.bfloat16),
             pltpu.VMEM((2, META, send_rows), jnp.bfloat16),
             pltpu.VMEM((len(parts), 2 * send_rows, own_rows), jnp.bfloat16),
-            pltpu.SemaphoreType.DMA((2 + len(parts) + peer_count,)),
+            pltpu.SemaphoreType.DMA((3 + len(parts),)),
+            pltpu.SemaphoreType.DMA((peer_count,)),
         ],
     )(own_up, mate_up, up_slots, *parts)
-    sent = [slots[0]] + [
-        lax.ppermute(slots[distance], "tok", [(t, t ^ distance) for t in range(peer_count)])
-        for distance in range(1, peer_count)
-    ]
+    sent = {}
+    for distance in sorted(range(1, peer_count), key=lambda d: (-bin(d >> 1).count("1"), d)):
+        sent[distance] = lax.ppermute(
+            slots[distance], "tok", [(t, t ^ distance) for t in range(peer_count)]
+        )
+    sent[0] = slots[0]
+    order = list(sent)
     input_grad, gate_grad, delta_scale, delta_codes = call(
-        finish_kernel,
+        functools.partial(finish_kernel, order=order),
         (
             jax.ShapeDtypeStruct((peer_count * cap, 2 * own_rows), jnp.bfloat16),
             jax.ShapeDtypeStruct(gate_pre.shape, jnp.bfloat16),
             jax.ShapeDtypeStruct(block_rows.shape, jnp.float32),
             jax.ShapeDtypeStruct(delta.shape, jnp.bfloat16),
         ),
-        in_specs=[HBM] * 3 + [VMEM] * peer_count,
-        out_specs=(VMEM,) * 4,
+        in_specs=[HBM] * (3 + peer_count),
+        out_specs=(HBM,) + (VMEM,) * 3,
         scratch_shapes=[
             pltpu.VMEM(gate_pre.shape, jnp.bfloat16),
             pltpu.VMEM(hidden_grad.shape, jnp.bfloat16),
             pltpu.VMEM(delta.shape, jnp.float32),
-            pltpu.SemaphoreType.DMA((3,)),
+            pltpu.VMEM((peer_count, 2 * cap, spread_width), jnp.bfloat16),
+            pltpu.SemaphoreType.DMA((3 + peer_count,)),
+            pltpu.SemaphoreType.DMA((peer_count,)),
         ],
-    )(gate_pre, hidden_grad, new_delta, *sent)
+    )(gate_pre, hidden_grad, new_delta, *[sent[distance] for distance in order])
     return (input_grad, gate_grad, new_delta, new_m, new_v, delta_scale, delta_codes)
 
 

time: 90.3 us -> 88.3 us (0.978)
  transfers between devices with their start and end apart: 20 -> 20, of which waited for: 11 -> 13; matrix products, arithmetic and copies ran while one was open for 0% -> 0% of each run, Pallas kernels for 23% -> 24%
where the time goes in v2:
time: 88.3 us; the launch traced here: 87.8 us
  Pallas kernels  29.9 us (34%)
  starting transfers between devices  29.2 us (33%)
  waiting for transfers between devices  28 us (32%)
    ppermute x3, waiting for transfers between devices, paired(): lax.ppermute(gradient_parts[step], 'tok', [(t, t ^ 2 * step) for t in ran...  8.79 us
    ppermute x7, starting transfers between devices, paired(): lax.ppermute(slots[distance], 'tok', [(t, t ^ distance) for t in range(pe...  8.54 us
    ppermute x7, waiting for transfers between devices, paired(): lax.ppermute(slots[distance], 'tok', [(t, t ^ distance) for t in range(pe...  6.58 us
    pallas_call x1, Pallas kernels, paired(): call(product_kernel, [jax.ShapeDtypeStruct((2 * send_rows, width), jnp.fl...  6.12 us
    ppermute x3, waiting for transfers between devices, paired(): lax.ppermute(backs[shift], 'col', [(z, z ^ shift) for z in range(chips)])  4.96 us
    all_to_all x1, starting transfers between devices, paired(): lax.all_to_all(first_out, 'tok', split_axis=0, concat_axis=0, tiled=True)  4.35 us
    ppermute x3, waiting for transfers between devices, hop(): lax.ppermute(codes, 'tok', [(t, t ^ (4 if t & 1 ^ turned else 2)) for t i...  4.31 us
    ppermute x3, starting transfers between devices, hop(): lax.ppermute(codes, 'tok', [(t, t ^ (4 if t & 1 ^ turned else 2)) for t i...  3.84 us
  transfers between devices with their start and end apart: 20, of which 13 were waited for; matrix products, arithmetic and copies ran while one was open for 0% of the time, Pallas kernels for 24%

profile of v2, /device:TPU:17, one launch (start us, length us, event | category | flops | bytes accessed | tf_op | source)
XLA Modules:
  0.0 87.8 jit_solution(9932390243165882263)
XLA Ops:
  1.4 1.2 %collective-permute-start.5 = (bf16[640,512]{1,0:T(8,128)(2,1)}, bf16[640,512]{1,0:T(8,128)(2,1)}, u32[]{:S(2)}, u32[]{:S(2)}) collective-permute-start(bf16[640,512]{1,0:T(8,128)(2,1)} %refs_0_.1), channel_id=1, source_target_pairs={{0,8},{4,20},{8,0},{12,28},{16,24},{20,4},{24,16},{28,12},{1,9},{5... | collective-permute-start | bytes 1966088 | tf_op jit(solution)/shard_map/ppermute | solution.py:566
  2.6 2.2 %shard_map.162 = bf16[8,64,512]{2,1,0:T(8,128)(2,1)} custom-call(bf16[256,512]{1,0:T(8,128)(2,1)} %gate_hbm.3, bf16[256,512]{1,0:T(8,128)(2,1)} %hidden_hbm.3, f32[32,2,2,256]{3,2,1,0:T(2,128)} %delta_hbm.3), custom_call_target="tpu_custom_call" | custom-call | tf_op jit(solution)/shard_map/pallas_call | solution.py:571
  4.8 4.4 %all-to-all-start = ((bf16[8,64,512]{2,1,0:T(8,128)(2,1)}), bf16[8,64,512]{2,1,0:T(8,128)(2,1)}, u32[]{:S(2)}, u32[]{:S(2)}) async-start(bf16[8,64,512]{2,1,0:T(8,128)(2,1)} %shard_map.162), calls=%async_computation | async-start | bytes 1048576 | tf_op jit(solution)/shard_map/all_to_all | solution.py:583
  9.1 1.4 %collective-permute-start.7 = (bf16[640,512]{1,0:T(8,128)(2,1)}, bf16[640,512]{1,0:T(8,128)(2,1)}, u32[]{:S(2)}, u32[]{:S(2)}) collective-permute-start(bf16[640,512]{1,0:T(8,128)(2,1)} %refs_0_.1), channel_id=1, source_target_pairs={{0,16},{4,12},{8,24},{12,4},{16,0},{20,28},{24,8},{28,20},{1,17},{... | collective-permute-start | bytes 1966088 | tf_op jit(solution)/shard_map/ppermute | solution.py:566
  11.4 1.2 %collective-permute-start.6 = (bf16[640,512]{1,0:T(8,128)(2,1)}, bf16[640,512]{1,0:T(8,128)(2,1)}, u32[]{:S(2)}, u32[]{:S(2)}) collective-permute-start(bf16[640,512]{1,0:T(8,128)(2,1)} %collective-permute-done.5.refs_1_), channel_id=1, source_target_pairs={{0,16},{4,12},{8,24},{12,4},{16,0},{20,28},{24,8},{28,20},{1,17},{... | collective-permute-start | bytes 1966088 | tf_op jit(solution)/shard_map/ppermute | solution.py:566
  12.6 3.4 %all-to-all-done.arrived_hbm = bf16[8,64,512]{2,1,0:T(8,128)(2,1)} async-done(((bf16[8,64,512]{2,1,0:T(8,128)(2,1)}), bf16[8,64,512]{2,1,0:T(8,128)(2,1)}, u32[]{:S(2)}, u32[]{:S(2)}) %all-to-all-start) | async-done | bytes 524320 | tf_op jit(solution)/shard_map/all_to_all | solution.py:583
  16.0 2.6 %shard_map.163.own_up = bf16[400,512]{1,0:T(8,128)(2,1)} custom-call(s32[2]{0:T(128)} %lengths_ref.1, s32[1,128]{1,0:T(1,128)} %bitcast.4, bf16[8,64,512]{2,1,0:T(8,128)(2,1)} %all-to-all-done.arrived_hbm), custom_call_target="tpu_custom_call" | custom-call | tf_op jit(solution)/shard_map/pallas_call | solution.py:584
  18.6 3.6 %collective-permute-start.1 = (bf16[400,512]{1,0:T(8,128)(2,1)}, bf16[400,512]{1,0:T(8,128)(2,1)}, u32[]{:S(2)}, u32[]{:S(2)}) collective-permute-start(bf16[400,512]{1,0:T(8,128)(2,1)} %shard_map.163.own_up), channel_id=1, source_target_pairs={{0,4},{4,0},{8,12},{12,8},{16,20},{20,16},{24,28},{28,24},{1,5},{5... | collective-permute-start | bytes 1228808 | tf_op jit(solution)/shard_map/ppermute | solution.py:595
  22.2 2.5 %collective-permute-done.7.refs_2_ = bf16[640,512]{1,0:T(8,128)(2,1)} collective-permute-done((bf16[640,512]{1,0:T(8,128)(2,1)}, bf16[640,512]{1,0:T(8,128)(2,1)}, u32[]{:S(2)}, u32[]{:S(2)}) %collective-permute-start.7) | collective-permute-done | bytes 655392 | tf_op jit(solution)/shard_map/ppermute | solution.py:566
  24.7 6.1 %shard_map.166 = (f32[256,512]{1,0:T(8,128)}, bf16[256,640]{1,0:T(8,128)(2,1)}, bf16[256,640]{1,0:T(8,128)(2,1)}, bf16[256,640]{1,0:T(8,128)(2,1)}, bf16[256,640]{1,0:T(8,128)(2,1)}) custom-call(f32[2,20]{1,0:T(2,128)} %bitcast.2, s32[2,2]{1,0:T(2,128)} %rows_ref.5, bf16[400,512]{1,0:T(8,128)(2,1)} %shard_map.163.own_up, ...), custom_call_target="tpu_custom_call" | custom-call | tf_op jit(solution)/shard_map/pallas_call | solution.py:603
  31.7 3.3 %shard_map.167 = (bf16[640,512]{1,0:T(8,128)(2,1)}, bf16[256,640]{1,0:T(8,128)(2,1)}, bf16[256,640]{1,0:T(8,128)(2,1)}, bf16[256,640]{1,0:T(8,128)(2,1)}, bf16[256,640]{1,0:T(8,128)(2,1)}) custom-call(f32[2,20]{1,0:T(2,128)} %bitcast.3, s32[2,2]{1,0:T(2,128)} %rows_ref.5, ...), custom_call_target="tpu_custom_call", output_to_operand_aliasing={{1}: (5, {}), {2}: (6, {}), {3}: (7, {}), {4}: (8, {})} | custom-call | tf_op jit(solution)/shard_map/pallas_call | solution.py:612
  35.1 2.3 %collective-permute-start.11 = (bf16[256,640]{1,0:T(8,128)(2,1)}, bf16[256,640]{1,0:T(8,128)(2,1)}, u32[]{:S(2)}, u32[]{:S(2)}) collective-permute-start(bf16[256,640]{1,0:T(8,128)(2,1)} %get-tuple-element.56), channel_id=1, source_target_pairs={{0,3},{1,2},{2,1},{3,0},{4,7},{5,6},{6,5},{7,4},{8,11},{9,10},{10,... | collective-permute-start | bytes 983048 | tf_op jit(solution)/shard_map/ppermute | solution.py:631
  37.5 1.2 %collective-permute-start.9 = (bf16[256,640]{1,0:T(8,128)(2,1)}, bf16[256,640]{1,0:T(8,128)(2,1)}, u32[]{:S(2)}, u32[]{:S(2)}) collective-permute-start(bf16[256,640]{1,0:T(8,128)(2,1)} %get-tuple-element.54), channel_id=1, source_target_pairs={{0,1},{1,0},{2,3},{3,2},{4,5},{5,4},{6,7},{7,6},{8,9},{9,8},{10,11... | collective-permute-start | bytes 983048 | tf_op jit(solution)/shard_map/ppermute | solution.py:631
  38.6 2.6 %shard_map.168 = (f32[128,512]{1,0:T(8,128)}, f32[128,512]{1,0:T(8,128)}) custom-call(bf16[128,5120]{1,0:T(8,128)(2,1)} %own_x.5, bf16[128,5120]{1,0:T(8,128)(2,1)} %collective-permute-done.mate_x, bf16[640,512]{1,0:T(8,128)(2,1)} %get-tuple-element.48.weight_hbm, f32[256,512]{1,0:T(8,128)} %get-tuple-element.49.sum_hbm), custom_call_target="tpu_custom_call" | custom-call | tf_op jit(solution)/shard_map/pallas_call | solution.py:632
  41.2 1.2 %collective-permute-start.8 = (f32[128,512]{1,0:T(8,128)}, f32[128,512]{1,0:T(8,128)}, u32[]{:S(2)}, u32[]{:S(2)}) collective-permute-start(f32[128,512]{1,0:T(8,128)} %get-tuple-element.51), channel_id=1, source_target_pairs={{0,4},{4,0},{8,12},{12,8},{16,20},{20,16},{24,28},{28,24},{1,5},{5... | collective-permute-start | bytes 786440 | tf_op jit(solution)/shard_map/ppermute | solution.py:644
  42.5 3.0 %shard_map.164 = (bf16[4,32,256]{2,1,0:T(8,128)(2,1)}, bf16[4,32,256]{2,1,0:T(8,128)(2,1)}, bf16[4,32,256]{2,1,0:T(8,128)(2,1)}, bf16[4,32,256]{2,1,0:T(8,128)(2,1)}) custom-call(s32[2,2]{1,0:T(2,128)} %rows_ref.5, bf16[128,5120]{1,0:T(8,128)(2,1)} %own_x.5, bf16[128,5120]{1,0:T(8,128)(2,1)} %collective-permute-done.mate_x, ...), custom_call_target="tpu_custom_call" | custom-call | tf_op jit(solution)/shard_map/pallas_call | solution.py:646
  45.4 1.2 %collective-permute-start.2 = (bf16[4,32,256]{2,1,0:T(8,128)(2,1)}, bf16[4,32,256]{2,1,0:T(8,128)(2,1)}, u32[]{:S(2)}, u32[]{:S(2)}) collective-permute-start(bf16[4,32,256]{2,1,0:T(8,128)(2,1)} %get-tuple-element.40), channel_id=1, source_target_pairs={{0,8},{4,12},{8,0},{12,4},{16,24},{20,28},{24,16},{28,20},{1,9},{5... | collective-permute-start | bytes 196616 | tf_op jit(solution)/shard_map/ppermute | solution.py:659
  46.7 2.8 %collective-permute-done.2.refs_1_ = bf16[4,32,256]{2,1,0:T(8,128)(2,1)} collective-permute-done((bf16[4,32,256]{2,1,0:T(8,128)(2,1)}, bf16[4,32,256]{2,1,0:T(8,128)(2,1)}, u32[]{:S(2)}, u32[]{:S(2)}) %collective-permute-start.2) | collective-permute-done | bytes 65568 | tf_op jit(solution)/shard_map/ppermute | solution.py:659
  50.1 3.1 %collective-permute-done.3.refs_2_ = bf16[4,32,256]{2,1,0:T(8,128)(2,1)} collective-permute-done((bf16[4,32,256]{2,1,0:T(8,128)(2,1)}, bf16[4,32,256]{2,1,0:T(8,128)(2,1)}, u32[]{:S(2)}, u32[]{:S(2)}) %collective-permute-start.3) | collective-permute-done | bytes 65568 | tf_op jit(solution)/shard_map/ppermute | solution.py:659
  53.3 1.5 %collective-permute-start.4 = (bf16[4,32,256]{2,1,0:T(8,128)(2,1)}, bf16[4,32,256]{2,1,0:T(8,128)(2,1)}, u32[]{:S(2)}, u32[]{:S(2)}) collective-permute-start(bf16[4,32,256]{2,1,0:T(8,128)(2,1)} %get-tuple-element.42), channel_id=1, source_target_pairs={{0,24},{4,28},{8,16},{12,20},{16,8},{20,12},{24,0},{28,4},{1,25},{... | collective-permute-start | bytes 196616 | tf_op jit(solution)/shard_map/ppermute | solution.py:659
  54.8 2.8 %collective-permute-done.4.refs_3_ = bf16[4,32,256]{2,1,0:T(8,128)(2,1)} collective-permute-done((bf16[4,32,256]{2,1,0:T(8,128)(2,1)}, bf16[4,32,256]{2,1,0:T(8,128)(2,1)}, u32[]{:S(2)}, u32[]{:S(2)}) %collective-permute-start.4) | collective-permute-done | bytes 65568 | tf_op jit(solution)/shard_map/ppermute | solution.py:659
  57.6 2.3 %shard_map.165 = (f32[32,2,2,256]{3,2,1,0:T(2,128)}, f32[32,2,2,256]{3,2,1,0:T(2,128)}, f32[32,2,2,256]{3,2,1,0:T(2,128)}, bf16[16,128]{1,0:T(8,128)(2,1)}) custom-call(f32[32,2,2,256]{3,2,1,0:T(2,128)} %delta_hbm.3, f32[32,2,2,256]{3,2,1,0:T(2,128)} %m_hbm.1, f32[32,2,2,256]{3,2,1,0:T(2,128)} %v_hbm.1, bf16[4,32,256]{2,1,0:T(8,128)(2,1)} %get-tuple-element.39.refs_0_, ...), custom_call_target="tpu_custom_call" | custom-call | tf_op jit(solution)/shard_map/pallas_call | solution.py:663
  59.9 2.2 %shard_map.169.up_slots = bf16[8,64,384]{2,1,0:T(8,128)(2,1)} custom-call(bf16[400,512]{1,0:T(8,128)(2,1)} %shard_map.163.own_up, f32[128,512]{1,0:T(8,128)} %get-tuple-element.50.own_sum, f32[128,512]{1,0:T(8,128)} %collective-permute-done.8.other_sum, bf16[16,128]{1,0:T(8,128)(2,1)} %get-tuple-element.52.tops_ref), custom_call_target="tpu_custom_call" | custom-call | tf_op jit(solution)/shard_map/pallas_call | solution.py:672
  62.1 5.0 %collective-permute-done.11.refs_3_ = bf16[256,640]{1,0:T(8,128)(2,1)} collective-permute-done((bf16[256,640]{1,0:T(8,128)(2,1)}, bf16[256,640]{1,0:T(8,128)(2,1)}, u32[]{:S(2)}, u32[]{:S(2)}) %collective-permute-start.11) | collective-permute-done | bytes 327712 | tf_op jit(solution)/shard_map/ppermute | solution.py:631
  67.1 2.7 %shard_map.170 = (bf16[64,1024]{1,0:T(8,128)(2,1)}, bf16[64,1024]{1,0:T(8,128)(2,1)}, bf16[64,1024]{1,0:T(8,128)(2,1)}, bf16[64,1024]{1,0:T(8,128)(2,1)}, bf16[6...) custom-call(bf16[400,512]{1,0:T(8,128)(2,1)} %shard_map.163.own_up, ...), custom_call_target="tpu_custom_call" | custom-call | tf_op jit(solution)/shard_map/pallas_call | solution.py:679
  69.8 1.8 %collective-permute-start.12 = (bf16[64,1024]{1,0:T(8,128)(2,1)}, bf16[64,1024]{1,0:T(8,128)(2,1)}, u32[]{:S(2)}, u32[]{:S(2)}) collective-permute-start(bf16[64,1024]{1,0:T(8,128)(2,1)} %get-tuple-element.57), channel_id=1, source_target_pairs={{0,24},{4,28},{8,16},{12,20},{16,8},{20,12},{24,0},{28,4},{1,25},{... | collective-permute-start | bytes 393224 | tf_op jit(solution)/shard_map/ppermute | solution.py:694
  71.6 1.3 %collective-permute-start.13 = (bf16[64,1024]{1,0:T(8,128)(2,1)}, bf16[64,1024]{1,0:T(8,128)(2,1)}, u32[]{:S(2)}, u32[]{:S(2)}) collective-permute-start(bf16[64,1024]{1,0:T(8,128)(2,1)} %get-tuple-element.58), channel_id=1, source_target_pairs={{0,28},{4,24},{8,20},{12,16},{16,12},{20,8},{24,4},{28,0},{1,29},{... | collective-permute-start | bytes 393224 | tf_op jit(solution)/shard_map/ppermute | solution.py:694
  72.9 1.1 %collective-permute-start.14 = (bf16[64,1024]{1,0:T(8,128)(2,1)}, bf16[64,1024]{1,0:T(8,128)(2,1)}, u32[]{:S(2)}, u32[]{:S(2)}) collective-permute-start(bf16[64,1024]{1,0:T(8,128)(2,1)} %get-tuple-element.59), channel_id=1, source_target_pairs={{0,8},{4,12},{8,0},{12,4},{16,24},{20,28},{24,16},{28,20},{1,9},{5... | collective-permute-start | bytes 393224 | tf_op jit(solution)/shard_map/ppermute | solution.py:694
  75.7 3.1 %collective-permute-start.17 = (bf16[64,1024]{1,0:T(8,128)(2,1)}, bf16[64,1024]{1,0:T(8,128)(2,1)}, u32[]{:S(2)}, u32[]{:S(2)}) collective-permute-start(bf16[64,1024]{1,0:T(8,128)(2,1)} %get-tuple-element.62), channel_id=1, source_target_pairs={{0,20},{4,16},{8,28},{12,24},{16,4},{20,0},{24,12},{28,8},{1,21},{... | collective-permute-start | bytes 393224 | tf_op jit(solution)/shard_map/ppermute | solution.py:694
  79.6 1.6 %collective-permute-done.14.refs_2_ = bf16[64,1024]{1,0:T(8,128)(2,1)} collective-permute-done((bf16[64,1024]{1,0:T(8,128)(2,1)}, bf16[64,1024]{1,0:T(8,128)(2,1)}, u32[]{:S(2)}, u32[]{:S(2)}) %collective-permute-start.14) | collective-permute-done | bytes 131104 | tf_op jit(solution)/shard_map/ppermute | solution.py:694
  81.1 3.7 %collective-permute-done.15.refs_3_ = bf16[64,1024]{1,0:T(8,128)(2,1)} collective-permute-done((bf16[64,1024]{1,0:T(8,128)(2,1)}, bf16[64,1024]{1,0:T(8,128)(2,1)}, u32[]{:S(2)}, u32[]{:S(2)}) %collective-permute-start.15) | collective-permute-done | bytes 131104 | tf_op jit(solution)/shard_map/ppermute | solution.py:694
  84.9 2.9 %shard_map.171 = (bf16[256,1280]{1,0:T(8,128)(2,1)}, bf16[256,512]{1,0:T(8,128)(2,1)}, f32[2,2]{1,0:T(2,128)}, bf16[32,2,2,256]{3,2,1,0:T(2,128)(2,1)}) custom-call(bf16[256,512]{1,0:T(8,128)(2,1)} %gate_hbm.3, bf16[256,512]{1,0:T(8,128)(2,1)} %hidden_hbm.3, f32[32,2,2,256]{3,2,1,0:T(2,128)} %get-tuple-element.34.delta_hbm, ...), custom_call_target="tpu_custom_call" | custom-call | tf_op jit(solution)/shard_map/pallas_call | solution.py:699
  (18 shorter events, 5.9 us)
Async XLA Ops:
  0.6 24.1 %collective-permute-start = (bf16[128,5120]{1,0:T(8,128)(2,1)}, bf16[128,5120]{1,0:T(8,128)(2,1)}, u32[]{:S(2)}, u32[]{:S(2)}) collective-permute-start(bf16[128,5120]{1,0:T(8,128)(2,1)} %own_x.5), channel_id=1, source_target_pairs={{0,4},{4,0},{8,12},{12,8},{16,20},{20,16},{24,28},{28,24},{1,5},{5... | collective-permute-start | bytes 3932168 | tf_op jit(solution)/shard_map/ppermute | solution.py:570
  1.4 10.0 %collective-permute-start.5 = (bf16[640,512]{1,0:T(8,128)(2,1)}, bf16[640,512]{1,0:T(8,128)(2,1)}, u32[]{:S(2)}, u32[]{:S(2)}) collective-permute-start(bf16[640,512]{1,0:T(8,128)(2,1)} %refs_0_.1), channel_id=1, source_target_pairs={{0,8},{4,20},{8,0},{12,28},{16,24},{20,4},{24,16},{28,12},{1,9},{5... | collective-permute-start | bytes 1966088 | tf_op jit(solution)/shard_map/ppermute | solution.py:566
  4.8 11.2 %all-to-all-start = ((bf16[8,64,512]{2,1,0:T(8,128)(2,1)}), bf16[8,64,512]{2,1,0:T(8,128)(2,1)}, u32[]{:S(2)}, u32[]{:S(2)}) async-start(bf16[8,64,512]{2,1,0:T(8,128)(2,1)} %shard_map.162), calls=%async_computation | async-start | bytes 1048576 | tf_op jit(solution)/shard_map/all_to_all | solution.py:583
  9.1 15.6 %collective-permute-start.7 = (bf16[640,512]{1,0:T(8,128)(2,1)}, bf16[640,512]{1,0:T(8,128)(2,1)}, u32[]{:S(2)}, u32[]{:S(2)}) collective-permute-start(bf16[640,512]{1,0:T(8,128)(2,1)} %refs_0_.1), channel_id=1, source_target_pairs={{0,16},{4,12},{8,24},{12,4},{16,0},{20,28},{24,8},{28,20},{1,17},{... | collective-permute-start | bytes 1966088 | tf_op jit(solution)/shard_map/ppermute | solution.py:566
  11.4 20.3 %collective-permute-start.6 = (bf16[640,512]{1,0:T(8,128)(2,1)}, bf16[640,512]{1,0:T(8,128)(2,1)}, u32[]{:S(2)}, u32[]{:S(2)}) collective-permute-start(bf16[640,512]{1,0:T(8,128)(2,1)} %collective-permute-done.5.refs_1_), channel_id=1, source_target_pairs={{0,16},{4,12},{8,24},{12,4},{16,0},{20,28},{24,8},{28,20},{1,17},{... | collective-permute-start | bytes 1966088 | tf_op jit(solution)/shard_map/ppermute | solution.py:566
  18.6 6.1 %collective-permute-start.1 = (bf16[400,512]{1,0:T(8,128)(2,1)}, bf16[400,512]{1,0:T(8,128)(2,1)}, u32[]{:S(2)}, u32[]{:S(2)}) collective-permute-start(bf16[400,512]{1,0:T(8,128)(2,1)} %shard_map.163.own_up), channel_id=1, source_target_pairs={{0,4},{4,0},{8,12},{12,8},{16,20},{20,16},{24,28},{28,24},{1,5},{5... | collective-permute-start | bytes 1228808 | tf_op jit(solution)/shard_map/ppermute | solution.py:595
  35.0 27.1 %collective-permute-start.10 = (bf16[256,640]{1,0:T(8,128)(2,1)}, bf16[256,640]{1,0:T(8,128)(2,1)}, u32[]{:S(2)}, u32[]{:S(2)}) collective-permute-start(bf16[256,640]{1,0:T(8,128)(2,1)} %get-tuple-element.55), channel_id=1, source_target_pairs={{0,2},{1,3},{2,0},{3,1},{4,6},{5,7},{6,4},{7,5},{8,10},{9,11},{10,... | collective-permute-start | bytes 983048 | tf_op jit(solution)/shard_map/ppermute | solution.py:631
  35.1 31.9 %collective-permute-start.11 = (bf16[256,640]{1,0:T(8,128)(2,1)}, bf16[256,640]{1,0:T(8,128)(2,1)}, u32[]{:S(2)}, u32[]{:S(2)}) collective-permute-start(bf16[256,640]{1,0:T(8,128)(2,1)} %get-tuple-element.56), channel_id=1, source_target_pairs={{0,3},{1,2},{2,1},{3,0},{4,7},{5,6},{6,5},{7,4},{8,11},{9,10},{10,... | collective-permute-start | bytes 983048 | tf_op jit(solution)/shard_map/ppermute | solution.py:631
  37.5 29.6 %collective-permute-start.9 = (bf16[256,640]{1,0:T(8,128)(2,1)}, bf16[256,640]{1,0:T(8,128)(2,1)}, u32[]{:S(2)}, u32[]{:S(2)}) collective-permute-start(bf16[256,640]{1,0:T(8,128)(2,1)} %get-tuple-element.54), channel_id=1, source_target_pairs={{0,1},{1,0},{2,3},{3,2},{4,5},{5,4},{6,7},{7,6},{8,9},{9,8},{10,11... | collective-permute-start | bytes 983048 | tf_op jit(solution)/shard_map/ppermute | solution.py:631
  41.2 18.7 %collective-permute-start.8 = (f32[128,512]{1,0:T(8,128)}, f32[128,512]{1,0:T(8,128)}, u32[]{:S(2)}, u32[]{:S(2)}) collective-permute-start(f32[128,512]{1,0:T(8,128)} %get-tuple-element.51), channel_id=1, source_target_pairs={{0,4},{4,0},{8,12},{12,8},{16,20},{20,16},{24,28},{28,24},{1,5},{5... | collective-permute-start | bytes 786440 | tf_op jit(solution)/shard_map/ppermute | solution.py:644
  45.4 4.1 %collective-permute-start.2 = (bf16[4,32,256]{2,1,0:T(8,128)(2,1)}, bf16[4,32,256]{2,1,0:T(8,128)(2,1)}, u32[]{:S(2)}, u32[]{:S(2)}) collective-permute-start(bf16[4,32,256]{2,1,0:T(8,128)(2,1)} %get-tuple-element.40), channel_id=1, source_target_pairs={{0,8},{4,12},{8,0},{12,4},{16,24},{20,28},{24,16},{28,20},{1,9},{5... | collective-permute-start | bytes 196616 | tf_op jit(solution)/shard_map/ppermute | solution.py:659
  49.5 3.7 %collective-permute-start.3 = (bf16[4,32,256]{2,1,0:T(8,128)(2,1)}, bf16[4,32,256]{2,1,0:T(8,128)(2,1)}, u32[]{:S(2)}, u32[]{:S(2)}) collective-permute-start(bf16[4,32,256]{2,1,0:T(8,128)(2,1)} %get-tuple-element.41), channel_id=1, source_target_pairs={{0,16},{4,20},{8,24},{12,28},{16,0},{20,4},{24,8},{28,12},{1,17},{... | collective-permute-start | bytes 196616 | tf_op jit(solution)/shard_map/ppermute | solution.py:659
  53.3 4.3 %collective-permute-start.4 = (bf16[4,32,256]{2,1,0:T(8,128)(2,1)}, bf16[4,32,256]{2,1,0:T(8,128)(2,1)}, u32[]{:S(2)}, u32[]{:S(2)}) collective-permute-start(bf16[4,32,256]{2,1,0:T(8,128)(2,1)} %get-tuple-element.42), channel_id=1, source_target_pairs={{0,24},{4,28},{8,16},{12,20},{16,8},{20,12},{24,0},{28,4},{1,25},{... | collective-permute-start | bytes 196616 | tf_op jit(solution)/shard_map/ppermute | solution.py:659
  69.8 5.9 %collective-permute-start.12 = (bf16[64,1024]{1,0:T(8,128)(2,1)}, bf16[64,1024]{1,0:T(8,128)(2,1)}, u32[]{:S(2)}, u32[]{:S(2)}) collective-permute-start(bf16[64,1024]{1,0:T(8,128)(2,1)} %get-tuple-element.57), channel_id=1, source_target_pairs={{0,24},{4,28},{8,16},{12,20},{16,8},{20,12},{24,0},{28,4},{1,25},{... | collective-permute-start | bytes 393224 | tf_op jit(solution)/shard_map/ppermute | solution.py:694
  71.6 8.0 %collective-permute-start.13 = (bf16[64,1024]{1,0:T(8,128)(2,1)}, bf16[64,1024]{1,0:T(8,128)(2,1)}, u32[]{:S(2)}, u32[]{:S(2)}) collective-permute-start(bf16[64,1024]{1,0:T(8,128)(2,1)} %get-tuple-element.58), channel_id=1, source_target_pairs={{0,28},{4,24},{8,20},{12,16},{16,12},{20,8},{24,4},{28,0},{1,29},{... | collective-permute-start | bytes 393224 | tf_op jit(solution)/shard_map/ppermute | solution.py:694
  72.9 8.2 %collective-permute-start.14 = (bf16[64,1024]{1,0:T(8,128)(2,1)}, bf16[64,1024]{1,0:T(8,128)(2,1)}, u32[]{:S(2)}, u32[]{:S(2)}) collective-permute-start(bf16[64,1024]{1,0:T(8,128)(2,1)} %get-tuple-element.59), channel_id=1, source_target_pairs={{0,8},{4,12},{8,0},{12,4},{16,24},{20,28},{24,16},{28,20},{1,9},{5... | collective-permute-start | bytes 393224 | tf_op jit(solution)/shard_map/ppermute | solution.py:694
  73.9 10.9 %collective-permute-start.15 = (bf16[64,1024]{1,0:T(8,128)(2,1)}, bf16[64,1024]{1,0:T(8,128)(2,1)}, u32[]{:S(2)}, u32[]{:S(2)}) collective-permute-start(bf16[64,1024]{1,0:T(8,128)(2,1)} %get-tuple-element.60), channel_id=1, source_target_pairs={{0,12},{4,8},{8,4},{12,0},{16,28},{20,24},{24,20},{28,16},{1,13},{... | collective-permute-start | bytes 393224 | tf_op jit(solution)/shard_map/ppermute | solution.py:694
  74.3 10.6 %collective-permute-start.16 = (bf16[64,1024]{1,0:T(8,128)(2,1)}, bf16[64,1024]{1,0:T(8,128)(2,1)}, u32[]{:S(2)}, u32[]{:S(2)}) collective-permute-start(bf16[64,1024]{1,0:T(8,128)(2,1)} %get-tuple-element.61), channel_id=1, source_target_pairs={{0,16},{4,20},{8,24},{12,28},{16,0},{20,4},{24,8},{28,12},{1,17},{... | collective-permute-start | bytes 393224 | tf_op jit(solution)/shard_map/ppermute | solution.py:694
  75.7 9.3 %collective-permute-start.17 = (bf16[64,1024]{1,0:T(8,128)(2,1)}, bf16[64,1024]{1,0:T(8,128)(2,1)}, u32[]{:S(2)}, u32[]{:S(2)}) collective-permute-start(bf16[64,1024]{1,0:T(8,128)(2,1)} %get-tuple-element.62), channel_id=1, source_target_pairs={{0,20},{4,16},{8,28},{12,24},{16,4},{20,0},{24,12},{28,8},{1,21},{... | collective-permute-start | bytes 393224 | tf_op jit(solution)/shard_map/ppermute | solution.py:694
  79.6 5.4 %collective-permute-start.18 = (bf16[64,1024]{1,0:T(8,128)(2,1)}, bf16[64,1024]{1,0:T(8,128)(2,1)}, u32[]{:S(2)}, u32[]{:S(2)}) collective-permute-start(bf16[64,1024]{1,0:T(8,128)(2,1)} %get-tuple-element.63), channel_id=1, source_target_pairs={{0,4},{4,0},{8,12},{12,8},{16,20},{20,16},{24,28},{28,24},{1,5},{5... | collective-permute-start | bytes 393224 | tf_op jit(solution)/shard_map/ppermute | solution.py:694

commit v3 on v2

--- a/solution.py
+++ b/solution.py
@@ -252,7 +252,7 @@
 
 
 def gradient_kernel(rows_ref, own_x, mate_x, own_up, mate_up, *refs):
-    out_refs, (held_ref, x_ref, up_ref, sems) = refs[:-4], refs[-4:]
+    keep_ref, send_ref, held_ref, x_ref, up_ref, sems = refs
     chips, spots, owned, width = held_ref.shape
     rows = own_x.shape[0]
     pairs = []
@@ -274,24 +274,26 @@
             preferred_element_type=jnp.float32,
         ).reshape(chips, 2, owned, width)
         held_ref[:, spot] = jnp.where(core == 0, full[:, 0], full[:, 1]).astype(jnp.bfloat16)
-    for distance, out_ref in enumerate(out_refs):
-        out_ref[...] = held_ref[own_chip ^ distance]
-
-
-def adam_kernel(delta_hbm, m_hbm, v_hbm, *refs):
-    delta_out, m_out, v_out, max_out, delta_ref, m_ref, v_ref, grad_ref, sems = refs[-9:]
-    chips = grad_ref.shape[0]
-    pairs = [(delta_hbm, delta_ref), (m_hbm, m_ref), (v_hbm, v_ref)]
-    for copy in fetch(pairs + [(refs[chip], grad_ref.at[chip]) for chip in range(chips)], sems):
+    for number in range(2):
+        keep_ref[number] = held_ref[own_chip ^ (2 * number)]
+        send_ref[number] = held_ref[own_chip ^ (2 * number + 1)]
+
+
+def halfway_kernel(keep_ref, came_ref, own_out, send_out):
+    own_out[...] = keep_ref[0].astype(jnp.float32) + came_ref[0].astype(jnp.float32)
+    send_out[...] = (keep_ref[1].astype(jnp.float32) + came_ref[1].astype(jnp.float32)).astype(jnp.bfloat16)
+
+
+def adam_kernel(own_ref, came_ref, delta_hbm, m_hbm, v_hbm, *refs):
+    delta_out, m_out, v_out, max_out, delta_ref, m_ref, v_ref, sems = refs
+    for copy in fetch([(delta_hbm, delta_ref), (m_hbm, m_ref), (v_hbm, v_ref)], sems):
         copy.wait()
     ids = lax.broadcasted_iota(jnp.int32, max_out.shape, 1)
     tops = jnp.zeros(max_out.shape, jnp.float32)
     for j in range(delta_ref.shape[1]):
         for k in range(K):
             spot = j * K + k
-            gradient = grad_ref[0, spot].astype(jnp.float32)
-            for chip in range(1, chips):
-                gradient = gradient + grad_ref[chip, spot].astype(jnp.float32)
+            gradient = own_ref[spot] + came_ref[spot].astype(jnp.float32)
             new_m = beta_first * m_ref[:, j, k, :] + (1.0 - beta_first) * gradient
             new_v = beta_second * v_ref[:, j, k, :] + (1.0 - beta_second) * gradient * gradient
             corrected_m = new_m / (1.0 - beta_first**STEP)
@@ -451,8 +453,8 @@
     mate_out[...] = full[rows:]
 
 
-def spread_up_kernel(own_up, own_sum, other_sum, tops_ref, out_ref):
-    peers, lines, _ = out_ref.shape
+def spread_up_kernel(own_up, own_sum, other_sum, tops_ref, side_ref, below_ref):
+    peers, lines, _ = side_ref.shape
     rows, width = own_sum.shape
     cap, half = lines // 2, width // 2
     target = own_up[rows : rows + META, :rows].astype(jnp.float32)
@@ -461,13 +463,14 @@
     placed = jnp.dot(place, value.astype(jnp.bfloat16), preferred_element_type=jnp.float32)
     placed = placed.astype(jnp.bfloat16).reshape(peers, cap, width)
     for side in range(2):
-        out_ref[:, side * cap : (side + 1) * cap, :half] = placed[:, :, side * half : (side + 1) * half]
+        side_ref[:, side * cap : (side + 1) * cap, :] = placed[:, :, side * LANE : (side + 1) * LANE]
+        below_ref[:, :, side * half : (side + 1) * half] = placed[:, side * META : (side + 1) * META, half:]
     for peer in range(peers):
-        out_ref[peer, :META, half:] = tops_ref[...]
-        out_ref[peer, META:, half:] = jnp.zeros((lines - META, LANE), jnp.bfloat16)
-
-
-def spread_kernel(own_up, mate_up, up_slots, *refs):
+        below_ref[peer, :, width : width + LANE] = tops_ref[...]
+        below_ref[peer, :, width + LANE :] = jnp.zeros((META, below_ref.shape[2] - width - LANE), jnp.bfloat16)
+
+
+def spread_kernel(own_up, mate_up, up_side, up_below, *refs):
     parts_hbm, out_refs = refs[:4], refs[4:-5]
     held_ref, meta_ref, parts_ref, sems, out_sems = refs[-5:]
     _, rows, size = parts_ref.shape
@@ -478,9 +481,10 @@
     token = lax.axis_index("tok")
     pairs = [(up.at[rows : rows + META, :rows], meta_ref.at[seat]) for seat, up in enumerate((own_up, mate_up))]
     pairs += [(part, parts_ref.at[n]) for n, part in enumerate(parts_hbm)]
-    pairs.append((up_slots, held_ref.at[:, :, size:]))
+    pairs.append((up_side, held_ref.at[:, : 2 * cap, size:]))
+    pairs.append((up_below, held_ref.at[:, 2 * cap :, :]))
     copies = fetch(pairs, sems)
-    for copy in copies[:-1]:
+    for copy in copies[:-2]:
         copy.wait()
     for seat in range(2):
         lines = slice(seat * rows, (seat + 1) * rows)
@@ -492,6 +496,7 @@
         placed = jnp.dot(place, summed.astype(jnp.bfloat16), preferred_element_type=jnp.float32)
         start = pl.multiple_of((core ^ seat) * cap, cap)
         held_ref[:, pl.ds(start, cap), :size] = placed.astype(jnp.bfloat16).reshape(peers, cap, size)
+    copies[-2].wait()
     copies[-1].wait()
     out_copies = fetch([(held_ref.at[token ^ d], far_ref) for d, far_ref in enumerate(out_refs)], out_sems)
     for copy in out_copies:
@@ -517,7 +522,7 @@
         copies[3 + number].wait()
         out_copies.append(
             pltpu.make_async_copy(
-                held_ref.at[number, :, :size], input_out.at[lines, lanes], out_sems.at[number]
+                held_ref.at[number, : 2 * cap, :size], input_out.at[lines, lanes], out_sems.at[number]
             )
         )
         out_copies[-1].start()
@@ -526,15 +531,17 @@
     tops = jnp.zeros((1, LANE), jnp.float32)
     for number, distance in enumerate(order):
         lines = pl.ds(pl.multiple_of((token ^ distance) * cap, cap), cap)
-        for side in range(2):
-            lanes = slice(side * half, (side + 1) * half)
-            gate = gate_ref[lines, lanes].astype(jnp.float32)
-            sigmoid_value = 1.0 / (1.0 + jnp.exp(-gate))
-            slope = sigmoid_value * (1.0 + gate * (1.0 - sigmoid_value))
-            value = held_ref[number, side * cap : (side + 1) * cap, size : size + half].astype(jnp.float32)
-            hidden = hidden_ref[lines, lanes].astype(jnp.float32)
-            gate_out[lines, lanes] = (hidden * value * slope).astype(jnp.bfloat16)
-        kinds = held_ref[number, :META, size + half :].astype(jnp.float32)
+        held = held_ref.at[number]
+        below = [held[2 * cap :, side * half : (side + 1) * half] for side in range(2)]
+        value = jnp.concatenate(
+            [held[:cap, size:], held[cap : 2 * cap, size:], jnp.concatenate(below, axis=0)], axis=1
+        ).astype(jnp.float32)
+        gate = gate_ref[lines, :].astype(jnp.float32)
+        sigmoid_value = 1.0 / (1.0 + jnp.exp(-gate))
+        slope = sigmoid_value * (1.0 + gate * (1.0 - sigmoid_value))
+        hidden = hidden_ref[lines, :].astype(jnp.float32)
+        gate_out[lines, :] = (hidden * value * slope).astype(jnp.bfloat16)
+        kinds = held[2 * cap :, 2 * half : 2 * half + LANE].astype(jnp.float32)
         tops = jnp.maximum(tops, kinds[0:1] + kinds[1:2] + kinds[2:3])
     lanes = lax.broadcasted_iota(jnp.int32, (1, LANE), 1)
     first = lax.broadcasted_iota(jnp.int32, scale_out.shape, 0)
@@ -627,7 +634,7 @@
         input_output_aliases={5 + n: 1 + n for n in range(chips)},
     )(scales, block_rows, own_up, mate_up, codes_far, *backs)
     parts = [backs[0]]
-    for shift in range(1, chips):
+    for shift in reversed(range(1, chips)):
         parts.append(lax.ppermute(backs[shift], "col", [(z, z ^ shift) for z in range(chips)]))
     own_sum, mate_sum = call(
         forward_kernel,
@@ -643,11 +650,12 @@
     )(rollout, mate_x, weight_far, early_sum)
     other_sum = lax.ppermute(mate_sum, "tok", mates)
 
-    gradient_parts = call(
+    block_pair = jax.ShapeDtypeStruct((2, spots, owned, BLK), jnp.bfloat16)
+    kept, leaving = call(
         gradient_kernel,
-        [jax.ShapeDtypeStruct((spots, owned, BLK), jnp.bfloat16)] * chips,
+        [block_pair] * 2,
         in_specs=[SMEM] + [HBM] * 4,
-        out_specs=[VMEM] * chips,
+        out_specs=[VMEM] * 2,
         scratch_shapes=[
             pltpu.VMEM((chips, spots, owned, BLK), jnp.bfloat16),
             pltpu.VMEM((spots, 2 * send_rows, BLK), jnp.bfloat16),
@@ -655,40 +663,46 @@
             pltpu.SemaphoreType.DMA((2 * spots + 2,)),
         ],
     )(block_rows, rollout, mate_x, own_up, mate_up)
-    gradient_arrived = [gradient_parts[0]] + [
-        lax.ppermute(gradient_parts[step], "tok", [(t, t ^ (2 * step)) for t in range(peer_count)])
-        for step in range(1, chips)
-    ]
+    came = lax.ppermute(leaving, "tok", [(t, t ^ 2) for t in range(peer_count)])
+    gradient_own, leaving = call(
+        halfway_kernel,
+        [jax.ShapeDtypeStruct((spots, owned, BLK), dtype) for dtype in (jnp.float32, jnp.bfloat16)],
+        in_specs=[VMEM] * 2,
+        out_specs=[VMEM] * 2,
+    )(kept, came)
+    came = lax.ppermute(leaving, "tok", [(t, t ^ 4) for t in range(peer_count)])
     moment = jax.ShapeDtypeStruct(delta.shape, jnp.float32)
     new_delta, new_m, new_v, tops = call(
         adam_kernel,
         (moment, moment, moment, jax.ShapeDtypeStruct((META, LANE), jnp.bfloat16)),
-        in_specs=[HBM] * (3 + chips),
+        in_specs=[VMEM] * 2 + [HBM] * 3,
         out_specs=(VMEM,) * 4,
-        scratch_shapes=[pltpu.VMEM(delta.shape, jnp.float32)] * 3
-        + [pltpu.VMEM((chips, spots, owned, BLK), jnp.bfloat16), pltpu.SemaphoreType.DMA((3 + chips,))],
-    )(delta, adam_m, adam_v, *gradient_arrived)
-
-    up_slots = call(
+        scratch_shapes=[pltpu.VMEM(delta.shape, jnp.float32)] * 3 + [pltpu.SemaphoreType.DMA((3,))],
+    )(gradient_own, came, delta, adam_m, adam_v)
+
+    spread_shape = (2 * cap + META, own_rows + LANE)
+    up_side, up_below = call(
         spread_up_kernel,
-        jax.ShapeDtypeStruct((peer_count, 2 * cap, width // 2 + LANE), jnp.bfloat16),
+        [
+            jax.ShapeDtypeStruct((peer_count, 2 * cap, LANE), jnp.bfloat16),
+            jax.ShapeDtypeStruct((peer_count, META, own_rows + LANE), jnp.bfloat16),
+        ],
         in_specs=[VMEM] * 4,
-        out_specs=VMEM,
+        out_specs=[VMEM] * 2,
     )(own_up, own_sum, other_sum, tops)
-    spread_width = own_rows + width // 2 + LANE
     slots = call(
         spread_kernel,
-        [jax.ShapeDtypeStruct((2 * cap, spread_width), jnp.bfloat16)] * peer_count,
-        in_specs=[HBM] * (3 + len(parts)),
+        [jax.ShapeDtypeStruct(spread_shape, jnp.bfloat16)] * peer_count,
+        in_specs=[HBM] * (4 + len(parts)),
         out_specs=[HBM] * peer_count,
         scratch_shapes=[
-            pltpu.VMEM((peer_count, 2 * cap, spread_width), jnp.bfloat16),
+            pltpu.VMEM((peer_count,) + spread_shape, jnp.bfloat16),
             pltpu.VMEM((2, META, send_rows), jnp.bfloat16),
             pltpu.VMEM((len(parts), 2 * send_rows, own_rows), jnp.bfloat16),
-            pltpu.SemaphoreType.DMA((3 + len(parts),)),
+            pltpu.SemaphoreType.DMA((4 + len(parts),)),
             pltpu.SemaphoreType.DMA((peer_count,)),
         ],
-    )(own_up, mate_up, up_slots, *parts)
+    )(own_up, mate_up, up_side, up_below, *parts)
     sent = {}
     for distance in sorted(range(1, peer_count), key=lambda d: (-bin(d >> 1).count("1"), d)):
         sent[distance] = lax.ppermute(
@@ -710,7 +724,7 @@
             pltpu.VMEM(gate_pre.shape, jnp.bfloat16),
             pltpu.VMEM(hidden_grad.shape, jnp.bfloat16),
             pltpu.VMEM(delta.shape, jnp.float32),
-            pltpu.VMEM((peer_count, 2 * cap, spread_width), jnp.bfloat16),
+            pltpu.VMEM((peer_count,) + spread_shape, jnp.bfloat16),
             pltpu.SemaphoreType.DMA((3 + peer_count,)),
             pltpu.SemaphoreType.DMA((peer_count,)),
         ],
@@ -724,7 +738,7 @@
         tok_size == 8 and col_size == 4
         and rollout.shape[0] == LANE
         and up_codes.shape[0] % LANE == 0
-        and up_codes.shape[1] % BLK == 0
+        and up_codes.shape[1] == 2 * BLK
     )
     if fits:
         return paired(tok_size, *arrays)

time: 88.3 us -> 89.6 us (1.015)
  the two profiles are of different devices: /device:TPU:17 before, /device:TPU:0 now
where the time goes in v3:
time: 89.6 us; the launch traced here: 89 us
  waiting for transfers between devices  32.7 us (36%)
  Pallas kernels  32.2 us (36%)
  starting transfers between devices  23.3 us (26%)
    ppermute x7, waiting for transfers between devices, paired(): lax.ppermute(slots[distance], 'tok', [(t, t ^ distance) for t in range(pe...  8.31 us
    pallas_call x1, Pallas kernels, paired(): call(product_kernel, [jax.ShapeDtypeStruct((2 * send_rows, width), jnp.fl...  6.11 us
    ppermute x3, starting transfers between devices, hop(): lax.ppermute(codes, 'tok', [(t, t ^ (4 if t & 1 ^ turned else 2)) for t i...  6.05 us
    ppermute x7, starting transfers between devices, paired(): lax.ppermute(slots[distance], 'tok', [(t, t ^ distance) for t in range(pe...  5.65 us
    all_to_all x1, waiting for transfers between devices, paired(): lax.all_to_all(first_out, 'tok', split_axis=0, concat_axis=0, tiled=True)  5.62 us
    ppermute x3, waiting for transfers between devices, paired(): lax.ppermute(backs[shift], 'col', [(z, z ^ shift) for z in range(chips)])  5.6 us
    ppermute x3, waiting for transfers between devices, hop(): lax.ppermute(codes, 'tok', [(t, t ^ (4 if t & 1 ^ turned else 2)) for t i...  4.95 us
    ppermute x1, waiting for transfers between devices, paired(): came = lax.ppermute(leaving, 'tok', [(t, t ^ 2) for t in range(peer_count)])  4.6 us
  transfers between devices with their start and end apart: 19, of which 12 were waited for; matrix products, arithmetic and copies ran while one was open for 0% of the time, Pallas kernels for 26%

profile of v3, /device:TPU:0, one launch (start us, length us, event | category | flops | bytes accessed | tf_op | source)
XLA Modules:
  0.0 89.0 jit_solution(1325199002700959902)
XLA Ops:
  1.1 2.6 %collective-permute-start.4 = (bf16[640,512]{1,0:T(8,128)(2,1)}, bf16[640,512]{1,0:T(8,128)(2,1)}, u32[]{:S(2)}, u32[]{:S(2)}) collective-permute-start(bf16[640,512]{1,0:T(8,128)(2,1)} %refs_0_.1), channel_id=1, source_target_pairs={{0,8},{4,20},{8,0},{12,28},{16,24},{20,4},{24,16},{28,12},{1,9},{5... | collective-permute-start | bytes 1966088 | tf_op jit(solution)/shard_map/ppermute | solution.py:573
  3.7 2.2 %shard_map.162 = bf16[8,64,512]{2,1,0:T(8,128)(2,1)} custom-call(bf16[256,512]{1,0:T(8,128)(2,1)} %gate_hbm.3, bf16[256,512]{1,0:T(8,128)(2,1)} %hidden_hbm.3, f32[32,2,2,256]{3,2,1,0:T(2,128)} %delta_hbm.3), custom_call_target="tpu_custom_call" | custom-call | tf_op jit(solution)/shard_map/pallas_call | solution.py:578
  5.9 4.2 %all-to-all-start = ((bf16[8,64,512]{2,1,0:T(8,128)(2,1)}), bf16[8,64,512]{2,1,0:T(8,128)(2,1)}, u32[]{:S(2)}, u32[]{:S(2)}) async-start(bf16[8,64,512]{2,1,0:T(8,128)(2,1)} %shard_map.162), calls=%async_computation | async-start | bytes 1048576 | tf_op jit(solution)/shard_map/all_to_all | solution.py:590
  10.0 1.9 %collective-permute-start.6 = (bf16[640,512]{1,0:T(8,128)(2,1)}, bf16[640,512]{1,0:T(8,128)(2,1)}, u32[]{:S(2)}, u32[]{:S(2)}) collective-permute-start(bf16[640,512]{1,0:T(8,128)(2,1)} %refs_0_.1), channel_id=1, source_target_pairs={{0,16},{4,12},{8,24},{12,4},{16,0},{20,28},{24,8},{28,20},{1,17},{... | collective-permute-start | bytes 1966088 | tf_op jit(solution)/shard_map/ppermute | solution.py:573
  12.0 1.1 %collective-permute-done.4.refs_1_ = bf16[640,512]{1,0:T(8,128)(2,1)} collective-permute-done((bf16[640,512]{1,0:T(8,128)(2,1)}, bf16[640,512]{1,0:T(8,128)(2,1)}, u32[]{:S(2)}, u32[]{:S(2)}) %collective-permute-start.4) | collective-permute-done | bytes 655392 | tf_op jit(solution)/shard_map/ppermute | solution.py:573
  13.1 1.6 %collective-permute-start.5 = (bf16[640,512]{1,0:T(8,128)(2,1)}, bf16[640,512]{1,0:T(8,128)(2,1)}, u32[]{:S(2)}, u32[]{:S(2)}) collective-permute-start(bf16[640,512]{1,0:T(8,128)(2,1)} %collective-permute-done.4.refs_1_), channel_id=1, source_target_pairs={{0,16},{4,12},{8,24},{12,4},{16,0},{20,28},{24,8},{28,20},{1,17},{... | collective-permute-start | bytes 1966088 | tf_op jit(solution)/shard_map/ppermute | solution.py:573
  14.6 5.6 %all-to-all-done.arrived_hbm = bf16[8,64,512]{2,1,0:T(8,128)(2,1)} async-done(((bf16[8,64,512]{2,1,0:T(8,128)(2,1)}), bf16[8,64,512]{2,1,0:T(8,128)(2,1)}, u32[]{:S(2)}, u32[]{:S(2)}) %all-to-all-start) | async-done | bytes 524320 | tf_op jit(solution)/shard_map/all_to_all | solution.py:590
  20.3 2.6 %shard_map.163.own_up = bf16[400,512]{1,0:T(8,128)(2,1)} custom-call(s32[2]{0:T(128)} %lengths_ref.1, s32[1,128]{1,0:T(1,128)} %bitcast.4, bf16[8,64,512]{2,1,0:T(8,128)(2,1)} %all-to-all-done.arrived_hbm), custom_call_target="tpu_custom_call" | custom-call | tf_op jit(solution)/shard_map/pallas_call | solution.py:591
  23.0 2.9 %collective-permute-done.6.refs_2_ = bf16[640,512]{1,0:T(8,128)(2,1)} collective-permute-done((bf16[640,512]{1,0:T(8,128)(2,1)}, bf16[640,512]{1,0:T(8,128)(2,1)}, u32[]{:S(2)}, u32[]{:S(2)}) %collective-permute-start.6) | collective-permute-done | bytes 655392 | tf_op jit(solution)/shard_map/ppermute | solution.py:573
  25.9 6.1 %shard_map.167 = (f32[256,512]{1,0:T(8,128)}, bf16[256,640]{1,0:T(8,128)(2,1)}, bf16[256,640]{1,0:T(8,128)(2,1)}, bf16[256,640]{1,0:T(8,128)(2,1)}, bf16[256,640]{1,0:T(8,128)(2,1)}) custom-call(f32[2,20]{1,0:T(2,128)} %bitcast.2, s32[2,2]{1,0:T(2,128)} %rows_ref.5, bf16[400,512]{1,0:T(8,128)(2,1)} %shard_map.163.own_up, ...), custom_call_target="tpu_custom_call" | custom-call | tf_op jit(solution)/shard_map/pallas_call | solution.py:610
  32.0 0.9 %collective-permute-done.5.codes_hbm = bf16[640,512]{1,0:T(8,128)(2,1)} collective-permute-done((bf16[640,512]{1,0:T(8,128)(2,1)}, bf16[640,512]{1,0:T(8,128)(2,1)}, u32[]{:S(2)}, u32[]{:S(2)}) %collective-permute-start.5) | collective-permute-done | bytes 655392 | tf_op jit(solution)/shard_map/ppermute | solution.py:573
  32.9 3.2 %shard_map.168 = (bf16[640,512]{1,0:T(8,128)(2,1)}, bf16[256,640]{1,0:T(8,128)(2,1)}, bf16[256,640]{1,0:T(8,128)(2,1)}, bf16[256,640]{1,0:T(8,128)(2,1)}, bf16[256,640]{1,0:T(8,128)(2,1)}) custom-call(f32[2,20]{1,0:T(2,128)} %bitcast.3, s32[2,2]{1,0:T(2,128)} %rows_ref.5, ...), custom_call_target="tpu_custom_call", output_to_operand_aliasing={{1}: (5, {}), {2}: (6, {}), {3}: (7, {}), {4}: (8, {})} | custom-call | tf_op jit(solution)/shard_map/pallas_call | solution.py:619
  36.2 1.6 %collective-permute-start.10 = (bf16[256,640]{1,0:T(8,128)(2,1)}, bf16[256,640]{1,0:T(8,128)(2,1)}, u32[]{:S(2)}, u32[]{:S(2)}) collective-permute-start(bf16[256,640]{1,0:T(8,128)(2,1)} %get-tuple-element.60), channel_id=1, source_target_pairs={{0,1},{1,0},{2,3},{3,2},{4,5},{5,4},{6,7},{7,6},{8,9},{9,8},{10,11... | collective-permute-start | bytes 983048 | tf_op jit(solution)/shard_map/ppermute | solution.py:638
  37.8 2.6 %collective-permute-start.8 = (bf16[256,640]{1,0:T(8,128)(2,1)}, bf16[256,640]{1,0:T(8,128)(2,1)}, u32[]{:S(2)}, u32[]{:S(2)}) collective-permute-start(bf16[256,640]{1,0:T(8,128)(2,1)} %get-tuple-element.58), channel_id=1, source_target_pairs={{0,3},{1,2},{2,1},{3,0},{4,7},{5,6},{6,5},{7,4},{8,11},{9,10},{10,... | collective-permute-start | bytes 983048 | tf_op jit(solution)/shard_map/ppermute | solution.py:638
  40.4 2.6 %shard_map.169 = (f32[128,512]{1,0:T(8,128)}, f32[128,512]{1,0:T(8,128)}) custom-call(bf16[128,5120]{1,0:T(8,128)(2,1)} %own_x.5, bf16[128,5120]{1,0:T(8,128)(2,1)} %collective-permute-done.mate_x, bf16[640,512]{1,0:T(8,128)(2,1)} %get-tuple-element.50.weight_hbm, f32[256,512]{1,0:T(8,128)} %get-tuple-element.51.sum_hbm), custom_call_target="tpu_custom_call" | custom-call | tf_op jit(solution)/shard_map/pallas_call | solution.py:639
  43.0 3.0 %shard_map.164 = (bf16[2,4,32,256]{3,2,1,0:T(8,128)(2,1)}, bf16[2,4,32,256]{3,2,1,0:T(8,128)(2,1)}) custom-call(s32[2,2]{1,0:T(2,128)} %rows_ref.5, bf16[128,5120]{1,0:T(8,128)(2,1)} %own_x.5, bf16[128,5120]{1,0:T(8,128)(2,1)} %collective-permute-done.mate_x, bf16[400,512]{1,0:T(8,128)(2,1)} %shard_map.163.own_up, ...), custom_call_target="tpu_custom_call" | custom-call | tf_op jit(solution)/shard_map/pallas_call | solution.py:654
  46.0 1.7 %collective-permute-start.2 = (bf16[2,4,32,256]{3,2,1,0:T(8,128)(2,1)}, bf16[2,4,32,256]{3,2,1,0:T(8,128)(2,1)}, u32[]{:S(2)}, u32[]{:S(2)}) collective-permute-start(bf16[2,4,32,256]{3,2,1,0:T(8,128)(2,1)} %get-tuple-element.42), channel_id=1, source_target_pairs={{0,8},{4,12},{8,0},{12,4},{16,24},{20,28},{24,16},{28,20},{1,9},{5... | collective-permute-start | bytes 393224 | tf_op jit(solution)/shard_map/ppermute | solution.py:666
  47.7 4.6 %collective-permute-done.2.came_ref = bf16[2,4,32,256]{3,2,1,0:T(8,128)(2,1)} collective-permute-done((bf16[2,4,32,256]{3,2,1,0:T(8,128)(2,1)}, bf16[2,4,32,256]{3,2,1,0:T(8,128)(2,1)}, u32[]{:S(2)}, u32[]{:S(2)}) %collective-permute-start.2) | collective-permute-done | bytes 131104 | tf_op jit(solution)/shard_map/ppermute | solution.py:666
  52.3 1.7 %shard_map.165 = (f32[4,32,256]{2,1,0:T(8,128)}, bf16[4,32,256]{2,1,0:T(8,128)(2,1)}) custom-call(bf16[2,4,32,256]{3,2,1,0:T(8,128)(2,1)} %get-tuple-element.41.keep_ref, bf16[2,4,32,256]{3,2,1,0:T(8,128)(2,1)} %collective-permute-done.2.came_ref), custom_call_target="tpu_custom_call" | custom-call | tf_op jit(solution)/shard_map/pallas_call | solution.py:667
  54.0 0.9 %collective-permute-start.3 = (bf16[4,32,256]{2,1,0:T(8,128)(2,1)}, bf16[4,32,256]{2,1,0:T(8,128)(2,1)}, u32[]{:S(2)}, u32[]{:S(2)}) collective-permute-start(bf16[4,32,256]{2,1,0:T(8,128)(2,1)} %get-tuple-element.44), channel_id=1, source_target_pairs={{0,16},{4,20},{8,24},{12,28},{16,0},{20,4},{24,8},{28,12},{1,17},{... | collective-permute-start | bytes 196616 | tf_op jit(solution)/shard_map/ppermute | solution.py:673
  54.9 3.7 %collective-permute-done.3.came_ref = bf16[4,32,256]{2,1,0:T(8,128)(2,1)} collective-permute-done((bf16[4,32,256]{2,1,0:T(8,128)(2,1)}, bf16[4,32,256]{2,1,0:T(8,128)(2,1)}, u32[]{:S(2)}, u32[]{:S(2)}) %collective-permute-start.3) | collective-permute-done | bytes 65568 | tf_op jit(solution)/shard_map/ppermute | solution.py:673
  58.6 3.1 %shard_map.166 = (f32[32,2,2,256]{3,2,1,0:T(2,128)}, f32[32,2,2,256]{3,2,1,0:T(2,128)}, f32[32,2,2,256]{3,2,1,0:T(2,128)}, bf16[16,128]{1,0:T(8,128)(2,1)}) custom-call(f32[4,32,256]{2,1,0:T(8,128)} %get-tuple-element.43.own_ref, bf16[4,32,256]{2,1,0:T(8,128)(2,1)} %collective-permute-done.3.came_ref, f32[32,2,2,256]{3,2,1,0:T(2,128)} %delta_hbm.3, ...), custom_call_target="tpu_custom_call" | custom-call | tf_op jit(solution)/shard_map/pallas_call | solution.py:675
  61.7 2.2 %shard_map.170 = (bf16[8,64,128]{2,1,0:T(8,128)(2,1)}, bf16[8,16,768]{2,1,0:T(8,128)(2,1)}) custom-call(bf16[400,512]{1,0:T(8,128)(2,1)} %shard_map.163.own_up, f32[128,512]{1,0:T(8,128)} %get-tuple-element.52.own_sum, f32[128,512]{1,0:T(8,128)} %collective-permute-done.7.other_sum, bf16[16,128]{1,0:T(8,128)(2,1)} %get-tuple-element.54.tops_ref), custom_call_target="tpu_custom_call" | custom-call | tf_op jit(solution)/shard_map/pallas_call | solution.py:684
  63.9 5.6 %collective-permute-done.9.refs_2_ = bf16[256,640]{1,0:T(8,128)(2,1)} collective-permute-done((bf16[256,640]{1,0:T(8,128)(2,1)}, bf16[256,640]{1,0:T(8,128)(2,1)}, u32[]{:S(2)}, u32[]{:S(2)}) %collective-permute-start.9) | collective-permute-done | bytes 327712 | tf_op jit(solution)/shard_map/ppermute | solution.py:638
  69.5 2.7 %shard_map.171 = (bf16[80,768]{1,0:T(8,128)(2,1)}, bf16[80,768]{1,0:T(8,128)(2,1)}, bf16[80,768]{1,0:T(8,128)(2,1)}, bf16[80,768]{1,0:T(8,128)(2,1)}, bf16[80,76...) custom-call(bf16[400,512]{1,0:T(8,128)(2,1)} %shard_map.163.own_up, ...), custom_call_target="tpu_custom_call" | custom-call | tf_op jit(solution)/shard_map/pallas_call | solution.py:693
  72.2 2.2 %collective-permute-start.11 = (bf16[80,768]{1,0:T(8,128)(2,1)}, bf16[80,768]{1,0:T(8,128)(2,1)}, u32[]{:S(2)}, u32[]{:S(2)}) collective-permute-start(bf16[80,768]{1,0:T(8,128)(2,1)} %get-tuple-element.61), channel_id=1, source_target_pairs={{0,24},{4,28},{8,16},{12,20},{16,8},{20,12},{24,0},{28,4},{1,25},{... | collective-permute-start | bytes 368648 | tf_op jit(solution)/shard_map/ppermute | solution.py:708
  74.9 1.7 %collective-permute-start.14 = (bf16[80,768]{1,0:T(8,128)(2,1)}, bf16[80,768]{1,0:T(8,128)(2,1)}, u32[]{:S(2)}, u32[]{:S(2)}) collective-permute-start(bf16[80,768]{1,0:T(8,128)(2,1)} %get-tuple-element.64), channel_id=1, source_target_pairs={{0,12},{4,8},{8,4},{12,0},{16,28},{20,24},{24,20},{28,16},{1,13},{... | collective-permute-start | bytes 368648 | tf_op jit(solution)/shard_map/ppermute | solution.py:708
  76.6 1.2 %collective-permute-start.15 = (bf16[80,768]{1,0:T(8,128)(2,1)}, bf16[80,768]{1,0:T(8,128)(2,1)}, u32[]{:S(2)}, u32[]{:S(2)}) collective-permute-start(bf16[80,768]{1,0:T(8,128)(2,1)} %get-tuple-element.65), channel_id=1, source_target_pairs={{0,16},{4,20},{8,24},{12,28},{16,0},{20,4},{24,8},{28,12},{1,17},{... | collective-permute-start | bytes 368648 | tf_op jit(solution)/shard_map/ppermute | solution.py:708
  78.4 2.9 %collective-permute-done.12.refs_1_ = bf16[80,768]{1,0:T(8,128)(2,1)} collective-permute-done((bf16[80,768]{1,0:T(8,128)(2,1)}, bf16[80,768]{1,0:T(8,128)(2,1)}, u32[]{:S(2)}, u32[]{:S(2)}) %collective-permute-start.12) | collective-permute-done | bytes 122912 | tf_op jit(solution)/shard_map/ppermute | solution.py:708
  81.3 2.3 %collective-permute-done.13.refs_2_ = bf16[80,768]{1,0:T(8,128)(2,1)} collective-permute-done((bf16[80,768]{1,0:T(8,128)(2,1)}, bf16[80,768]{1,0:T(8,128)(2,1)}, u32[]{:S(2)}, u32[]{:S(2)}) %collective-permute-start.13) | collective-permute-done | bytes 122912 | tf_op jit(solution)/shard_map/ppermute | solution.py:708
  83.6 2.1 %collective-permute-done.14.refs_3_ = bf16[80,768]{1,0:T(8,128)(2,1)} collective-permute-done((bf16[80,768]{1,0:T(8,128)(2,1)}, bf16[80,768]{1,0:T(8,128)(2,1)}, u32[]{:S(2)}, u32[]{:S(2)}) %collective-permute-start.14) | collective-permute-done | bytes 122912 | tf_op jit(solution)/shard_map/ppermute | solution.py:708
  86.2 2.9 %shard_map.172 = (bf16[256,1280]{1,0:T(8,128)(2,1)}, bf16[256,512]{1,0:T(8,128)(2,1)}, f32[2,2]{1,0:T(2,128)}, bf16[32,2,2,256]{3,2,1,0:T(2,128)(2,1)}) custom-call(bf16[256,512]{1,0:T(8,128)(2,1)} %gate_hbm.3, bf16[256,512]{1,0:T(8,128)(2,1)} %hidden_hbm.3, f32[32,2,2,256]{3,2,1,0:T(2,128)} %get-tuple-element.36.delta_hbm, ...), custom_call_target="tpu_custom_call" | custom-call | tf_op jit(solution)/shard_map/pallas_call | solution.py:713
  (17 shorter events, 2.2 us)
Async XLA Ops:
  0.6 25.3 %collective-permute-start = (bf16[128,5120]{1,0:T(8,128)(2,1)}, bf16[128,5120]{1,0:T(8,128)(2,1)}, u32[]{:S(2)}, u32[]{:S(2)}) collective-permute-start(bf16[128,5120]{1,0:T(8,128)(2,1)} %own_x.5), channel_id=1, source_target_pairs={{0,4},{4,0},{8,12},{12,8},{16,20},{20,16},{24,28},{28,24},{1,5},{5... | collective-permute-start | bytes 3932168 | tf_op jit(solution)/shard_map/ppermute | solution.py:577
  1.1 11.9 %collective-permute-start.4 = (bf16[640,512]{1,0:T(8,128)(2,1)}, bf16[640,512]{1,0:T(8,128)(2,1)}, u32[]{:S(2)}, u32[]{:S(2)}) collective-permute-start(bf16[640,512]{1,0:T(8,128)(2,1)} %refs_0_.1), channel_id=1, source_target_pairs={{0,8},{4,20},{8,0},{12,28},{16,24},{20,4},{24,16},{28,12},{1,9},{5... | collective-permute-start | bytes 1966088 | tf_op jit(solution)/shard_map/ppermute | solution.py:573
  5.9 14.4 %all-to-all-start = ((bf16[8,64,512]{2,1,0:T(8,128)(2,1)}), bf16[8,64,512]{2,1,0:T(8,128)(2,1)}, u32[]{:S(2)}, u32[]{:S(2)}) async-start(bf16[8,64,512]{2,1,0:T(8,128)(2,1)} %shard_map.162), calls=%async_computation | async-start | bytes 1048576 | tf_op jit(solution)/shard_map/all_to_all | solution.py:590
  10.0 15.9 %collective-permute-start.6 = (bf16[640,512]{1,0:T(8,128)(2,1)}, bf16[640,512]{1,0:T(8,128)(2,1)}, u32[]{:S(2)}, u32[]{:S(2)}) collective-permute-start(bf16[640,512]{1,0:T(8,128)(2,1)} %refs_0_.1), channel_id=1, source_target_pairs={{0,16},{4,12},{8,24},{12,4},{16,0},{20,28},{24,8},{28,20},{1,17},{... | collective-permute-start | bytes 1966088 | tf_op jit(solution)/shard_map/ppermute | solution.py:573
  13.1 19.8 %collective-permute-start.5 = (bf16[640,512]{1,0:T(8,128)(2,1)}, bf16[640,512]{1,0:T(8,128)(2,1)}, u32[]{:S(2)}, u32[]{:S(2)}) collective-permute-start(bf16[640,512]{1,0:T(8,128)(2,1)} %collective-permute-done.4.refs_1_), channel_id=1, source_target_pairs={{0,16},{4,12},{8,24},{12,4},{16,0},{20,28},{24,8},{28,20},{1,17},{... | collective-permute-start | bytes 1966088 | tf_op jit(solution)/shard_map/ppermute | solution.py:573
  22.9 3.0 %collective-permute-start.1 = (bf16[400,512]{1,0:T(8,128)(2,1)}, bf16[400,512]{1,0:T(8,128)(2,1)}, u32[]{:S(2)}, u32[]{:S(2)}) collective-permute-start(bf16[400,512]{1,0:T(8,128)(2,1)} %shard_map.163.own_up), channel_id=1, source_target_pairs={{0,4},{4,0},{8,12},{12,8},{16,20},{20,16},{24,28},{28,24},{1,5},{5... | collective-permute-start | bytes 1228808 | tf_op jit(solution)/shard_map/ppermute | solution.py:602
  36.2 27.7 %collective-permute-start.10 = (bf16[256,640]{1,0:T(8,128)(2,1)}, bf16[256,640]{1,0:T(8,128)(2,1)}, u32[]{:S(2)}, u32[]{:S(2)}) collective-permute-start(bf16[256,640]{1,0:T(8,128)(2,1)} %get-tuple-element.60), channel_id=1, source_target_pairs={{0,1},{1,0},{2,3},{3,2},{4,5},{5,4},{6,7},{7,6},{8,9},{9,8},{10,11... | collective-permute-start | bytes 983048 | tf_op jit(solution)/shard_map/ppermute | solution.py:638
  37.8 26.1 %collective-permute-start.8 = (bf16[256,640]{1,0:T(8,128)(2,1)}, bf16[256,640]{1,0:T(8,128)(2,1)}, u32[]{:S(2)}, u32[]{:S(2)}) collective-permute-start(bf16[256,640]{1,0:T(8,128)(2,1)} %get-tuple-element.58), channel_id=1, source_target_pairs={{0,3},{1,2},{2,1},{3,0},{4,7},{5,6},{6,5},{7,4},{8,11},{9,10},{10,... | collective-permute-start | bytes 983048 | tf_op jit(solution)/shard_map/ppermute | solution.py:638
  40.4 29.1 %collective-permute-start.9 = (bf16[256,640]{1,0:T(8,128)(2,1)}, bf16[256,640]{1,0:T(8,128)(2,1)}, u32[]{:S(2)}, u32[]{:S(2)}) collective-permute-start(bf16[256,640]{1,0:T(8,128)(2,1)} %get-tuple-element.59), channel_id=1, source_target_pairs={{0,2},{1,3},{2,0},{3,1},{4,6},{5,7},{6,4},{7,5},{8,10},{9,11},{10,... | collective-permute-start | bytes 983048 | tf_op jit(solution)/shard_map/ppermute | solution.py:638
  43.0 18.7 %collective-permute-start.7 = (f32[128,512]{1,0:T(8,128)}, f32[128,512]{1,0:T(8,128)}, u32[]{:S(2)}, u32[]{:S(2)}) collective-permute-start(f32[128,512]{1,0:T(8,128)} %get-tuple-element.53), channel_id=1, source_target_pairs={{0,4},{4,0},{8,12},{12,8},{16,20},{20,16},{24,28},{28,24},{1,5},{5... | collective-permute-start | bytes 786440 | tf_op jit(solution)/shard_map/ppermute | solution.py:651
  46.0 6.3 %collective-permute-start.2 = (bf16[2,4,32,256]{3,2,1,0:T(8,128)(2,1)}, bf16[2,4,32,256]{3,2,1,0:T(8,128)(2,1)}, u32[]{:S(2)}, u32[]{:S(2)}) collective-permute-start(bf16[2,4,32,256]{3,2,1,0:T(8,128)(2,1)} %get-tuple-element.42), channel_id=1, source_target_pairs={{0,8},{4,12},{8,0},{12,4},{16,24},{20,28},{24,16},{28,20},{1,9},{5... | collective-permute-start | bytes 393224 | tf_op jit(solution)/shard_map/ppermute | solution.py:666
  54.0 4.6 %collective-permute-start.3 = (bf16[4,32,256]{2,1,0:T(8,128)(2,1)}, bf16[4,32,256]{2,1,0:T(8,128)(2,1)}, u32[]{:S(2)}, u32[]{:S(2)}) collective-permute-start(bf16[4,32,256]{2,1,0:T(8,128)(2,1)} %get-tuple-element.44), channel_id=1, source_target_pairs={{0,16},{4,20},{8,24},{12,28},{16,0},{20,4},{24,8},{28,12},{1,17},{... | collective-permute-start | bytes 196616 | tf_op jit(solution)/shard_map/ppermute | solution.py:673
  72.2 6.2 %collective-permute-start.11 = (bf16[80,768]{1,0:T(8,128)(2,1)}, bf16[80,768]{1,0:T(8,128)(2,1)}, u32[]{:S(2)}, u32[]{:S(2)}) collective-permute-start(bf16[80,768]{1,0:T(8,128)(2,1)} %get-tuple-element.61), channel_id=1, source_target_pairs={{0,24},{4,28},{8,16},{12,20},{16,8},{20,12},{24,0},{28,4},{1,25},{... | collective-permute-start | bytes 368648 | tf_op jit(solution)/shard_map/ppermute | solution.py:708
  74.3 6.9 %collective-permute-start.12 = (bf16[80,768]{1,0:T(8,128)(2,1)}, bf16[80,768]{1,0:T(8,128)(2,1)}, u32[]{:S(2)}, u32[]{:S(2)}) collective-permute-start(bf16[80,768]{1,0:T(8,128)(2,1)} %get-tuple-element.62), channel_id=1, source_target_pairs={{0,28},{4,24},{8,20},{12,16},{16,12},{20,8},{24,4},{28,0},{1,29},{... | collective-permute-start | bytes 368648 | tf_op jit(solution)/shard_map/ppermute | solution.py:708
  74.3 9.2 %collective-permute-start.13 = (bf16[80,768]{1,0:T(8,128)(2,1)}, bf16[80,768]{1,0:T(8,128)(2,1)}, u32[]{:S(2)}, u32[]{:S(2)}) collective-permute-start(bf16[80,768]{1,0:T(8,128)(2,1)} %get-tuple-element.63), channel_id=1, source_target_pairs={{0,8},{4,12},{8,0},{12,4},{16,24},{20,28},{24,16},{28,20},{1,9},{5... | collective-permute-start | bytes 368648 | tf_op jit(solution)/shard_map/ppermute | solution.py:708
  74.9 10.8 %collective-permute-start.14 = (bf16[80,768]{1,0:T(8,128)(2,1)}, bf16[80,768]{1,0:T(8,128)(2,1)}, u32[]{:S(2)}, u32[]{:S(2)}) collective-permute-start(bf16[80,768]{1,0:T(8,128)(2,1)} %get-tuple-element.64), channel_id=1, source_target_pairs={{0,12},{4,8},{8,4},{12,0},{16,28},{20,24},{24,20},{28,16},{1,13},{... | collective-permute-start | bytes 368648 | tf_op jit(solution)/shard_map/ppermute | solution.py:708
  76.6 9.1 %collective-permute-start.15 = (bf16[80,768]{1,0:T(8,128)(2,1)}, bf16[80,768]{1,0:T(8,128)(2,1)}, u32[]{:S(2)}, u32[]{:S(2)}) collective-permute-start(bf16[80,768]{1,0:T(8,128)(2,1)} %get-tuple-element.65), channel_id=1, source_target_pairs={{0,16},{4,20},{8,24},{12,28},{16,0},{20,4},{24,8},{28,12},{1,17},{... | collective-permute-start | bytes 368648 | tf_op jit(solution)/shard_map/ppermute | solution.py:708
  78.4 7.8 %collective-permute-start.16 = (bf16[80,768]{1,0:T(8,128)(2,1)}, bf16[80,768]{1,0:T(8,128)(2,1)}, u32[]{:S(2)}, u32[]{:S(2)}) collective-permute-start(bf16[80,768]{1,0:T(8,128)(2,1)} %get-tuple-element.66), channel_id=1, source_target_pairs={{0,20},{4,16},{8,28},{12,24},{16,4},{20,0},{24,12},{28,8},{1,21},{... | collective-permute-start | bytes 368648 | tf_op jit(solution)/shard_map/ppermute | solution.py:708
  81.2 4.9 %collective-permute-start.17 = (bf16[80,768]{1,0:T(8,128)(2,1)}, bf16[80,768]{1,0:T(8,128)(2,1)}, u32[]{:S(2)}, u32[]{:S(2)}) collective-permute-start(bf16[80,768]{1,0:T(8,128)(2,1)} %get-tuple-element.67), channel_id=1, source_target_pairs={{0,4},{4,0},{8,12},{12,8},{16,20},{20,16},{24,28},{28,24},{1,5},{5... | collective-permute-start | bytes 368648 | tf_op jit(solution)/shard_map/ppermute | solution.py:708

commit v4 on v3

--- a/solution.py
+++ b/solution.py
@@ -252,7 +252,7 @@
 
 
 def gradient_kernel(rows_ref, own_x, mate_x, own_up, mate_up, *refs):
-    keep_ref, send_ref, held_ref, x_ref, up_ref, sems = refs
+    out_refs, (held_ref, x_ref, up_ref, sems) = refs[:-4], refs[-4:]
     chips, spots, owned, width = held_ref.shape
     rows = own_x.shape[0]
     pairs = []
@@ -274,26 +274,24 @@
             preferred_element_type=jnp.float32,
         ).reshape(chips, 2, owned, width)
         held_ref[:, spot] = jnp.where(core == 0, full[:, 0], full[:, 1]).astype(jnp.bfloat16)
-    for number in range(2):
-        keep_ref[number] = held_ref[own_chip ^ (2 * number)]
-        send_ref[number] = held_ref[own_chip ^ (2 * number + 1)]
-
-
-def halfway_kernel(keep_ref, came_ref, own_out, send_out):
-    own_out[...] = keep_ref[0].astype(jnp.float32) + came_ref[0].astype(jnp.float32)
-    send_out[...] = (keep_ref[1].astype(jnp.float32) + came_ref[1].astype(jnp.float32)).astype(jnp.bfloat16)
-
-
-def adam_kernel(own_ref, came_ref, delta_hbm, m_hbm, v_hbm, *refs):
-    delta_out, m_out, v_out, max_out, delta_ref, m_ref, v_ref, sems = refs
-    for copy in fetch([(delta_hbm, delta_ref), (m_hbm, m_ref), (v_hbm, v_ref)], sems):
+    for distance, out_ref in enumerate(out_refs):
+        out_ref[...] = held_ref[own_chip ^ distance]
+
+
+def adam_kernel(delta_hbm, m_hbm, v_hbm, *refs):
+    delta_out, m_out, v_out, max_out, delta_ref, m_ref, v_ref, grad_ref, sems = refs[-9:]
+    chips = grad_ref.shape[0]
+    pairs = [(delta_hbm, delta_ref), (m_hbm, m_ref), (v_hbm, v_ref)]
+    for copy in fetch(pairs + [(refs[chip], grad_ref.at[chip]) for chip in range(chips)], sems):
         copy.wait()
     ids = lax.broadcasted_iota(jnp.int32, max_out.shape, 1)
     tops = jnp.zeros(max_out.shape, jnp.float32)
     for j in range(delta_ref.shape[1]):
         for k in range(K):
             spot = j * K + k
-            gradient = own_ref[spot] + came_ref[spot].astype(jnp.float32)
+            gradient = grad_ref[0, spot].astype(jnp.float32)
+            for chip in range(1, chips):
+                gradient = gradient + grad_ref[chip, spot].astype(jnp.float32)
             new_m = beta_first * m_ref[:, j, k, :] + (1.0 - beta_first) * gradient
             new_v = beta_second * v_ref[:, j, k, :] + (1.0 - beta_second) * gradient * gradient
             corrected_m = new_m / (1.0 - beta_first**STEP)
@@ -634,7 +632,7 @@
         input_output_aliases={5 + n: 1 + n for n in range(chips)},
     )(scales, block_rows, own_up, mate_up, codes_far, *backs)
     parts = [backs[0]]
-    for shift in reversed(range(1, chips)):
+    for shift in range(1, chips):
         parts.append(lax.ppermute(backs[shift], "col", [(z, z ^ shift) for z in range(chips)]))
     own_sum, mate_sum = call(
         forward_kernel,
@@ -650,12 +648,11 @@
     )(rollout, mate_x, weight_far, early_sum)
     other_sum = lax.ppermute(mate_sum, "tok", mates)
 
-    block_pair = jax.ShapeDtypeStruct((2, spots, owned, BLK), jnp.bfloat16)
-    kept, leaving = call(
+    gradient_parts = call(
         gradient_kernel,
-        [block_pair] * 2,
+        [jax.ShapeDtypeStruct((spots, owned, BLK), jnp.bfloat16)] * chips,
         in_specs=[SMEM] + [HBM] * 4,
-        out_specs=[VMEM] * 2,
+        out_specs=[VMEM] * chips,
         scratch_shapes=[
             pltpu.VMEM((chips, spots, owned, BLK), jnp.bfloat16),
             pltpu.VMEM((spots, 2 * send_rows, BLK), jnp.bfloat16),
@@ -663,22 +660,19 @@
             pltpu.SemaphoreType.DMA((2 * spots + 2,)),
         ],
     )(block_rows, rollout, mate_x, own_up, mate_up)
-    came = lax.ppermute(leaving, "tok", [(t, t ^ 2) for t in range(peer_count)])
-    gradient_own, leaving = call(
-        halfway_kernel,
-        [jax.ShapeDtypeStruct((spots, owned, BLK), dtype) for dtype in (jnp.float32, jnp.bfloat16)],
-        in_specs=[VMEM] * 2,
-        out_specs=[VMEM] * 2,
-    )(kept, came)
-    came = lax.ppermute(leaving, "tok", [(t, t ^ 4) for t in range(peer_count)])
+    gradient_arrived = [gradient_parts[0]] + [
+        lax.ppermute(gradient_parts[step], "tok", [(t, t ^ (2 * step)) for t in range(peer_count)])
+        for step in range(1, chips)
+    ]
     moment = jax.ShapeDtypeStruct(delta.shape, jnp.float32)
     new_delta, new_m, new_v, tops = call(
         adam_kernel,
         (moment, moment, moment, jax.ShapeDtypeStruct((META, LANE), jnp.bfloat16)),
-        in_specs=[VMEM] * 2 + [HBM] * 3,
+        in_specs=[HBM] * (3 + chips),
         out_specs=(VMEM,) * 4,
-        scratch_shapes=[pltpu.VMEM(delta.shape, jnp.float32)] * 3 + [pltpu.SemaphoreType.DMA((3,))],
-    )(gradient_own, came, delta, adam_m, adam_v)
+        scratch_shapes=[pltpu.VMEM(delta.shape, jnp.float32)] * 3
+        + [pltpu.VMEM((chips, spots, owned, BLK), jnp.bfloat16), pltpu.SemaphoreType.DMA((3 + chips,))],
+    )(delta, adam_m, adam_v, *gradient_arrived)
 
     spread_shape = (2 * cap + META, own_rows + LANE)
     up_side, up_below = call(

time: 89.6 us -> 87.6 us (0.978)
  the two profiles are of different devices: /device:TPU:0 before, /device:TPU:17 now
where the time goes in v4:
time: 87.6 us; the launch traced here: 87.1 us
  Pallas kernels  29.7 us (34%)
  starting transfers between devices  29.3 us (33%)
  waiting for transfers between devices  27.4 us (31%)
    ppermute x3, waiting for transfers between devices, paired(): lax.ppermute(gradient_parts[step], 'tok', [(t, t ^ 2 * step) for t in ran...  8.85 us
    ppermute x7, starting transfers between devices, paired(): lax.ppermute(slots[distance], 'tok', [(t, t ^ distance) for t in range(pe...  8.49 us
    pallas_call x1, Pallas kernels, paired(): call(product_kernel, [jax.ShapeDtypeStruct((2 * send_rows, width), jnp.fl...  6.07 us
    ppermute x7, waiting for transfers between devices, paired(): lax.ppermute(slots[distance], 'tok', [(t, t ^ distance) for t in range(pe...  5.94 us
    ppermute x3, waiting for transfers between devices, paired(): lax.ppermute(backs[shift], 'col', [(z, z ^ shift) for z in range(chips)])  4.86 us
    all_to_all x1, starting transfers between devices, paired(): lax.all_to_all(first_out, 'tok', split_axis=0, concat_axis=0, tiled=True)  4.36 us
    ppermute x3, waiting for transfers between devices, hop(): lax.ppermute(codes, 'tok', [(t, t ^ (4 if t & 1 ^ turned else 2)) for t i...  4.35 us
    ppermute x3, starting transfers between devices, hop(): lax.ppermute(codes, 'tok', [(t, t ^ (4 if t & 1 ^ turned else 2)) for t i...  3.84 us
  transfers between devices with their start and end apart: 20, of which 13 were waited for; matrix products, arithmetic and copies ran while one was open for 0% of the time, Pallas kernels for 24%

profile of v4, /device:TPU:17, one launch (start us, length us, event | category | flops | bytes accessed | tf_op | source)
XLA Modules:
  0.0 87.1 jit_solution(11213989607577369117)
XLA Ops:
  1.4 1.2 %collective-permute-start.5 = (bf16[640,512]{1,0:T(8,128)(2,1)}, bf16[640,512]{1,0:T(8,128)(2,1)}, u32[]{:S(2)}, u32[]{:S(2)}) collective-permute-start(bf16[640,512]{1,0:T(8,128)(2,1)} %refs_0_.1), channel_id=1, source_target_pairs={{0,8},{4,20},{8,0},{12,28},{16,24},{20,4},{24,16},{28,12},{1,9},{5... | collective-permute-start | bytes 1966088 | tf_op jit(solution)/shard_map/ppermute | solution.py:571
  2.6 2.2 %shard_map.162 = bf16[8,64,512]{2,1,0:T(8,128)(2,1)} custom-call(bf16[256,512]{1,0:T(8,128)(2,1)} %gate_hbm.3, bf16[256,512]{1,0:T(8,128)(2,1)} %hidden_hbm.3, f32[32,2,2,256]{3,2,1,0:T(2,128)} %delta_hbm.3), custom_call_target="tpu_custom_call" | custom-call | tf_op jit(solution)/shard_map/pallas_call | solution.py:576
  4.8 4.4 %all-to-all-start = ((bf16[8,64,512]{2,1,0:T(8,128)(2,1)}), bf16[8,64,512]{2,1,0:T(8,128)(2,1)}, u32[]{:S(2)}, u32[]{:S(2)}) async-start(bf16[8,64,512]{2,1,0:T(8,128)(2,1)} %shard_map.162), calls=%async_computation | async-start | bytes 1048576 | tf_op jit(solution)/shard_map/all_to_all | solution.py:588
  9.1 1.4 %collective-permute-start.7 = (bf16[640,512]{1,0:T(8,128)(2,1)}, bf16[640,512]{1,0:T(8,128)(2,1)}, u32[]{:S(2)}, u32[]{:S(2)}) collective-permute-start(bf16[640,512]{1,0:T(8,128)(2,1)} %refs_0_.1), channel_id=1, source_target_pairs={{0,16},{4,12},{8,24},{12,4},{16,0},{20,28},{24,8},{28,20},{1,17},{... | collective-permute-start | bytes 1966088 | tf_op jit(solution)/shard_map/ppermute | solution.py:571
  11.4 1.2 %collective-permute-start.6 = (bf16[640,512]{1,0:T(8,128)(2,1)}, bf16[640,512]{1,0:T(8,128)(2,1)}, u32[]{:S(2)}, u32[]{:S(2)}) collective-permute-start(bf16[640,512]{1,0:T(8,128)(2,1)} %collective-permute-done.5.refs_1_), channel_id=1, source_target_pairs={{0,16},{4,12},{8,24},{12,4},{16,0},{20,28},{24,8},{28,20},{1,17},{... | collective-permute-start | bytes 1966088 | tf_op jit(solution)/shard_map/ppermute | solution.py:571
  12.6 3.4 %all-to-all-done.arrived_hbm = bf16[8,64,512]{2,1,0:T(8,128)(2,1)} async-done(((bf16[8,64,512]{2,1,0:T(8,128)(2,1)}), bf16[8,64,512]{2,1,0:T(8,128)(2,1)}, u32[]{:S(2)}, u32[]{:S(2)}) %all-to-all-start) | async-done | bytes 524320 | tf_op jit(solution)/shard_map/all_to_all | solution.py:588
  16.0 2.6 %shard_map.163.own_up = bf16[400,512]{1,0:T(8,128)(2,1)} custom-call(s32[2]{0:T(128)} %lengths_ref.1, s32[1,128]{1,0:T(1,128)} %bitcast.4, bf16[8,64,512]{2,1,0:T(8,128)(2,1)} %all-to-all-done.arrived_hbm), custom_call_target="tpu_custom_call" | custom-call | tf_op jit(solution)/shard_map/pallas_call | solution.py:589
  18.6 3.6 %collective-permute-start.1 = (bf16[400,512]{1,0:T(8,128)(2,1)}, bf16[400,512]{1,0:T(8,128)(2,1)}, u32[]{:S(2)}, u32[]{:S(2)}) collective-permute-start(bf16[400,512]{1,0:T(8,128)(2,1)} %shard_map.163.own_up), channel_id=1, source_target_pairs={{0,4},{4,0},{8,12},{12,8},{16,20},{20,16},{24,28},{28,24},{1,5},{5... | collective-permute-start | bytes 1228808 | tf_op jit(solution)/shard_map/ppermute | solution.py:600
  22.2 2.5 %collective-permute-done.7.refs_2_ = bf16[640,512]{1,0:T(8,128)(2,1)} collective-permute-done((bf16[640,512]{1,0:T(8,128)(2,1)}, bf16[640,512]{1,0:T(8,128)(2,1)}, u32[]{:S(2)}, u32[]{:S(2)}) %collective-permute-start.7) | collective-permute-done | bytes 655392 | tf_op jit(solution)/shard_map/ppermute | solution.py:571
  24.7 6.1 %shard_map.166 = (f32[256,512]{1,0:T(8,128)}, bf16[256,640]{1,0:T(8,128)(2,1)}, bf16[256,640]{1,0:T(8,128)(2,1)}, bf16[256,640]{1,0:T(8,128)(2,1)}, bf16[256,640]{1,0:T(8,128)(2,1)}) custom-call(f32[2,20]{1,0:T(2,128)} %bitcast.2, s32[2,2]{1,0:T(2,128)} %rows_ref.5, bf16[400,512]{1,0:T(8,128)(2,1)} %shard_map.163.own_up, ...), custom_call_target="tpu_custom_call" | custom-call | tf_op jit(solution)/shard_map/pallas_call | solution.py:608
  31.7 3.2 %shard_map.167 = (bf16[640,512]{1,0:T(8,128)(2,1)}, bf16[256,640]{1,0:T(8,128)(2,1)}, bf16[256,640]{1,0:T(8,128)(2,1)}, bf16[256,640]{1,0:T(8,128)(2,1)}, bf16[256,640]{1,0:T(8,128)(2,1)}) custom-call(f32[2,20]{1,0:T(2,128)} %bitcast.3, s32[2,2]{1,0:T(2,128)} %rows_ref.5, ...), custom_call_target="tpu_custom_call", output_to_operand_aliasing={{1}: (5, {}), {2}: (6, {}), {3}: (7, {}), {4}: (8, {})} | custom-call | tf_op jit(solution)/shard_map/pallas_call | solution.py:617
  35.1 2.4 %collective-permute-start.11 = (bf16[256,640]{1,0:T(8,128)(2,1)}, bf16[256,640]{1,0:T(8,128)(2,1)}, u32[]{:S(2)}, u32[]{:S(2)}) collective-permute-start(bf16[256,640]{1,0:T(8,128)(2,1)} %get-tuple-element.60), channel_id=1, source_target_pairs={{0,3},{1,2},{2,1},{3,0},{4,7},{5,6},{6,5},{7,4},{8,11},{9,10},{10,... | collective-permute-start | bytes 983048 | tf_op jit(solution)/shard_map/ppermute | solution.py:636
  37.6 1.0 %collective-permute-start.9 = (bf16[256,640]{1,0:T(8,128)(2,1)}, bf16[256,640]{1,0:T(8,128)(2,1)}, u32[]{:S(2)}, u32[]{:S(2)}) collective-permute-start(bf16[256,640]{1,0:T(8,128)(2,1)} %get-tuple-element.58), channel_id=1, source_target_pairs={{0,1},{1,0},{2,3},{3,2},{4,5},{5,4},{6,7},{7,6},{8,9},{9,8},{10,11... | collective-permute-start | bytes 983048 | tf_op jit(solution)/shard_map/ppermute | solution.py:636
  38.6 2.6 %shard_map.168 = (f32[128,512]{1,0:T(8,128)}, f32[128,512]{1,0:T(8,128)}) custom-call(bf16[128,5120]{1,0:T(8,128)(2,1)} %own_x.5, bf16[128,5120]{1,0:T(8,128)(2,1)} %collective-permute-done.mate_x, bf16[640,512]{1,0:T(8,128)(2,1)} %get-tuple-element.50.weight_hbm, f32[256,512]{1,0:T(8,128)} %get-tuple-element.51.sum_hbm), custom_call_target="tpu_custom_call" | custom-call | tf_op jit(solution)/shard_map/pallas_call | solution.py:637
  41.2 1.4 %collective-permute-start.8 = (f32[128,512]{1,0:T(8,128)}, f32[128,512]{1,0:T(8,128)}, u32[]{:S(2)}, u32[]{:S(2)}) collective-permute-start(f32[128,512]{1,0:T(8,128)} %get-tuple-element.53), channel_id=1, source_target_pairs={{0,4},{4,0},{8,12},{12,8},{16,20},{20,16},{24,28},{28,24},{1,5},{5... | collective-permute-start | bytes 786440 | tf_op jit(solution)/shard_map/ppermute | solution.py:649
  42.5 3.0 %shard_map.164 = (bf16[4,32,256]{2,1,0:T(8,128)(2,1)}, bf16[4,32,256]{2,1,0:T(8,128)(2,1)}, bf16[4,32,256]{2,1,0:T(8,128)(2,1)}, bf16[4,32,256]{2,1,0:T(8,128)(2,1)}) custom-call(s32[2,2]{1,0:T(2,128)} %rows_ref.5, bf16[128,5120]{1,0:T(8,128)(2,1)} %own_x.5, bf16[128,5120]{1,0:T(8,128)(2,1)} %collective-permute-done.mate_x, ...), custom_call_target="tpu_custom_call" | custom-call | tf_op jit(solution)/shard_map/pallas_call | solution.py:651
  45.5 1.3 %collective-permute-start.2 = (bf16[4,32,256]{2,1,0:T(8,128)(2,1)}, bf16[4,32,256]{2,1,0:T(8,128)(2,1)}, u32[]{:S(2)}, u32[]{:S(2)}) collective-permute-start(bf16[4,32,256]{2,1,0:T(8,128)(2,1)} %get-tuple-element.42), channel_id=1, source_target_pairs={{0,8},{4,12},{8,0},{12,4},{16,24},{20,28},{24,16},{28,20},{1,9},{5... | collective-permute-start | bytes 196616 | tf_op jit(solution)/shard_map/ppermute | solution.py:664
  46.8 2.8 %collective-permute-done.2.refs_1_ = bf16[4,32,256]{2,1,0:T(8,128)(2,1)} collective-permute-done((bf16[4,32,256]{2,1,0:T(8,128)(2,1)}, bf16[4,32,256]{2,1,0:T(8,128)(2,1)}, u32[]{:S(2)}, u32[]{:S(2)}) %collective-permute-start.2) | collective-permute-done | bytes 65568 | tf_op jit(solution)/shard_map/ppermute | solution.py:664
  50.1 3.2 %collective-permute-done.3.refs_2_ = bf16[4,32,256]{2,1,0:T(8,128)(2,1)} collective-permute-done((bf16[4,32,256]{2,1,0:T(8,128)(2,1)}, bf16[4,32,256]{2,1,0:T(8,128)(2,1)}, u32[]{:S(2)}, u32[]{:S(2)}) %collective-permute-start.3) | collective-permute-done | bytes 65568 | tf_op jit(solution)/shard_map/ppermute | solution.py:664
  53.3 1.5 %collective-permute-start.4 = (bf16[4,32,256]{2,1,0:T(8,128)(2,1)}, bf16[4,32,256]{2,1,0:T(8,128)(2,1)}, u32[]{:S(2)}, u32[]{:S(2)}) collective-permute-start(bf16[4,32,256]{2,1,0:T(8,128)(2,1)} %get-tuple-element.44), channel_id=1, source_target_pairs={{0,24},{4,28},{8,16},{12,20},{16,8},{20,12},{24,0},{28,4},{1,25},{... | collective-permute-start | bytes 196616 | tf_op jit(solution)/shard_map/ppermute | solution.py:664
  54.9 2.8 %collective-permute-done.4.refs_3_ = bf16[4,32,256]{2,1,0:T(8,128)(2,1)} collective-permute-done((bf16[4,32,256]{2,1,0:T(8,128)(2,1)}, bf16[4,32,256]{2,1,0:T(8,128)(2,1)}, u32[]{:S(2)}, u32[]{:S(2)}) %collective-permute-start.4) | collective-permute-done | bytes 65568 | tf_op jit(solution)/shard_map/ppermute | solution.py:664
  57.7 2.3 %shard_map.165 = (f32[32,2,2,256]{3,2,1,0:T(2,128)}, f32[32,2,2,256]{3,2,1,0:T(2,128)}, f32[32,2,2,256]{3,2,1,0:T(2,128)}, bf16[16,128]{1,0:T(8,128)(2,1)}) custom-call(f32[32,2,2,256]{3,2,1,0:T(2,128)} %delta_hbm.3, f32[32,2,2,256]{3,2,1,0:T(2,128)} %m_hbm.1, f32[32,2,2,256]{3,2,1,0:T(2,128)} %v_hbm.1, bf16[4,32,256]{2,1,0:T(8,128)(2,1)} %get-tuple-element.41.refs_0_, ...), custom_call_target="tpu_custom_call" | custom-call | tf_op jit(solution)/shard_map/pallas_call | solution.py:668
  60.0 2.2 %shard_map.169 = (bf16[8,64,128]{2,1,0:T(8,128)(2,1)}, bf16[8,16,768]{2,1,0:T(8,128)(2,1)}) custom-call(bf16[400,512]{1,0:T(8,128)(2,1)} %shard_map.163.own_up, f32[128,512]{1,0:T(8,128)} %get-tuple-element.52.own_sum, f32[128,512]{1,0:T(8,128)} %collective-permute-done.8.other_sum, bf16[16,128]{1,0:T(8,128)(2,1)} %get-tuple-element.54.tops_ref), custom_call_target="tpu_custom_call" | custom-call | tf_op jit(solution)/shard_map/pallas_call | solution.py:678
  62.2 4.9 %collective-permute-done.11.refs_3_ = bf16[256,640]{1,0:T(8,128)(2,1)} collective-permute-done((bf16[256,640]{1,0:T(8,128)(2,1)}, bf16[256,640]{1,0:T(8,128)(2,1)}, u32[]{:S(2)}, u32[]{:S(2)}) %collective-permute-start.11) | collective-permute-done | bytes 327712 | tf_op jit(solution)/shard_map/ppermute | solution.py:636
  67.0 2.7 %shard_map.170 = (bf16[80,768]{1,0:T(8,128)(2,1)}, bf16[80,768]{1,0:T(8,128)(2,1)}, bf16[80,768]{1,0:T(8,128)(2,1)}, bf16[80,768]{1,0:T(8,128)(2,1)}, bf16[80,76...) custom-call(bf16[400,512]{1,0:T(8,128)(2,1)} %shard_map.163.own_up, ...), custom_call_target="tpu_custom_call" | custom-call | tf_op jit(solution)/shard_map/pallas_call | solution.py:687
  69.8 1.8 %collective-permute-start.12 = (bf16[80,768]{1,0:T(8,128)(2,1)}, bf16[80,768]{1,0:T(8,128)(2,1)}, u32[]{:S(2)}, u32[]{:S(2)}) collective-permute-start(bf16[80,768]{1,0:T(8,128)(2,1)} %get-tuple-element.61), channel_id=1, source_target_pairs={{0,24},{4,28},{8,16},{12,20},{16,8},{20,12},{24,0},{28,4},{1,25},{... | collective-permute-start | bytes 368648 | tf_op jit(solution)/shard_map/ppermute | solution.py:702
  71.6 1.2 %collective-permute-start.13 = (bf16[80,768]{1,0:T(8,128)(2,1)}, bf16[80,768]{1,0:T(8,128)(2,1)}, u32[]{:S(2)}, u32[]{:S(2)}) collective-permute-start(bf16[80,768]{1,0:T(8,128)(2,1)} %get-tuple-element.62), channel_id=1, source_target_pairs={{0,28},{4,24},{8,20},{12,16},{16,12},{20,8},{24,4},{28,0},{1,29},{... | collective-permute-start | bytes 368648 | tf_op jit(solution)/shard_map/ppermute | solution.py:702
  72.8 1.1 %collective-permute-start.14 = (bf16[80,768]{1,0:T(8,128)(2,1)}, bf16[80,768]{1,0:T(8,128)(2,1)}, u32[]{:S(2)}, u32[]{:S(2)}) collective-permute-start(bf16[80,768]{1,0:T(8,128)(2,1)} %get-tuple-element.63), channel_id=1, source_target_pairs={{0,8},{4,12},{8,0},{12,4},{16,24},{20,28},{24,16},{28,20},{1,9},{5... | collective-permute-start | bytes 368648 | tf_op jit(solution)/shard_map/ppermute | solution.py:702
  75.5 2.7 %collective-permute-start.17 = (bf16[80,768]{1,0:T(8,128)(2,1)}, bf16[80,768]{1,0:T(8,128)(2,1)}, u32[]{:S(2)}, u32[]{:S(2)}) collective-permute-start(bf16[80,768]{1,0:T(8,128)(2,1)} %get-tuple-element.66), channel_id=1, source_target_pairs={{0,20},{4,16},{8,28},{12,24},{16,4},{20,0},{24,12},{28,8},{1,21},{... | collective-permute-start | bytes 368648 | tf_op jit(solution)/shard_map/ppermute | solution.py:702
  79.3 1.5 %collective-permute-done.14.refs_2_ = bf16[80,768]{1,0:T(8,128)(2,1)} collective-permute-done((bf16[80,768]{1,0:T(8,128)(2,1)}, bf16[80,768]{1,0:T(8,128)(2,1)}, u32[]{:S(2)}, u32[]{:S(2)}) %collective-permute-start.14) | collective-permute-done | bytes 122912 | tf_op jit(solution)/shard_map/ppermute | solution.py:702
  80.8 3.2 %collective-permute-done.15.refs_3_ = bf16[80,768]{1,0:T(8,128)(2,1)} collective-permute-done((bf16[80,768]{1,0:T(8,128)(2,1)}, bf16[80,768]{1,0:T(8,128)(2,1)}, u32[]{:S(2)}, u32[]{:S(2)}) %collective-permute-start.15) | collective-permute-done | bytes 122912 | tf_op jit(solution)/shard_map/ppermute | solution.py:702
  84.2 2.9 %shard_map.171 = (bf16[256,1280]{1,0:T(8,128)(2,1)}, bf16[256,512]{1,0:T(8,128)(2,1)}, f32[2,2]{1,0:T(2,128)}, bf16[32,2,2,256]{3,2,1,0:T(2,128)(2,1)}) custom-call(bf16[256,512]{1,0:T(8,128)(2,1)} %gate_hbm.3, bf16[256,512]{1,0:T(8,128)(2,1)} %hidden_hbm.3, f32[32,2,2,256]{3,2,1,0:T(2,128)} %get-tuple-element.36.delta_hbm, ...), custom_call_target="tpu_custom_call" | custom-call | tf_op jit(solution)/shard_map/pallas_call | solution.py:707
  (18 shorter events, 6.0 us)
Async XLA Ops:
  0.6 24.1 %collective-permute-start = (bf16[128,5120]{1,0:T(8,128)(2,1)}, bf16[128,5120]{1,0:T(8,128)(2,1)}, u32[]{:S(2)}, u32[]{:S(2)}) collective-permute-start(bf16[128,5120]{1,0:T(8,128)(2,1)} %own_x.5), channel_id=1, source_target_pairs={{0,4},{4,0},{8,12},{12,8},{16,20},{20,16},{24,28},{28,24},{1,5},{5... | collective-permute-start | bytes 3932168 | tf_op jit(solution)/shard_map/ppermute | solution.py:575
  1.4 10.0 %collective-permute-start.5 = (bf16[640,512]{1,0:T(8,128)(2,1)}, bf16[640,512]{1,0:T(8,128)(2,1)}, u32[]{:S(2)}, u32[]{:S(2)}) collective-permute-start(bf16[640,512]{1,0:T(8,128)(2,1)} %refs_0_.1), channel_id=1, source_target_pairs={{0,8},{4,20},{8,0},{12,28},{16,24},{20,4},{24,16},{28,12},{1,9},{5... | collective-permute-start | bytes 1966088 | tf_op jit(solution)/shard_map/ppermute | solution.py:571
  4.8 11.2 %all-to-all-start = ((bf16[8,64,512]{2,1,0:T(8,128)(2,1)}), bf16[8,64,512]{2,1,0:T(8,128)(2,1)}, u32[]{:S(2)}, u32[]{:S(2)}) async-start(bf16[8,64,512]{2,1,0:T(8,128)(2,1)} %shard_map.162), calls=%async_computation | async-start | bytes 1048576 | tf_op jit(solution)/shard_map/all_to_all | solution.py:588
  9.1 15.6 %collective-permute-start.7 = (bf16[640,512]{1,0:T(8,128)(2,1)}, bf16[640,512]{1,0:T(8,128)(2,1)}, u32[]{:S(2)}, u32[]{:S(2)}) collective-permute-start(bf16[640,512]{1,0:T(8,128)(2,1)} %refs_0_.1), channel_id=1, source_target_pairs={{0,16},{4,12},{8,24},{12,4},{16,0},{20,28},{24,8},{28,20},{1,17},{... | collective-permute-start | bytes 1966088 | tf_op jit(solution)/shard_map/ppermute | solution.py:571
  11.4 20.3 %collective-permute-start.6 = (bf16[640,512]{1,0:T(8,128)(2,1)}, bf16[640,512]{1,0:T(8,128)(2,1)}, u32[]{:S(2)}, u32[]{:S(2)}) collective-permute-start(bf16[640,512]{1,0:T(8,128)(2,1)} %collective-permute-done.5.refs_1_), channel_id=1, source_target_pairs={{0,16},{4,12},{8,24},{12,4},{16,0},{20,28},{24,8},{28,20},{1,17},{... | collective-permute-start | bytes 1966088 | tf_op jit(solution)/shard_map/ppermute | solution.py:571
  18.6 6.1 %collective-permute-start.1 = (bf16[400,512]{1,0:T(8,128)(2,1)}, bf16[400,512]{1,0:T(8,128)(2,1)}, u32[]{:S(2)}, u32[]{:S(2)}) collective-permute-start(bf16[400,512]{1,0:T(8,128)(2,1)} %shard_map.163.own_up), channel_id=1, source_target_pairs={{0,4},{4,0},{8,12},{12,8},{16,20},{20,16},{24,28},{28,24},{1,5},{5... | collective-permute-start | bytes 1228808 | tf_op jit(solution)/shard_map/ppermute | solution.py:600
  35.0 27.2 %collective-permute-start.10 = (bf16[256,640]{1,0:T(8,128)(2,1)}, bf16[256,640]{1,0:T(8,128)(2,1)}, u32[]{:S(2)}, u32[]{:S(2)}) collective-permute-start(bf16[256,640]{1,0:T(8,128)(2,1)} %get-tuple-element.59), channel_id=1, source_target_pairs={{0,2},{1,3},{2,0},{3,1},{4,6},{5,7},{6,4},{7,5},{8,10},{9,11},{10,... | collective-permute-start | bytes 983048 | tf_op jit(solution)/shard_map/ppermute | solution.py:636
  35.1 31.9 %collective-permute-start.11 = (bf16[256,640]{1,0:T(8,128)(2,1)}, bf16[256,640]{1,0:T(8,128)(2,1)}, u32[]{:S(2)}, u32[]{:S(2)}) collective-permute-start(bf16[256,640]{1,0:T(8,128)(2,1)} %get-tuple-element.60), channel_id=1, source_target_pairs={{0,3},{1,2},{2,1},{3,0},{4,7},{5,6},{6,5},{7,4},{8,11},{9,10},{10,... | collective-permute-start | bytes 983048 | tf_op jit(solution)/shard_map/ppermute | solution.py:636
  37.6 29.4 %collective-permute-start.9 = (bf16[256,640]{1,0:T(8,128)(2,1)}, bf16[256,640]{1,0:T(8,128)(2,1)}, u32[]{:S(2)}, u32[]{:S(2)}) collective-permute-start(bf16[256,640]{1,0:T(8,128)(2,1)} %get-tuple-element.58), channel_id=1, source_target_pairs={{0,1},{1,0},{2,3},{3,2},{4,5},{5,4},{6,7},{7,6},{8,9},{9,8},{10,11... | collective-permute-start | bytes 983048 | tf_op jit(solution)/shard_map/ppermute | solution.py:636
  41.2 18.8 %collective-permute-start.8 = (f32[128,512]{1,0:T(8,128)}, f32[128,512]{1,0:T(8,128)}, u32[]{:S(2)}, u32[]{:S(2)}) collective-permute-start(f32[128,512]{1,0:T(8,128)} %get-tuple-element.53), channel_id=1, source_target_pairs={{0,4},{4,0},{8,12},{12,8},{16,20},{20,16},{24,28},{28,24},{1,5},{5... | collective-permute-start | bytes 786440 | tf_op jit(solution)/shard_map/ppermute | solution.py:649
  45.5 4.1 %collective-permute-start.2 = (bf16[4,32,256]{2,1,0:T(8,128)(2,1)}, bf16[4,32,256]{2,1,0:T(8,128)(2,1)}, u32[]{:S(2)}, u32[]{:S(2)}) collective-permute-start(bf16[4,32,256]{2,1,0:T(8,128)(2,1)} %get-tuple-element.42), channel_id=1, source_target_pairs={{0,8},{4,12},{8,0},{12,4},{16,24},{20,28},{24,16},{28,20},{1,9},{5... | collective-permute-start | bytes 196616 | tf_op jit(solution)/shard_map/ppermute | solution.py:664
  49.6 3.7 %collective-permute-start.3 = (bf16[4,32,256]{2,1,0:T(8,128)(2,1)}, bf16[4,32,256]{2,1,0:T(8,128)(2,1)}, u32[]{:S(2)}, u32[]{:S(2)}) collective-permute-start(bf16[4,32,256]{2,1,0:T(8,128)(2,1)} %get-tuple-element.43), channel_id=1, source_target_pairs={{0,16},{4,20},{8,24},{12,28},{16,0},{20,4},{24,8},{28,12},{1,17},{... | collective-permute-start | bytes 196616 | tf_op jit(solution)/shard_map/ppermute | solution.py:664
  53.3 4.3 %collective-permute-start.4 = (bf16[4,32,256]{2,1,0:T(8,128)(2,1)}, bf16[4,32,256]{2,1,0:T(8,128)(2,1)}, u32[]{:S(2)}, u32[]{:S(2)}) collective-permute-start(bf16[4,32,256]{2,1,0:T(8,128)(2,1)} %get-tuple-element.44), channel_id=1, source_target_pairs={{0,24},{4,28},{8,16},{12,20},{16,8},{20,12},{24,0},{28,4},{1,25},{... | collective-permute-start | bytes 196616 | tf_op jit(solution)/shard_map/ppermute | solution.py:664
  69.8 5.7 %collective-permute-start.12 = (bf16[80,768]{1,0:T(8,128)(2,1)}, bf16[80,768]{1,0:T(8,128)(2,1)}, u32[]{:S(2)}, u32[]{:S(2)}) collective-permute-start(bf16[80,768]{1,0:T(8,128)(2,1)} %get-tuple-element.61), channel_id=1, source_target_pairs={{0,24},{4,28},{8,16},{12,20},{16,8},{20,12},{24,0},{28,4},{1,25},{... | collective-permute-start | bytes 368648 | tf_op jit(solution)/shard_map/ppermute | solution.py:702
  71.6 7.3 %collective-permute-start.13 = (bf16[80,768]{1,0:T(8,128)(2,1)}, bf16[80,768]{1,0:T(8,128)(2,1)}, u32[]{:S(2)}, u32[]{:S(2)}) collective-permute-start(bf16[80,768]{1,0:T(8,128)(2,1)} %get-tuple-element.62), channel_id=1, source_target_pairs={{0,28},{4,24},{8,20},{12,16},{16,12},{20,8},{24,4},{28,0},{1,29},{... | collective-permute-start | bytes 368648 | tf_op jit(solution)/shard_map/ppermute | solution.py:702
  72.8 8.0 %collective-permute-start.14 = (bf16[80,768]{1,0:T(8,128)(2,1)}, bf16[80,768]{1,0:T(8,128)(2,1)}, u32[]{:S(2)}, u32[]{:S(2)}) collective-permute-start(bf16[80,768]{1,0:T(8,128)(2,1)} %get-tuple-element.63), channel_id=1, source_target_pairs={{0,8},{4,12},{8,0},{12,4},{16,24},{20,28},{24,16},{28,20},{1,9},{5... | collective-permute-start | bytes 368648 | tf_op jit(solution)/shard_map/ppermute | solution.py:702
  74.0 10.1 %collective-permute-start.15 = (bf16[80,768]{1,0:T(8,128)(2,1)}, bf16[80,768]{1,0:T(8,128)(2,1)}, u32[]{:S(2)}, u32[]{:S(2)}) collective-permute-start(bf16[80,768]{1,0:T(8,128)(2,1)} %get-tuple-element.64), channel_id=1, source_target_pairs={{0,12},{4,8},{8,4},{12,0},{16,28},{20,24},{24,20},{28,16},{1,13},{... | collective-permute-start | bytes 368648 | tf_op jit(solution)/shard_map/ppermute | solution.py:702
  74.2 9.8 %collective-permute-start.16 = (bf16[80,768]{1,0:T(8,128)(2,1)}, bf16[80,768]{1,0:T(8,128)(2,1)}, u32[]{:S(2)}, u32[]{:S(2)}) collective-permute-start(bf16[80,768]{1,0:T(8,128)(2,1)} %get-tuple-element.65), channel_id=1, source_target_pairs={{0,16},{4,20},{8,24},{12,28},{16,0},{20,4},{24,8},{28,12},{1,17},{... | collective-permute-start | bytes 368648 | tf_op jit(solution)/shard_map/ppermute | solution.py:702
  75.5 8.7 %collective-permute-start.17 = (bf16[80,768]{1,0:T(8,128)(2,1)}, bf16[80,768]{1,0:T(8,128)(2,1)}, u32[]{:S(2)}, u32[]{:S(2)}) collective-permute-start(bf16[80,768]{1,0:T(8,128)(2,1)} %get-tuple-element.66), channel_id=1, source_target_pairs={{0,20},{4,16},{8,28},{12,24},{16,4},{20,0},{24,12},{28,8},{1,21},{... | collective-permute-start | bytes 368648 | tf_op jit(solution)/shard_map/ppermute | solution.py:702
  78.9 5.3 %collective-permute-start.18 = (bf16[80,768]{1,0:T(8,128)(2,1)}, bf16[80,768]{1,0:T(8,128)(2,1)}, u32[]{:S(2)}, u32[]{:S(2)}) collective-permute-start(bf16[80,768]{1,0:T(8,128)(2,1)} %get-tuple-element.67), channel_id=1, source_target_pairs={{0,4},{4,0},{8,12},{12,8},{16,20},{20,16},{24,28},{28,24},{1,5},{5... | collective-permute-start | bytes 368648 | tf_op jit(solution)/shard_map/ppermute | solution.py:702
